TPU v7x, 128 devices: a whole 4x4x4 slice. The times are simulated.
128 devices in a mesh: lat: 32 (over x, z, core), lev: 4 (over y).
Axes of the slice: x: 4, y: 4, z: 4, core: 2. Of those that a mesh axis runs over, the one named last changes fastest.
Arguments:
- fields: float32 [4, 256, 128, 1024], P(None, 'lat', 'lev'), may hold values from -6 to 6
- thickness: float32 [256, 128, 1024], P('lat', 'lev'), may hold values from 0.5 to 1.5
- courant_lon: float32 [256, 128, 1024], P('lat', 'lev'), may hold values from -0.8 to 0.8
- courant_lat: float32 [256, 128, 1024], P('lat', 'lev'), may hold values from -0.8 to 0.8
- exchange: float32 [2, 128, 128], replicated, may hold values from -0.5 to 0.5
- solar_profile: float32 [128], replicated, may hold values from 0.1 to 1
- owners: int32 [2048, 1], P(('lat', 'lev')), may hold values from 0 to 31; in each aligned block of 16 rows (0 to 15, 16 to 31, ...) at most 2 rows name the same one
- daylight: int32 [2048], P(('lat', 'lev')), may hold values 0 or 1
Outputs:
- remapped: float32 [4, 256, 128, 1024], P(None, 'lat', None, 'lev')
- heating: float32 [256, 128, 1024], P('lat', None, 'lev')
- owner_heat: float32 [32, 4], P('lat', 'lev')
Inputs may be any that keep to these rules, and one draw needn't show every extreme that they name: `owners`: among the rows of one device at most 2 name the same owner.
All inputs are finite; a program needn't handle non-finite values. No bound on the sum of `daylight` on one device may be relied on, other than what follows from the above.
Results may differ from a plain program's by a relative error of at most 0.0003.
Values sent between devices are 32-bit elements; how exact they have to be, the bound alone decides.
No kernel may reach another device: no remote copies, remote signals or barrier semaphores. Data moves between devices by JAX's collectives and lax.ppermute only.
A program may use at most 128 MiB of HBM per device.

v0:
```python
import jax
import jax.numpy as jnp
from jax import lax
from jax.sharding import PartitionSpec as P

BLOCK_COLS = 128


HIGH = lax.Precision.HIGHEST


def with_halo(cells, sides, width):
    for axis, dim in sides:
        count = lax.axis_size(axis)
        ends = count - 1
        head = lax.slice_in_dim(cells, 0, width, axis=dim)
        tail = lax.slice_in_dim(cells, cells.shape[dim] - width, cells.shape[dim], axis=dim)
        cells = jnp.concatenate(
            [
                lax.ppermute(tail, axis, [(i, (i + 1) % count) for i in range(ends)]),
                cells,
                lax.ppermute(head, axis, [((i + 1) % count, i) for i in range(ends)]),
            ],
            axis=dim,
        )
    return cells


def wendroff(values, courant, plus, minus):
    return (
        values
        - 0.5 * courant * (plus - minus)
        + 0.5 * courant * courant * (plus - 2.0 * values + minus)
    )


def remap_row(row_fields, row_thick):
    levels = row_thick.shape[0]
    index = jnp.arange(levels)
    lower = (index[:, None] >= index[None, :]).astype(jnp.float32)
    upper_edge = jnp.dot(lower, row_thick, precision=HIGH, preferred_element_type=jnp.float32)
    lower_edge = upper_edge - row_thick
    spacing = upper_edge[-1] / levels
    steps_f = index.astype(jnp.float32)
    ref_lo = steps_f[:, None] * spacing[None, :]
    ref_hi = (steps_f + 1.0)[:, None] * spacing[None, :]
    intersection = jnp.maximum(
        jnp.minimum(ref_hi[:, None, :], upper_edge[None, :, :])
        - jnp.maximum(ref_lo[:, None, :], lower_edge[None, :, :]),
        0.0,
    )
    mixed = jnp.einsum("ijc,fjc->fic", intersection, row_fields, precision=HIGH)
    return mixed / spacing[None, None, :]


def physics(temp, humid, day, exchange, solar, form):
    square = humid * humid
    absorb = square / (1.0 + square)
    clear = 1.0 / (1.0 + square)
    heat = jnp.einsum(form, exchange[0], absorb * temp, precision=HIGH)
    heat = heat + jnp.einsum(form, exchange[1], clear * temp, precision=HIGH)
    return heat + day * solar * clear


def remap_rows(piece):
    count = piece.shape[1]

    def one_row(row):
        whole_row = lax.dynamic_index_in_dim(piece, row, 1, keepdims=False)
        return remap_row(whole_row[:-1], whole_row[-1])

    return jnp.moveaxis(lax.map(one_row, jnp.arange(count)), 0, 1)


def per_device(
    fields, thickness, courant_lon, courant_lat, exchange, solar_profile, owners, daylight
):
    plus = jnp.roll(fields, -1, axis=3)
    minus = jnp.roll(fields, 1, axis=3)
    stepped = wendroff(fields, courant_lon[None], plus, minus)
    padded = with_halo(stepped, (("lat", 1),), 1)
    stepped = wendroff(stepped, courant_lat[None], padded[:, 2:], padded[:, :-2])
    moving = jnp.concatenate([stepped, thickness[None]], axis=0)
    remapped = remap_rows(lax.all_to_all(moving, "lev", split_axis=3, concat_axis=2, tiled=True))
    lat_rows = remapped.shape[1]
    levels = remapped.shape[2]
    piece_cols = remapped.shape[3]
    per_row = piece_cols // BLOCK_COLS
    local_blocks = lat_rows * per_row
    owner_count = lax.axis_size("lat")
    cols = remapped[:2].reshape(2, lat_rows, levels, per_row, BLOCK_COLS)
    owner_ids = owners[:, 0]
    onehot = (owner_ids[:, None] == jnp.arange(owner_count)[None, :]).astype(jnp.float32)
    scale = 1.0 / (levels * BLOCK_COLS)
    day_grid = daylight.astype(jnp.float32).reshape(lat_rows, 1, per_row, 1)
    heat = physics(
        cols[0], cols[1], day_grid, exchange, solar_profile[:, None, None], "ij,ajkc->aikc"
    )
    means = (jnp.sum(heat, axis=(1, 3)) * scale).reshape(local_blocks)
    shares = jnp.sum(onehot * means[:, None], axis=0)
    owner_heat = lax.psum_scatter(shares, "lat", scatter_dimension=0, tiled=True).reshape(1, 1)
    heating = heat.reshape(lat_rows, levels, piece_cols)
    return (remapped, heating, owner_heat)


def solution(mesh):
    placed = (
        P(None, "lat", "lev", None),
        P("lat", "lev", None),
        P("lat", "lev", None),
        P("lat", "lev", None),
        P(),
        P(),
        P(("lat", "lev"), None),
        P(("lat", "lev")),
    )
    return jax.shard_map(
        per_device,
        mesh=mesh,
        in_specs=placed,
        out_specs=(P(None, "lat", None, "lev"), P("lat", None, "lev"), P("lat", "lev")),
        check_vma=False,
    )
```

profile of v0, /device:TPU:1, one launch (start us, length us, event | category | flops | bytes accessed | tf_op | source)
XLA Modules:
  0.0 565.4 jit_solution(14817491728790050722)
XLA Ops:
  0.7 5.0 fusion.31
  6.2 2.3 multiply_add_fusion.1
  8.6 3.3 collective-permute-start
  12.0 3.5 collective-permute-start.1
  15.8 4.7 collective-permute-done
  20.4 1.2 collective-permute-done.1
  21.6 2.1 multiply_add_fusion
  23.7 3.0 pad_maximum_fusion
  26.7 13.2 %copy.62 = f32[5,8,32,1024]{2,1,0,3:T(8,128)} copy(f32[5,8,32,1024]{3,2,1,0:T(8,128)} %pad_maximum_fusion) | data formatting | bytes 10485760 | tf_op jit(solution)/shard_map/concatenate | solution.py:83
  39.9 23.5 %reshape.120 = f32[4,1,327680]{2,1,0:T(1,128)} reshape(f32[1024,5,8,32]{3,2,1,0:T(8,128)} %bitcast.67) | data formatting | bytes 10485760
  63.4 5.4 all-to-all-start
  69.6 54.1 %all-to-all-done = f32[4,1,327680]{2,1,0:T(1,128)} async-done(((f32[4,1,327680]{2,1,0:T(1,128)}), f32[4,1,327680]{2,1,0:T(1,128)}, u32[]{:S(2)}, u32[]{:S(2)}) %all-to-all-start) | async-done | bytes 5242912 | tf_op jit(solution)/shard_map/all_to_all | solution.py:84
  124.2 17.8 %reduce = f32[4,327680]{1,0:T(4,128)} reduce(f32[4,1,327680]{2,1,0:T(1,128)} %all-to-all-done, f32[]{:T(128)} %broadcast.130), dimensions={1}, to_apply=%all_to_all.13.reduce_sub_computation | reduce | bytes 10485764 | tf_op jit(solution)/shard_map/all_to_all | solution.py:84
  142.1 16.7 %reshape.121 = f32[1024,5,8,32]{3,2,1,0:T(8,128)} reshape(f32[4,327680]{1,0:T(4,128)} %reduce) | data formatting | bytes 10485760
  158.8 14.0 %copy.63 = f32[5,8,4,32,256]{4,3,2,1,0:T(8,128)} copy(f32[5,8,4,32,256]{3,1,0,4,2:T(8,128)} %bitcast.68) | data formatting | bytes 10485760 | tf_op jit(solution)/shard_map/all_to_all | solution.py:84
  172.8 318.3 %while.10 = (s32[]{:T(128)}, f32[8,4,128,256]{3,2,0,1:T(8,128)}, s32[8]{0:T(128)S(1)}, f32[5,8,128,256]{3,2,1,0:T(8,128)}, s32[]{:T(128)}, /*index=5*/s32[]{:T(128)}, s32[]{:T(128)}, s32[]{}) while((s32[]{:T(128)}, f32[8,4,128,256]{3,2,0,1:T(8,128)}, s32[8]{0:T(128)S(1)}, f32[5,8,128,256]{3,2,1,0:T(8,128)}, s32[]{:T(128)}, ...), condition=%wide.region_1.2_spmd, body=%wide.region_0.1_spmd.sunk | while | flops 268681856 | bytes 7086739 | solution.py:72
  175.3 1.2 fusion.43
  176.9 1.1 dynamic-slice_bitcast_fusion.4
  178.2 33.3 %fusion.44 = f32[1,4,128,256]{2,1,3,0:T(4,128)S(1)} fusion(f32[4,128,256]{1,0,2:T(4,128)S(1)} %copy.81, f32[128,256]{0,1:T(8,128)S(1)} %copy.82, f32[128,256]{0,1:T(8,128)S(1)} %get-tuple-element.99, f32[128,256]{0,1:T(8,128)S(1)} %copy.83, f32[128,256]{0,1:T(8,128)S(1)} %get-tuple-element.100, f32[256]{0:T(256)S(1)} %bitcast.78), kind=kOutput, calls=%fused_computation.11.clone.1 | convolution fusion | flops 218234880 | bytes 1573888 | tf_op jit(solution)/shard_map/while/body/eval_jaxpr/ijc,fjc->fic/dot_general | solution.py:52
  215.1 1.2 fusion.43
  216.6 1.1 dynamic-slice_bitcast_fusion.4
  218.0 33.3 %fusion.44 = f32[1,4,128,256]{2,1,3,0:T(4,128)S(1)} fusion(f32[4,128,256]{1,0,2:T(4,128)S(1)} %copy.81, f32[128,256]{0,1:T(8,128)S(1)} %copy.82, f32[128,256]{0,1:T(8,128)S(1)} %get-tuple-element.99, f32[128,256]{0,1:T(8,128)S(1)} %copy.83, f32[128,256]{0,1:T(8,128)S(1)} %get-tuple-element.100, f32[256]{0:T(256)S(1)} %bitcast.78), kind=kOutput, calls=%fused_computation.11.clone.1 | convolution fusion | flops 218234880 | bytes 1573888 | tf_op jit(solution)/shard_map/while/body/eval_jaxpr/ijc,fjc->fic/dot_general | solution.py:52
  251.5 0.8 constant_dynamic-update-slice_fusion.2
  254.9 1.2 fusion.43
  256.4 1.1 dynamic-slice_bitcast_fusion.4
  257.7 33.3 %fusion.44 = f32[1,4,128,256]{2,1,3,0:T(4,128)S(1)} fusion(f32[4,128,256]{1,0,2:T(4,128)S(1)} %copy.81, f32[128,256]{0,1:T(8,128)S(1)} %copy.82, f32[128,256]{0,1:T(8,128)S(1)} %get-tuple-element.99, f32[128,256]{0,1:T(8,128)S(1)} %copy.83, f32[128,256]{0,1:T(8,128)S(1)} %get-tuple-element.100, f32[256]{0:T(256)S(1)} %bitcast.78), kind=kOutput, calls=%fused_computation.11.clone.1 | convolution fusion | flops 218234880 | bytes 1573888 | tf_op jit(solution)/shard_map/while/body/eval_jaxpr/ijc,fjc->fic/dot_general | solution.py:52
  294.7 1.2 fusion.43
  296.2 1.1 dynamic-slice_bitcast_fusion.4
  297.5 33.3 %fusion.44 = f32[1,4,128,256]{2,1,3,0:T(4,128)S(1)} fusion(f32[4,128,256]{1,0,2:T(4,128)S(1)} %copy.81, f32[128,256]{0,1:T(8,128)S(1)} %copy.82, f32[128,256]{0,1:T(8,128)S(1)} %get-tuple-element.99, f32[128,256]{0,1:T(8,128)S(1)} %copy.83, f32[128,256]{0,1:T(8,128)S(1)} %get-tuple-element.100, f32[256]{0:T(256)S(1)} %bitcast.78), kind=kOutput, calls=%fused_computation.11.clone.1 | convolution fusion | flops 218234880 | bytes 1573888 | tf_op jit(solution)/shard_map/while/body/eval_jaxpr/ijc,fjc->fic/dot_general | solution.py:52
  334.4 1.2 fusion.43
  336.0 1.1 dynamic-slice_bitcast_fusion.4
  337.3 33.3 %fusion.44 = f32[1,4,128,256]{2,1,3,0:T(4,128)S(1)} fusion(f32[4,128,256]{1,0,2:T(4,128)S(1)} %copy.81, f32[128,256]{0,1:T(8,128)S(1)} %copy.82, f32[128,256]{0,1:T(8,128)S(1)} %get-tuple-element.99, f32[128,256]{0,1:T(8,128)S(1)} %copy.83, f32[128,256]{0,1:T(8,128)S(1)} %get-tuple-element.100, f32[256]{0:T(256)S(1)} %bitcast.78), kind=kOutput, calls=%fused_computation.11.clone.1 | convolution fusion | flops 218234880 | bytes 1573888 | tf_op jit(solution)/shard_map/while/body/eval_jaxpr/ijc,fjc->fic/dot_general | solution.py:52
  374.2 1.2 fusion.43
  375.8 1.1 dynamic-slice_bitcast_fusion.4
  377.1 33.3 %fusion.44 = f32[1,4,128,256]{2,1,3,0:T(4,128)S(1)} fusion(f32[4,128,256]{1,0,2:T(4,128)S(1)} %copy.81, f32[128,256]{0,1:T(8,128)S(1)} %copy.82, f32[128,256]{0,1:T(8,128)S(1)} %get-tuple-element.99, f32[128,256]{0,1:T(8,128)S(1)} %copy.83, f32[128,256]{0,1:T(8,128)S(1)} %get-tuple-element.100, f32[256]{0:T(256)S(1)} %bitcast.78), kind=kOutput, calls=%fused_computation.11.clone.1 | convolution fusion | flops 218234880 | bytes 1573888 | tf_op jit(solution)/shard_map/while/body/eval_jaxpr/ijc,fjc->fic/dot_general | solution.py:52
  414.0 1.2 fusion.43
  415.6 1.1 dynamic-slice_bitcast_fusion.4
  416.9 33.3 %fusion.44 = f32[1,4,128,256]{2,1,3,0:T(4,128)S(1)} fusion(f32[4,128,256]{1,0,2:T(4,128)S(1)} %copy.81, f32[128,256]{0,1:T(8,128)S(1)} %copy.82, f32[128,256]{0,1:T(8,128)S(1)} %get-tuple-element.99, f32[128,256]{0,1:T(8,128)S(1)} %copy.83, f32[128,256]{0,1:T(8,128)S(1)} %get-tuple-element.100, f32[256]{0:T(256)S(1)} %bitcast.78), kind=kOutput, calls=%fused_computation.11.clone.1 | convolution fusion | flops 218234880 | bytes 1573888 | tf_op jit(solution)/shard_map/while/body/eval_jaxpr/ijc,fjc->fic/dot_general | solution.py:52
  453.8 1.2 fusion.43
  455.3 1.1 dynamic-slice_bitcast_fusion.4
  456.7 33.3 %fusion.44 = f32[1,4,128,256]{2,1,3,0:T(4,128)S(1)} fusion(f32[4,128,256]{1,0,2:T(4,128)S(1)} %copy.81, f32[128,256]{0,1:T(8,128)S(1)} %copy.82, f32[128,256]{0,1:T(8,128)S(1)} %get-tuple-element.99, f32[128,256]{0,1:T(8,128)S(1)} %copy.83, f32[128,256]{0,1:T(8,128)S(1)} %get-tuple-element.100, f32[256]{0:T(256)S(1)} %bitcast.78), kind=kOutput, calls=%fused_computation.11.clone.1 | convolution fusion | flops 218234880 | bytes 1573888 | tf_op jit(solution)/shard_map/while/body/eval_jaxpr/ijc,fjc->fic/dot_general | solution.py:52
  491.1 1.9 add_divide_fusion
  493.0 1.3 copy.71
  495.0 2.2 fusion.26
  497.2 1.1 fusion.33
  498.3 1.3 copy.68
  499.8 64.4 %all-reduce = f32[32]{0:T(128)S(1)} all-reduce(f32[32]{0:T(128)S(1)} %select_reduce_fusion), channel_id=2, replica_groups=mesh['lat'=32,'lev'=4] {'lat'}, use_global_device_ids=true, to_apply=%region_4.5.clone | all-reduce | flops 32 | bytes 256
  564.2 1.2 dynamic-slice.1
  (113 shorter events, 19.4 us)
Async XLA Ops:
  0.6 5.0 copy-start
  0.6 5.3 copy-start.1
  6.2 9.3 %copy-start.2 = (f32[8,32,1024]{2,1,0:T(8,128)S(1)}, f32[8,32,1024]{2,1,0:T(8,128)}, u32[]{:S(2)}) copy-start(f32[8,32,1024]{2,1,0:T(8,128)} %param.13) | copy-start | bytes 3145732
  8.6 11.8 %collective-permute-start = (f32[4,1,32,1024]{3,2,1,0:T(8,128)S(1)}, f32[4,1,32,1024]{3,2,1,0:T(8,128)S(1)}, u32[]{:S(2)}, u32[]{:S(2)}) collective-permute-start(f32[4,1,32,1024]{3,2,1,0:T(8,128)S(1)} %get-tuple-element.57), channel_id=1, source_target_pairs={{4,0},{8,4},{12,8},{16,12},{20,16},{24,20},{28,24},{32,28},{36,32}... | collective-permute-start | bytes 1572872 | tf_op jit(solution)/shard_map/ppermute | solution.py:22
  12.0 9.6 %collective-permute-start.1 = (f32[4,1,32,1024]{3,2,1,0:T(8,128)S(1)}, f32[4,1,32,1024]{3,2,1,0:T(8,128)S(1)}, u32[]{:S(2)}, u32[]{:S(2)}) collective-permute-start(f32[4,1,32,1024]{3,2,1,0:T(8,128)S(1)} %get-tuple-element.56), channel_id=1, source_target_pairs={{0,4},{4,8},{8,12},{12,16},{16,20},{20,24},{24,28},{28,32},{32,36}... | collective-permute-start | bytes 1572872 | tf_op jit(solution)/shard_map/ppermute | solution.py:20
  21.6 2.1 copy-start.3
  63.4 5.4 copy-start.6
  63.4 5.5 copy-start.8
  63.4 6.1 %copy-start.5 = (f32[128]{0:T(128)S(1)}, f32[128]{0:T(128)}, u32[]{:S(2)}) copy-start(f32[128]{0:T(128)} %param.15) | copy-start | bytes 1540
  63.4 60.3 %all-to-all-start = ((f32[4,1,327680]{2,1,0:T(1,128)}), f32[4,1,327680]{2,1,0:T(1,128)}, u32[]{:S(2)}, u32[]{:S(2)}) async-start(f32[4,1,327680]{2,1,0:T(1,128)} %reshape.120), calls=%async_computation | async-start | bytes 10485760 | tf_op jit(solution)/shard_map/all_to_all | solution.py:84
  493.0 2.0 copy-start.4
  495.0 4.7 copy-start.7
where the time goes:
time: 569 us; the launch traced here: 565 us
  matrix products  279 us (49%)
  local copies, waits for them, and re-layouts  104 us (18%)
  blocking collectives  64.4 us (11%)
  waiting for transfers between devices  60 us (11%)
  other arithmetic  28.7 us (5%)
  loops' own time  16.2 us (3%)
  starting transfers between devices  12.2 us (2%)
    dot_general x8, matrix products, remap_row(): mixed = jnp.einsum('ijc,fjc->fic', intersection, row_fields, precision=HIGH)  267 us
    unnamed x1, blocking collectives  64.4 us
    all_to_all x1, waiting for transfers between devices, per_device(): lax.all_to_all(moving, 'lev', split_axis=3, concat_axis=2, tiled=True)  54.1 us
    unnamed x23, local copies, waits for them, and re-layouts  43.4 us
    all_to_all x1, other arithmetic, per_device(): lax.all_to_all(moving, 'lev', split_axis=3, concat_axis=2, tiled=True)  17.8 us
    another operation x1, loops' own time, remap_rows(): return jnp.moveaxis(lax.map(one_row, jnp.arange(count)), 0, 1)  16.2 us
    all_to_all x2, local copies, waits for them, and re-layouts, per_device(): lax.all_to_all(moving, 'lev', split_axis=3, concat_axis=2, tiled=True)  14.5 us
    concatenate x1, local copies, waits for them, and re-layouts, per_device(): moving = jnp.concatenate([stepped, thickness[None]], axis=0)  13.2 us
  transfers between devices with their start and end apart: 3, of which 3 were waited for; matrix products, arithmetic and copies ran while one was open for 0% of the time, Pallas kernels for 0%

commit v1 on v0

v1 whole, which is shorter than its diff:
```python
import jax
import jax.numpy as jnp
from jax import lax
from jax.experimental import pallas as pl
from jax.experimental.pallas import tpu as pltpu
from jax.sharding import PartitionSpec as P

F32 = jnp.float32
HIGH = lax.Precision.HIGHEST
ANY = pl.BlockSpec(memory_space=pl.ANY)
SMEM = pl.BlockSpec(memory_space=pltpu.SMEM)
BLOCK = 128
STEP = 8
VMEM_LIMIT = 48 * 1024 * 1024


def cost(flops, nbytes):
    return pl.CostEstimate(flops=flops, bytes_accessed=nbytes, transcendentals=0)


def params():
    return pltpu.CompilerParams(vmem_limit_bytes=VMEM_LIMIT)


def coefs(c):
    sq = 0.5 * c * c
    half = 0.5 * c
    return 1.0 - 2.0 * sq, sq - half, sq + half


def lon_step(x, w):
    n = x.shape[-1]
    mid, up, down = w
    return mid * x + up * pltpu.roll(x, n - 1, 1) + down * pltpu.roll(x, 1, 1)


def prep_kernel(head_in, tail_in, c_head, c_tail, thick, head, tail, t1, t2, t3, sems):
    step = pl.program_id(0)
    me = lax.axis_index("lev")
    width = t1.shape[-1]

    def copies():
        out = []
        for s, dst in enumerate((t1, t2, t3)):
            at = pl.multiple_of(lax.rem(me + s + 1, 4) * width, width)
            out.append(pltpu.make_async_copy(thick.at[:, :, pl.ds(at, width)], dst, sems.at[s]))
        return out

    @pl.when(step == 0)
    def _():
        for c in copies():
            c.start()

    for src, cour, dst in ((head_in, c_head, head), (tail_in, c_tail, tail)):
        w = coefs(cour[0])
        for f in range(src.shape[0]):
            dst[f] = lon_step(src[f, 0], w)

    @pl.when(step == pl.num_programs(0) - 1)
    def _():
        for c in copies():
            c.wait()


def prep(fields, courant_lon, thickness):
    nf, rows, levs, lon = fields.shape
    width = lon // 4
    edge = lambda r: pl.BlockSpec((nf, 1, 8, lon), lambda i: (0, r, i, 0))
    cedge = lambda r: pl.BlockSpec((1, 8, lon), lambda i: (r, i, 0))
    out_edge = pl.BlockSpec((nf, 8, lon), lambda i: (0, i, 0))
    piece = jax.ShapeDtypeStruct((rows, levs, width), F32)
    side = jax.ShapeDtypeStruct((nf, levs, lon), F32)
    return pl.pallas_call(
        prep_kernel,
        grid=(levs // 8,),
        in_specs=[edge(0), edge(rows - 1), cedge(0), cedge(rows - 1), ANY],
        out_specs=[out_edge, out_edge, ANY, ANY, ANY],
        out_shape=[side, side, piece, piece, piece],
        scratch_shapes=[pltpu.SemaphoreType.DMA((3,))],
        compiler_params=params(),
        cost_estimate=cost(10 * 2 * nf * levs * lon, 6 * 1024 * 1024),
        name="prep",
    )(fields, fields, courant_lon, courant_lon, thickness)


def advect_kernel(q, c_lon, c_lat, prev, nxt, o0, o1, o2, o3, keep, sems):
    step = pl.program_id(0)
    last = pl.num_programs(0) - 1
    me = lax.axis_index("lev")
    width = o0.shape[-1]
    nf, rows = q.shape[0], q.shape[1]

    def copies(k):
        out = []
        for s, dst in enumerate((o0, o1, o2, o3)):
            at = pl.multiple_of(lax.rem(me + s, 4) * width, width)
            lev = pl.multiple_of(k * 8, 8)
            out.append(
                pltpu.make_async_copy(
                    keep.at[k, :, :, :, pl.ds(at, width)], dst.at[:, :, pl.ds(lev, 8), :], sems.at[k, s]
                )
            )
        return out

    before = [prev[f] for f in range(nf)]
    w = coefs(c_lon[0])
    here = [lon_step(q[f, 0], w) for f in range(nf)]
    for r in range(rows):
        if r + 1 < rows:
            w = coefs(c_lon[r + 1])
            after = [lon_step(q[f, r + 1], w) for f in range(nf)]
        else:
            after = [nxt[f] for f in range(nf)]
        mid, up, down = coefs(c_lat[r])
        for f in range(nf):
            keep[step, f, r] = mid * here[f] + up * after[f] + down * before[f]
        before, here = here, after
    for c in copies(step):
        c.start()

    @pl.when(step == last)
    def _():
        for k in range(4):
            for c in copies(k):
                c.wait()


def advect(group, fields, c_lon, c_lat, prev, nxt):
    nf, rows, levs, lon = fields.shape
    half = nf // 2
    width = lon // 4
    steps = levs // 8
    cspec = pl.BlockSpec((rows, 8, lon), lambda i: (0, i, 0))
    hspec = pl.BlockSpec((half, 8, lon), lambda i: (group, i, 0))
    piece = jax.ShapeDtypeStruct((half, rows, levs, width), F32)
    return pl.pallas_call(
        advect_kernel,
        grid=(steps,),
        in_specs=[pl.BlockSpec((half, rows, 8, lon), lambda i: (group, 0, i, 0)), cspec, cspec, hspec, hspec],
        out_specs=[ANY] * 4,
        out_shape=[piece] * 4,
        scratch_shapes=[pltpu.VMEM((steps, half, rows, 8, lon), F32), pltpu.SemaphoreType.DMA((steps, 4))],
        compiler_params=params(),
        cost_estimate=cost(25 * half * rows * levs * lon, 7 * 1024 * 1024),
        name="advect",
    )(fields, c_lon, c_lat, prev, nxt)


def edges_kernel(own, r1, r2, r3, e_ref, lo_ref, n_ref, col):
    r = pl.program_id(0)
    me = lax.axis_index("lev")
    quarter = own.shape[1]
    levels = 4 * quarter
    for s, src in enumerate((own, r1, r2, r3)):
        at = pl.multiple_of(lax.rem(me + 4 - s, 4) * quarter, quarter)
        col[pl.ds(at, quarter), :] = src[0]
    i = lax.broadcasted_iota(jnp.int32, (levels, levels), 0)
    j = lax.broadcasted_iota(jnp.int32, (levels, levels), 1)
    lower = (i >= j).astype(F32)
    upper = jnp.dot(lower, col[...], precision=HIGH, preferred_element_type=F32)
    e = upper * (levels / upper[levels - 1 :, :])
    e_ref[0] = e
    first = jnp.min(e, axis=1, keepdims=True)
    final = jnp.max(e, axis=1, keepdims=True)
    start = (lax.broadcasted_iota(jnp.int32, (levels, BLOCK), 1) * 8).astype(F32)
    lo = jnp.sum((final <= start).astype(F32), axis=0, keepdims=True)
    hi = jnp.sum((first < start + 8.0).astype(F32), axis=0, keepdims=True)
    lo = jnp.minimum(lo, levels - 1.0).astype(jnp.int32)
    hi = jnp.minimum(hi, levels - 1.0).astype(jnp.int32)
    n = lax.shift_right_logical(hi - lo + STEP, 3)
    lo_ref[0] = jnp.maximum(jnp.minimum(lo, levels - STEP * n), 0)
    n_ref[0] = n


def edges(own, r1, r2, r3):
    rows, quarter, _ = own.shape
    width = r1.shape[-1]
    levels = 4 * quarter
    mine = lax.dynamic_slice_in_dim(own, lax.axis_index("lev") * width, width, 2)
    spec = pl.BlockSpec((1, quarter, width), lambda r: (r, 0, 0))
    bound = jax.ShapeDtypeStruct((rows, 1, BLOCK), jnp.int32)
    bspec = pl.BlockSpec((1, 1, BLOCK), lambda r: (r, 0, 0))
    return pl.pallas_call(
        edges_kernel,
        grid=(rows,),
        in_specs=[spec] * 4,
        out_specs=[pl.BlockSpec((1, levels, width), lambda r: (r, 0, 0)), bspec, bspec],
        out_shape=[jax.ShapeDtypeStruct((rows, levels, width), F32), bound, bound],
        scratch_shapes=[pltpu.VMEM((levels, width), F32)],
        compiler_params=params(),
        cost_estimate=cost(12 * rows * levels * levels * width, 2 * 1024 * 1024),
        name="edges",
    )(mine, r1, r2, r3)


def remap_row(r, lo_ref, n_ref, e_ref, pieces, cols, out):
    me = lax.axis_index("lev")
    nf = cols.shape[0]
    width = cols.shape[2]
    quarter = pieces[0].shape[2]
    for s, src in enumerate(pieces):
        at = pl.multiple_of(lax.rem(me + 4 - s, 4) * quarter, quarter)
        for f in range(nf):
            cols[f, pl.ds(at, quarter), :] = src[f, 0]
    level = lax.broadcasted_iota(jnp.int32, (8, width), 0)
    groups = 4 * quarter // 8

    def group(g, _):
        index = (level + g * 8).astype(F32)
        lo = lo_ref[r, 0, g]

        def some(k, carry):
            old = carry[0]
            accs = list(carry[1:])
            j0 = lo + k * STEP
            for t in range(STEP):
                u = jnp.minimum(jnp.maximum(e_ref[0, pl.ds(j0 + t, 1), :] - index, 0.0), 1.0)
                w = u - old
                old = u
                for f in range(nf):
                    accs[f] = accs[f] + w * cols[f, pl.ds(j0 + t, 1), :]
            return (old, *accs)

        zero = jnp.zeros((8, width), F32)
        res = lax.fori_loop(0, n_ref[r, 0, g], some, (zero,) * (nf + 1))
        at = pl.multiple_of(g * 8, 8)
        for f in range(nf):
            out[f, 0, pl.ds(at, 8), :] = res[1 + f]
        return 0

    lax.fori_loop(0, groups, group, 0)


def heat_kernel(
    lo_ref, n_ref, own_ref, day_ref, e_ref, p0, p1, p2, p3, exch, solar, out, heating, shares, cols
):
    r = pl.program_id(0)
    remap_row(r, lo_ref, n_ref, e_ref, (p0, p1, p2, p3), cols, out)
    temp = out[0, 0]
    hum = out[1, 0]
    levels, width = temp.shape
    square = hum * hum
    clear = 1.0 / (1.0 + square)
    absorb = square * clear
    heat = jnp.dot(exch[0], absorb * temp, precision=HIGH, preferred_element_type=F32)
    heat = heat + jnp.dot(exch[1], clear * temp, precision=HIGH, preferred_element_type=F32)
    lane = lax.broadcasted_iota(jnp.int32, (1, width), 1)
    d0 = jnp.full((1, width), day_ref[2 * r], jnp.int32)
    d1 = jnp.full((1, width), day_ref[2 * r + 1], jnp.int32)
    day = jnp.where(lane < BLOCK, d0, d1).astype(F32)
    heat = heat + (day * solar[...]) * clear
    heating[0] = heat
    total = jnp.sum(heat, axis=0, keepdims=True)
    line = lax.broadcasted_iota(jnp.int32, (1, BLOCK), 1)

    @pl.when(r == 0)
    def _():
        shares[...] = jnp.zeros_like(shares)

    acc = shares[...]
    for b in range(2):
        mean = jnp.sum(total[:, b * BLOCK : (b + 1) * BLOCK], axis=1, keepdims=True) * (1.0 / (levels * BLOCK))
        acc = acc + jnp.where(line == own_ref[2 * r + b], mean, 0.0)
    shares[...] = acc


def remap_kernel(lo_ref, n_ref, e_ref, p0, p1, p2, p3, base, out, cols):
    remap_row(pl.program_id(0), lo_ref, n_ref, e_ref, (p0, p1, p2, p3), cols, out)


def remap(group, lo, n, e, pieces, base=None, heat_args=None):
    half, rows, quarter, width = pieces[0].shape
    levels = 4 * quarter
    espec = pl.BlockSpec((1, levels, width), lambda r: (r, 0, 0))
    pspec = pl.BlockSpec((half, 1, quarter, width), lambda r: (0, r, 0, 0))
    ospec = pl.BlockSpec((half, 1, levels, width), lambda r: (group, r, 0, 0))
    full = jax.ShapeDtypeStruct((2 * half, rows, levels, width), F32)
    common = dict(
        grid=(rows,),
        scratch_shapes=[pltpu.VMEM((half, levels, width), F32)],
        compiler_params=params(),
    )
    if heat_args is None:
        return pl.pallas_call(
            remap_kernel,
            in_specs=[SMEM, SMEM, espec] + [pspec] * 4 + [ANY],
            out_specs=ospec,
            out_shape=full,
            input_output_aliases={7: 0},
            cost_estimate=cost(200 * half * rows * levels * width, 5 * 1024 * 1024),
            name="remap",
            **common,
        )(lo, n, e, *pieces, base)
    owners, day, exchange, solar = heat_args
    hspec = pl.BlockSpec((1, levels, width), lambda r: (r, 0, 0))
    return pl.pallas_call(
        heat_kernel,
        in_specs=[SMEM, SMEM, SMEM, SMEM, espec]
        + [pspec] * 4
        + [pl.BlockSpec((2, levels, levels), lambda r: (0, 0, 0)), pl.BlockSpec((levels, 1), lambda r: (0, 0))],
        out_specs=[ospec, hspec, pl.BlockSpec((1, BLOCK), lambda r: (0, 0))],
        out_shape=[full, jax.ShapeDtypeStruct((rows, levels, width), F32), jax.ShapeDtypeStruct((1, BLOCK), F32)],
        cost_estimate=cost(300 * half * rows * levels * width, 7 * 1024 * 1024),
        name="heat",
        **common,
    )(lo, n, owners, day, e, *pieces, exchange, solar)


def per_device(fields, thickness, courant_lon, courant_lat, exchange, solar_profile, owners, daylight):
    count = lax.axis_size("lat")
    ends = count - 1
    turn = lambda s: [(i, (i + s) % 4) for i in range(4)]
    around = lambda ps: [ps[0]] + [lax.ppermute(p, "lev", turn(s + 1)) for s, p in enumerate(ps[1:])]

    head, tail, t1, t2, t3 = prep(fields, courant_lon, thickness)
    prev = lax.ppermute(tail, "lat", [(i, i + 1) for i in range(ends)])
    nxt = lax.ppermute(head, "lat", [(i + 1, i) for i in range(ends)])
    thick = around([thickness, t1, t2, t3])
    e, lo, n = edges(*thick)
    first = around(advect(0, fields, courant_lon, courant_lat, prev, nxt))
    second = around(advect(1, fields, courant_lon, courant_lat, prev, nxt))
    heat_args = (owners[:, 0], daylight, exchange, solar_profile[:, None])
    remapped, heating, shares = remap(0, lo, n, e, first, heat_args=heat_args)
    remapped = remap(1, lo, n, e, second, base=remapped)
    shares = shares[0, :count].reshape(count, 1, 1)
    owner_heat = jnp.sum(lax.all_to_all(shares, "lat", split_axis=0, concat_axis=0, tiled=True)).reshape(1, 1)
    return (remapped, heating, owner_heat)


def solution(mesh):
    placed = (
        P(None, "lat", "lev", None),
        P("lat", "lev", None),
        P("lat", "lev", None),
        P("lat", "lev", None),
        P(),
        P(),
        P(("lat", "lev"), None),
        P(("lat", "lev")),
    )
    return jax.shard_map(
        per_device,
        mesh=mesh,
        in_specs=placed,
        out_specs=(P(None, "lat", None, "lev"), P("lat", None, "lev"), P("lat", "lev")),
        check_vma=False,
    )
```

time: 569 us -> 120 us (0.21)
  matrix products: 279 us -> 0 us
  local copies, waits for them, and re-layouts: 104 us -> 12.1 us
  blocking collectives: 64.4 us -> 0 us
  Pallas kernels: 0 us -> 43.1 us
  waiting for transfers between devices: 60 us -> 22 us
  starting transfers between devices: 12.2 us -> 40.6 us
  other arithmetic: 28.7 us -> 0.63 us
  loops' own time: 16.2 us -> 0 us
    dot_general x18 -> x0, matrix products: 279 us -> none  [the longest x8 267 us: remap_row(): mixed = jnp.einsum('ijc,fjc->fic', intersection, row_fields, precision=HIGH)]
    unnamed x1 -> x0, blocking collectives: 64.4 us -> none
    all_to_all x1, waiting for transfers between devices: 54.1 us -> 0.01 us  [per_device(): lax.all_to_all(shares, 'lat', split_axis=0, concat_axis=0, tiled=True)]
    pallas_call x0 -> x6, Pallas kernels: none -> 43.1 us  [the longest x1 15.8 us: remap(): pl.pallas_call(heat_kernel, in_specs=[SMEM, SMEM, SMEM, SMEM, espec] + [p...]
    unnamed x23 -> x34, local copies, waits for them, and re-layouts: 43.4 us -> 10.3 us
    ppermute x2 -> x11, starting transfers between devices: 6.86 us -> 25 us  [the longest x9 18.1 us: per_device(): lax.ppermute(p, 'lev', turn(s + 1))]
    all_to_all x1 -> x0, other arithmetic: 17.8 us -> none  [per_device(): lax.all_to_all(moving, 'lev', split_axis=3, concat_axis=2, tiled=True)]
    another operation x1 -> x0, loops' own time: 16.2 us -> none  [remap_rows(): return jnp.moveaxis(lax.map(one_row, jnp.arange(count)), 0, 1)]
  transfers between devices with their start and end apart: 3 -> 12, of which waited for: 3 -> 3; matrix products, arithmetic and copies ran while one was open for 0% -> 1% of each run, Pallas kernels for 0% -> 30%
where the time goes in v1:
time: 120 us; the launch traced here: 119 us
  Pallas kernels  43.1 us (36%)
  starting transfers between devices  40.6 us (34%)
  waiting for transfers between devices  22 us (18%)
  local copies, waits for them, and re-layouts  12.1 us (10%)
    ppermute x9, starting transfers between devices, per_device(): lax.ppermute(p, 'lev', turn(s + 1))  18.1 us
    pallas_call x1, Pallas kernels, remap(): pl.pallas_call(heat_kernel, in_specs=[SMEM, SMEM, SMEM, SMEM, espec] + [p...  15.8 us
    all_to_all x1, starting transfers between devices, per_device(): lax.all_to_all(shares, 'lat', split_axis=0, concat_axis=0, tiled=True)  15.7 us
    ppermute x9, waiting for transfers between devices, per_device(): lax.ppermute(p, 'lev', turn(s + 1))  13.4 us
    pallas_call x1, Pallas kernels, remap(): pl.pallas_call(remap_kernel, in_specs=[SMEM, SMEM, espec] + [pspec] * 4 +...  11.8 us
    unnamed x34, local copies, waits for them, and re-layouts  10.3 us
    pallas_call x2, Pallas kernels, advect(): pl.pallas_call(advect_kernel, grid=(steps,), in_specs=[pl.BlockSpec((half...  9.3 us
    ppermute x1, starting transfers between devices, per_device(): prev = lax.ppermute(tail, 'lat', [(i, i + 1) for i in range(ends)])  4.94 us
  transfers between devices with their start and end apart: 12, of which 3 were waited for; matrix products, arithmetic and copies ran while one was open for 1% of the time, Pallas kernels for 30%

profile of v1, /device:TPU:1, one launch (start us, length us, event | category | flops | bytes accessed | tf_op | source)
XLA Modules:
  0.0 119.2 jit_solution(6507179442884951487)
XLA Ops:
  0.6 1.2 %copy-done = f32[8,32,1024]{2,1,0:T(8,128)S(1)} copy-done((f32[8,32,1024]{2,1,0:T(8,128)S(1)}, f32[8,32,1024]{2,1,0:T(8,128)}, u32[]{:S(2)}) %copy-start) | copy-done | bytes 1048600
  1.9 1.2 %copy-done.2 = f32[8,32,1024]{2,1,0:T(8,128)S(1)} copy-done((f32[8,32,1024]{2,1,0:T(8,128)S(1)}, f32[8,32,1024]{2,1,0:T(8,128)}, u32[]{:S(2)}) %copy-start.2) | copy-done | bytes 1048600
  3.1 2.9 %prep.1 = (f32[4,32,1024]{2,1,0:T(8,128)S(1)}, f32[4,32,1024]{2,1,0:T(8,128)S(1)}, f32[8,32,256]{2,1,0:T(8,128)S(1)}, f32[8,32,256]{2,1,0:T(8,128)S(1)}, f32[8,32,256]{2,1,0:T(8,128)S(1)}) custom-call(f32[4,8,32,1024]{3,2,1,0:T(8,128)} %q.3, f32[4,8,32,1024]{3,2,1,0:T(8,128)} %q.3, f32[8,32,1024]{2,1,0:T(8,128)S(1)} %copy-done, f32[8,32,1024]{2,1,0:T(8,128)S(1)} %copy-done, ...), custom_call_target="tpu_custom_call" | custom-call | flops 2621440 | bytes 6291456 | tf_op jit(solution)/shard_map/prep/pallas_call | solution.py:73
  6.0 4.9 %collective-permute-start.3 = (f32[4,32,1024]{2,1,0:T(8,128)S(1)}, f32[4,32,1024]{2,1,0:T(8,128)S(1)}, u32[]{:S(2)}, u32[]{:S(2)}) collective-permute-start(f32[4,32,1024]{2,1,0:T(8,128)S(1)} %get-tuple-element.28), channel_id=1, source_target_pairs={{0,4},{4,8},{8,12},{12,16},{16,20},{20,24},{24,28},{28,32},{32,36}... | collective-permute-start | bytes 1572872 | tf_op jit(solution)/shard_map/ppermute | solution.py:316
  10.9 1.9 %collective-permute-start.4 = (f32[4,32,1024]{2,1,0:T(8,128)S(1)}, f32[4,32,1024]{2,1,0:T(8,128)S(1)}, u32[]{:S(2)}, u32[]{:S(2)}) collective-permute-start(f32[4,32,1024]{2,1,0:T(8,128)S(1)} %get-tuple-element.29), channel_id=1, source_target_pairs={{4,0},{8,4},{12,8},{16,12},{20,16},{24,20},{28,24},{32,28},{36,32}... | collective-permute-start | bytes 1572872 | tf_op jit(solution)/shard_map/ppermute | solution.py:317
  12.9 4.2 %collective-permute-done.3.prev = f32[4,32,1024]{2,1,0:T(8,128)S(1)} collective-permute-done((f32[4,32,1024]{2,1,0:T(8,128)S(1)}, f32[4,32,1024]{2,1,0:T(8,128)S(1)}, u32[]{:S(2)}, u32[]{:S(2)}) %collective-permute-start.3) | collective-permute-done | bytes 524320 | tf_op jit(solution)/shard_map/ppermute | solution.py:316
  17.0 4.4 %collective-permute-done.4.nxt = f32[4,32,1024]{2,1,0:T(8,128)S(1)} collective-permute-done((f32[4,32,1024]{2,1,0:T(8,128)S(1)}, f32[4,32,1024]{2,1,0:T(8,128)S(1)}, u32[]{:S(2)}, u32[]{:S(2)}) %collective-permute-start.4) | collective-permute-done | bytes 524320 | tf_op jit(solution)/shard_map/ppermute | solution.py:317
  21.4 4.6 %advect.3 = (f32[2,8,32,256]{3,2,1,0:T(8,128)S(1)}, f32[2,8,32,256]{3,2,1,0:T(8,128)S(1)}, f32[2,8,32,256]{3,2,1,0:T(8,128)}, f32[2,8,32,256]{3,2,1,0:T(8,128)}) custom-call(f32[4,8,32,1024]{3,2,1,0:T(8,128)} %q.3, f32[8,32,1024]{2,1,0:T(8,128)S(1)} %copy-done, f32[8,32,1024]{2,1,0:T(8,128)S(1)} %copy-done.1, ...), custom_call_target="tpu_custom_call" | custom-call | flops 13107200 | bytes 7340032 | tf_op jit(solution)/shard_map/advect/pallas_call | solution.py:136
  26.1 0.0 copy-start.3
  26.1 0.0 copy-start.16
  26.1 1.4 %collective-permute-start.8 = (f32[2,8,32,256]{3,2,1,0:T(8,128)S(1)}, f32[2,8,32,256]{3,2,1,0:T(8,128)S(1)}, u32[]{:S(2)}, u32[]{:S(2)}) collective-permute-start(f32[2,8,32,256]{3,2,1,0:T(8,128)S(1)} %get-tuple-element.35), channel_id=1, source_target_pairs={{0,1},{1,2},{2,3},{3,0},{4,5},{5,6},{6,7},{7,4},{8,9},{9,10},{10,1... | collective-permute-start | bytes 1572872 | tf_op jit(solution)/shard_map/ppermute | solution.py:313
  27.5 1.3 %collective-permute-start = (f32[8,32,256]{2,1,0:T(8,128)S(1)}, f32[8,32,256]{2,1,0:T(8,128)S(1)}, u32[]{:S(2)}, u32[]{:S(2)}) collective-permute-start(f32[8,32,256]{2,1,0:T(8,128)S(1)} %get-tuple-element.22), channel_id=1, source_target_pairs={{0,1},{1,2},{2,3},{3,0},{4,5},{5,6},{6,7},{7,4},{8,9},{9,10},{10,1... | collective-permute-start | bytes 786440 | tf_op jit(solution)/shard_map/ppermute | solution.py:313
  28.8 1.4 %collective-permute-start.1 = (f32[8,32,256]{2,1,0:T(8,128)S(1)}, f32[8,32,256]{2,1,0:T(8,128)S(1)}, u32[]{:S(2)}, u32[]{:S(2)}) collective-permute-start(f32[8,32,256]{2,1,0:T(8,128)S(1)} %get-tuple-element.23), channel_id=1, source_target_pairs={{0,2},{1,3},{2,0},{3,1},{4,6},{5,7},{6,4},{7,5},{8,10},{9,11},{10,... | collective-permute-start | bytes 786440 | tf_op jit(solution)/shard_map/ppermute | solution.py:313
  30.2 2.0 %collective-permute-start.2 = (f32[8,32,256]{2,1,0:T(8,128)S(1)}, f32[8,32,256]{2,1,0:T(8,128)S(1)}, u32[]{:S(2)}, u32[]{:S(2)}) collective-permute-start(f32[8,32,256]{2,1,0:T(8,128)S(1)} %get-tuple-element.24), channel_id=1, source_target_pairs={{0,3},{1,0},{2,1},{3,2},{4,7},{5,4},{6,5},{7,6},{8,11},{9,8},{10,9... | collective-permute-start | bytes 786440 | tf_op jit(solution)/shard_map/ppermute | solution.py:313
  32.2 0.3 collective-permute-start.9
  32.5 13.4 %collective-permute-done.r1 = f32[8,32,256]{2,1,0:T(8,128)S(1)} collective-permute-done((f32[8,32,256]{2,1,0:T(8,128)S(1)}, f32[8,32,256]{2,1,0:T(8,128)S(1)}, u32[]{:S(2)}, u32[]{:S(2)}) %collective-permute-start) | collective-permute-done | bytes 262176 | tf_op jit(solution)/shard_map/ppermute | solution.py:313
  45.9 0.7 copy-done.10
  46.6 2.8 %collective-permute-start.10 = (f32[2,8,32,256]{3,2,1,0:T(8,128)}, f32[2,8,32,256]{3,2,1,0:T(8,128)}, u32[]{:S(2)}, u32[]{:S(2)}) collective-permute-start(f32[2,8,32,256]{3,2,1,0:T(8,128)} %get-tuple-element.37), channel_id=1, source_target_pairs={{0,3},{1,0},{2,1},{3,2},{4,7},{5,4},{6,5},{7,6},{8,11},{9,8},{10,9... | collective-permute-start | bytes 1572872 | tf_op jit(solution)/shard_map/ppermute | solution.py:313
  49.3 4.7 %advect.2 = (f32[2,8,32,256]{3,2,1,0:T(8,128)S(1)}, f32[2,8,32,256]{3,2,1,0:T(8,128)}, f32[2,8,32,256]{3,2,1,0:T(8,128)}, f32[2,8,32,256]{3,2,1,0:T(8,128)}) custom-call(f32[4,8,32,1024]{3,2,1,0:T(8,128)} %q.3, f32[8,32,1024]{2,1,0:T(8,128)S(1)} %copy-done, f32[8,32,1024]{2,1,0:T(8,128)S(1)} %copy-done.1, f32[4,32,1024]{2,1,0:T(8,128)S(1)} %collective-permute-done.3.prev, ...), custom_call_target="tpu_custom_call" | custom-call | flops 13107200 | bytes 7340032 | tf_op jit(solution)/shard_map/advect/pallas_call | solution.py:136
  54.0 0.0 collective-permute-done.1.r2
  54.0 0.0 copy-start.12
  54.0 0.7 copy-done.12
  54.7 3.7 %collective-permute-start.5 = (f32[2,8,32,256]{3,2,1,0:T(8,128)}, f32[2,8,32,256]{3,2,1,0:T(8,128)S(1)}, u32[]{:S(2)}, u32[]{:S(2)}) collective-permute-start(f32[2,8,32,256]{3,2,1,0:T(8,128)} %get-tuple-element.31), channel_id=1, source_target_pairs={{0,1},{1,2},{2,3},{3,0},{4,5},{5,6},{6,7},{7,4},{8,9},{9,10},{10,1... | collective-permute-start | bytes 1572872 | tf_op jit(solution)/shard_map/ppermute | solution.py:313
  58.5 0.0 collective-permute-done.2.r3
  58.5 0.7 copy-done.14
  59.2 4.5 %collective-permute-start.6 = (f32[2,8,32,256]{3,2,1,0:T(8,128)}, f32[2,8,32,256]{3,2,1,0:T(8,128)S(1)}, u32[]{:S(2)}, u32[]{:S(2)}) collective-permute-start(f32[2,8,32,256]{3,2,1,0:T(8,128)} %get-tuple-element.32), channel_id=1, source_target_pairs={{0,2},{1,3},{2,0},{3,1},{4,6},{5,7},{6,4},{7,5},{8,10},{9,11},{10,... | collective-permute-start | bytes 1572872 | tf_op jit(solution)/shard_map/ppermute | solution.py:313
  63.7 0.0 collective-permute-done.8.p1
  63.7 0.8 copy-done.5
  64.5 0.7 collective-permute-start.7
  65.2 0.1 copy.13.solar
  65.3 1.0 constant_dynamic-slice_fusion.own
  66.3 0.9 copy-done.11
  67.2 0.9 copy-done.13
  68.2 0.9 copy-done.15
  69.1 3.3 %edges.1 = (f32[8,128,256]{2,1,0:T(8,128)S(1)}, s32[8,1,128]{2,1,0:T(1,128)S(1)}, s32[8,1,128]{2,1,0:T(1,128)S(1)}) custom-call(f32[8,32,256]{2,1,0:T(8,128)S(1)} %constant_dynamic-slice_fusion.own, f32[8,32,256]{2,1,0:T(8,128)S(1)} %copy-done.11, f32[8,32,256]{2,1,0:T(8,128)S(1)} %copy-done.13, f32[8,32,256]{2,1,0:T(8,128)S(1)} %copy-done.15), custom_call_target="tpu_custom_call" | custom-call | flops 402653184 | bytes 2097152 | tf_op jit(solution)/shard_map/edges/pallas_call | solution.py:183
  72.5 0.0 collective-permute-done.9.p2
  72.5 0.0 collective-permute-done.10.p3
  72.5 1.0 copy-done.4
  73.6 1.0 copy-done.6
  74.6 15.8 %heat.1 = (f32[4,8,128,256]{3,2,1,0:T(8,128)}, f32[8,128,256]{2,1,0:T(8,128)}, f32[1,128]{1,0:T(1,128)S(1)}) custom-call(s32[8,1,128]{2,1,0:T(1,128)S(1)} %get-tuple-element.25.lo_ref, s32[8,1,128]{2,1,0:T(1,128)S(1)} %get-tuple-element.26.n_ref, s32[16]{0:T(128)S(1)} %bitcast.5, s32[16]{0:T(128)S(1)} %copy-done.9, ...), custom_call_target="tpu_custom_call" | custom-call | flops 157286400 | bytes 7340032 | tf_op jit(solution)/shard_map/heat/pallas_call | solution.py:296
  90.4 0.7 copy.14
  91.1 15.7 %all-to-all-start = ((f32[32,1,1]{2,1,0:T(1,128)}), f32[32,1,1]{2,1,0:T(1,128)S(1)}, u32[]{:S(2)}, u32[]{:S(2)}) async-start(f32[32,1,1]{2,1,0:T(1,128)} %copy.14), calls=%async_computation | async-start | bytes 32768 | tf_op jit(solution)/shard_map/all_to_all | solution.py:326
  106.7 0.0 collective-permute-done.5.p1
  106.8 0.0 collective-permute-done.6.p2
  106.8 0.0 collective-permute-done.7.p3
  106.8 11.8 %remap.1 = f32[4,8,128,256]{3,2,1,0:T(8,128)} custom-call(s32[8,1,128]{2,1,0:T(1,128)S(1)} %get-tuple-element.25.lo_ref, s32[8,1,128]{2,1,0:T(1,128)S(1)} %get-tuple-element.26.n_ref, f32[8,128,256]{2,1,0:T(8,128)S(1)} %get-tuple-element.27.e_ref, f32[2,8,32,256]{3,2,1,0:T(8,128)S(1)} %get-tuple-element.30.p0, ...), custom_call_target="tpu_custom_call", output_to_operand_aliasing={{}: (7, {})} | custom-call | flops 104857600 | bytes 5242880 | tf_op jit(solution)/shard_map/remap/pallas_call | solution.py:284
  118.6 0.0 all-to-all-done
  118.6 0.6 reduce_sum.9
  (21 shorter events, 0.0 us)
Async XLA Ops:
  0.6 1.2 %copy-start = (f32[8,32,1024]{2,1,0:T(8,128)S(1)}, f32[8,32,1024]{2,1,0:T(8,128)}, u32[]{:S(2)}) copy-start(f32[8,32,1024]{2,1,0:T(8,128)} %c_lon.3) | copy-start | bytes 3145732
  1.9 1.2 %copy-start.2 = (f32[8,32,1024]{2,1,0:T(8,128)S(1)}, f32[8,32,1024]{2,1,0:T(8,128)}, u32[]{:S(2)}) copy-start(f32[8,32,1024]{2,1,0:T(8,128)} %thick.1) | copy-start | bytes 3145732
  3.1 18.4 %copy-start.1 = (f32[8,32,1024]{2,1,0:T(8,128)S(1)}, f32[8,32,1024]{2,1,0:T(8,128)}, u32[]{:S(2)}) copy-start(f32[8,32,1024]{2,1,0:T(8,128)} %c_lat.3) | copy-start | bytes 3145732
  6.0 11.0 %collective-permute-start.3 = (f32[4,32,1024]{2,1,0:T(8,128)S(1)}, f32[4,32,1024]{2,1,0:T(8,128)S(1)}, u32[]{:S(2)}, u32[]{:S(2)}) collective-permute-start(f32[4,32,1024]{2,1,0:T(8,128)S(1)} %get-tuple-element.28), channel_id=1, source_target_pairs={{0,4},{4,8},{8,12},{12,16},{16,20},{20,24},{24,28},{28,32},{32,36}... | collective-permute-start | bytes 1572872 | tf_op jit(solution)/shard_map/ppermute | solution.py:316
  10.9 10.5 %collective-permute-start.4 = (f32[4,32,1024]{2,1,0:T(8,128)S(1)}, f32[4,32,1024]{2,1,0:T(8,128)S(1)}, u32[]{:S(2)}, u32[]{:S(2)}) collective-permute-start(f32[4,32,1024]{2,1,0:T(8,128)S(1)} %get-tuple-element.29), channel_id=1, source_target_pairs={{4,0},{8,4},{12,8},{16,12},{20,16},{24,20},{28,24},{32,28},{36,32}... | collective-permute-start | bytes 1572872 | tf_op jit(solution)/shard_map/ppermute | solution.py:317
  26.1 37.6 %copy-start.3 = (f32[2,8,32,256]{3,2,1,0:T(8,128)}, f32[2,8,32,256]{3,2,1,0:T(8,128)S(1)}, u32[]{:S(2)}) copy-start(f32[2,8,32,256]{3,2,1,0:T(8,128)S(1)} %get-tuple-element.34.p0) | copy-start | bytes 1572868
  26.1 39.1 %copy-start.16 = (f32[128]{0:T(128)S(1)}, f32[128]{0:T(128)}, u32[]{:S(2)}) copy-start(f32[128]{0:T(128)} %param.13) | copy-start | bytes 1540
  26.1 37.6 %collective-permute-start.8 = (f32[2,8,32,256]{3,2,1,0:T(8,128)S(1)}, f32[2,8,32,256]{3,2,1,0:T(8,128)S(1)}, u32[]{:S(2)}, u32[]{:S(2)}) collective-permute-start(f32[2,8,32,256]{3,2,1,0:T(8,128)S(1)} %get-tuple-element.35), channel_id=1, source_target_pairs={{0,1},{1,2},{2,3},{3,0},{4,5},{5,6},{6,7},{7,4},{8,9},{9,10},{10,1... | collective-permute-start | bytes 1572872 | tf_op jit(solution)/shard_map/ppermute | solution.py:313
  27.5 18.4 %collective-permute-start = (f32[8,32,256]{2,1,0:T(8,128)S(1)}, f32[8,32,256]{2,1,0:T(8,128)S(1)}, u32[]{:S(2)}, u32[]{:S(2)}) collective-permute-start(f32[8,32,256]{2,1,0:T(8,128)S(1)} %get-tuple-element.22), channel_id=1, source_target_pairs={{0,1},{1,2},{2,3},{3,0},{4,5},{5,6},{6,7},{7,4},{8,9},{9,10},{10,1... | collective-permute-start | bytes 786440 | tf_op jit(solution)/shard_map/ppermute | solution.py:313
  28.8 25.2 %collective-permute-start.1 = (f32[8,32,256]{2,1,0:T(8,128)S(1)}, f32[8,32,256]{2,1,0:T(8,128)S(1)}, u32[]{:S(2)}, u32[]{:S(2)}) collective-permute-start(f32[8,32,256]{2,1,0:T(8,128)S(1)} %get-tuple-element.23), channel_id=1, source_target_pairs={{0,2},{1,3},{2,0},{3,1},{4,6},{5,7},{6,4},{7,5},{8,10},{9,11},{10,... | collective-permute-start | bytes 786440 | tf_op jit(solution)/shard_map/ppermute | solution.py:313
  30.2 28.3 %collective-permute-start.2 = (f32[8,32,256]{2,1,0:T(8,128)S(1)}, f32[8,32,256]{2,1,0:T(8,128)S(1)}, u32[]{:S(2)}, u32[]{:S(2)}) collective-permute-start(f32[8,32,256]{2,1,0:T(8,128)S(1)} %get-tuple-element.24), channel_id=1, source_target_pairs={{0,3},{1,0},{2,1},{3,2},{4,7},{5,4},{6,5},{7,6},{8,11},{9,8},{10,9... | collective-permute-start | bytes 786440 | tf_op jit(solution)/shard_map/ppermute | solution.py:313
  32.2 40.3 %collective-permute-start.9 = (f32[2,8,32,256]{3,2,1,0:T(8,128)}, f32[2,8,32,256]{3,2,1,0:T(8,128)}, u32[]{:S(2)}, u32[]{:S(2)}) collective-permute-start(f32[2,8,32,256]{3,2,1,0:T(8,128)} %get-tuple-element.36), channel_id=1, source_target_pairs={{0,2},{1,3},{2,0},{3,1},{4,6},{5,7},{6,4},{7,5},{8,10},{9,11},{10,... | collective-permute-start | bytes 1572872 | tf_op jit(solution)/shard_map/ppermute | solution.py:313
  45.9 0.7 copy-start.10
  46.6 25.9 %copy-start.7 = (f32[2,128,128]{2,1,0:T(8,128)S(1)}, f32[2,128,128]{2,1,0:T(8,128)}, u32[]{:S(2)}) copy-start(f32[2,128,128]{2,1,0:T(8,128)} %exch.1) | copy-start | bytes 393220
  46.6 25.9 %copy-start.8 = (s32[16,1]{0,1:T(1,128)S(1)}, s32[16,1]{0,1:T(1,128)}, u32[]{:S(2)}) copy-start(s32[16,1]{0,1:T(1,128)} %param.14) | copy-start | bytes 196
  46.6 25.9 %copy-start.9 = (s32[16]{0:T(128)S(1)}, s32[16]{0:T(128)}, u32[]{:S(2)}) copy-start(s32[16]{0:T(128)} %day_ref.1) | copy-start | bytes 196
  46.6 25.9 %collective-permute-start.10 = (f32[2,8,32,256]{3,2,1,0:T(8,128)}, f32[2,8,32,256]{3,2,1,0:T(8,128)}, u32[]{:S(2)}, u32[]{:S(2)}) collective-permute-start(f32[2,8,32,256]{3,2,1,0:T(8,128)} %get-tuple-element.37), channel_id=1, source_target_pairs={{0,3},{1,0},{2,1},{3,2},{4,7},{5,4},{6,5},{7,6},{8,11},{9,8},{10,9... | collective-permute-start | bytes 1572872 | tf_op jit(solution)/shard_map/ppermute | solution.py:313
  54.0 0.7 copy-start.12
  54.7 52.0 %collective-permute-start.5 = (f32[2,8,32,256]{3,2,1,0:T(8,128)}, f32[2,8,32,256]{3,2,1,0:T(8,128)S(1)}, u32[]{:S(2)}, u32[]{:S(2)}) collective-permute-start(f32[2,8,32,256]{3,2,1,0:T(8,128)} %get-tuple-element.31), channel_id=1, source_target_pairs={{0,1},{1,2},{2,3},{3,0},{4,5},{5,6},{6,7},{7,4},{8,9},{9,10},{10,1... | collective-permute-start | bytes 1572872 | tf_op jit(solution)/shard_map/ppermute | solution.py:313
  58.5 0.7 copy-start.14
  59.2 47.6 %collective-permute-start.6 = (f32[2,8,32,256]{3,2,1,0:T(8,128)}, f32[2,8,32,256]{3,2,1,0:T(8,128)S(1)}, u32[]{:S(2)}, u32[]{:S(2)}) collective-permute-start(f32[2,8,32,256]{3,2,1,0:T(8,128)} %get-tuple-element.32), channel_id=1, source_target_pairs={{0,2},{1,3},{2,0},{3,1},{4,6},{5,7},{6,4},{7,5},{8,10},{9,11},{10,... | collective-permute-start | bytes 1572872 | tf_op jit(solution)/shard_map/ppermute | solution.py:313
  63.7 0.8 copy-start.5
  64.5 42.3 %collective-permute-start.7 = (f32[2,8,32,256]{3,2,1,0:T(8,128)}, f32[2,8,32,256]{3,2,1,0:T(8,128)S(1)}, u32[]{:S(2)}, u32[]{:S(2)}) collective-permute-start(f32[2,8,32,256]{3,2,1,0:T(8,128)} %get-tuple-element.33), channel_id=1, source_target_pairs={{0,3},{1,0},{2,1},{3,2},{4,7},{5,4},{6,5},{7,6},{8,11},{9,8},{10,9... | collective-permute-start | bytes 1572872 | tf_op jit(solution)/shard_map/ppermute | solution.py:313
  66.3 1.0 copy-start.11
  67.2 0.9 copy-start.13
  68.2 0.9 copy-start.15
  72.5 1.0 copy-start.4
  73.5 1.0 copy-start.6
  91.1 27.5 %all-to-all-start = ((f32[32,1,1]{2,1,0:T(1,128)}), f32[32,1,1]{2,1,0:T(1,128)S(1)}, u32[]{:S(2)}, u32[]{:S(2)}) async-start(f32[32,1,1]{2,1,0:T(1,128)} %copy.14), calls=%async_computation | async-start | bytes 32768 | tf_op jit(solution)/shard_map/all_to_all | solution.py:326

commit v2 on v1

v2 whole, which is shorter than its diff:
```python
import jax
import jax.numpy as jnp
from jax import lax
from jax.experimental import pallas as pl
from jax.experimental.pallas import tpu as pltpu
from jax.sharding import PartitionSpec as P

F32 = jnp.float32
HIGH = lax.Precision.HIGHEST
ANY = pl.BlockSpec(memory_space=pl.ANY)
SMEM = pl.BlockSpec(memory_space=pltpu.SMEM)
BLOCK = 128
PAD = 48
RUN = 4
BUNCH = 4
MIB = 1024 * 1024


COST = pl.CostEstimate(flops=1, bytes_accessed=1, transcendentals=0)


def params(mib):
    return pltpu.CompilerParams(vmem_limit_bytes=mib * MIB)


def coefs(c):
    sq = 0.5 * c * c
    half = 0.5 * c
    return 1.0 - 2.0 * sq, sq - half, sq + half


def lon_step(x, w):
    n = x.shape[-1]
    mid, up, down = w
    return mid * x + up * pltpu.roll(x, n - 1, 1) + down * pltpu.roll(x, 1, 1)


def prep_kernel(head_in, tail_in, c_head, c_tail, thick, head, tail, sent, sems):
    step = pl.program_id(0)

    def copies():
        out = []
        for s in range(4):
            for h in range(2):
                at = (2 * s + h) * BLOCK
                out.append(pltpu.make_async_copy(thick.at[:, :, pl.ds(at, BLOCK)], sent.at[s, :, h], sems.at[s, h]))
        return out

    @pl.when(step == 0)
    def _():
        for c in copies():
            c.start()

    for src, cour, dst in ((head_in, c_head, head), (tail_in, c_tail, tail)):
        w = coefs(cour[0])
        for f in range(src.shape[0]):
            dst[f] = lon_step(src[f, 0], w)

    @pl.when(step == pl.num_programs(0) - 1)
    def _():
        for c in copies():
            c.wait()


def prep(fields, courant_lon, thickness):
    nf, rows, levs, lon = fields.shape
    edge = lambda r: pl.BlockSpec((nf, 1, 8, lon), lambda i: (0, r, i, 0))
    cedge = lambda r: pl.BlockSpec((1, 8, lon), lambda i: (r, i, 0))
    out_edge = pl.BlockSpec((nf, 8, lon), lambda i: (0, i, 0))
    piece = jax.ShapeDtypeStruct((4, rows, 2, levs, BLOCK), F32)
    side = jax.ShapeDtypeStruct((nf, levs, lon), F32)
    return pl.pallas_call(
        prep_kernel,
        grid=(levs // 8,),
        in_specs=[edge(0), edge(rows - 1), cedge(0), cedge(rows - 1), ANY],
        out_specs=[out_edge, out_edge, ANY],
        out_shape=[side, side, piece],
        scratch_shapes=[pltpu.SemaphoreType.DMA((4, 2))],
        compiler_params=params(58),
        cost_estimate=COST,
        name="prep",
    )(fields, fields, courant_lon, courant_lon, thickness)


def advect_kernel(q, c_lon, c_lat, prev, nxt, after, *rest):
    *sent, keep, sems = rest
    step = pl.program_id(0)
    last = pl.num_programs(0) - 1
    nf, rows = q.shape[0], q.shape[1]

    def copies(k):
        out = []
        for s in range(4):
            for h in range(2):
                at, dst = (2 * s + h) * BLOCK, sent[0].at[s] if len(sent) == 1 else sent[s]
                if len(sent) > 1:
                    at = pl.multiple_of(lax.rem(lax.axis_index("lev") + s, 4) * (2 * BLOCK) + h * BLOCK, BLOCK)
                lev = pl.multiple_of(k * 8, 8)
                out.append(
                    pltpu.make_async_copy(
                        keep.at[k, :, :, :, pl.ds(at, BLOCK)], dst.at[:, :, h, pl.ds(lev, 8), :], sems.at[k, s, h]
                    )
                )
        return out

    before = [prev[f] for f in range(nf)]
    w = coefs(c_lon[0])
    here = [lon_step(q[f, 0], w) for f in range(nf)]
    for r in range(rows):
        if r + 1 < rows:
            w = coefs(c_lon[r + 1])
            ahead = [lon_step(q[f, r + 1], w) for f in range(nf)]
        else:
            ahead = [nxt[f] for f in range(nf)]
        mid, up, down = coefs(c_lat[r])
        for f in range(nf):
            keep[step, f, r] = mid * here[f] + up * ahead[f] + down * before[f]
        before, here = here, ahead
    for c in copies(step):
        c.start()

    @pl.when(step == last)
    def _():
        for k in range(4):
            for c in copies(k):
                c.wait()


def advect(group, fields, c_lon, c_lat, prev, nxt, stacked, after):
    nf, rows, levs, lon = fields.shape
    half = nf // 2
    steps = levs // 8
    cspec = pl.BlockSpec((rows, 8, lon), lambda i: (0, i, 0))
    hspec = pl.BlockSpec((half, 8, lon), lambda i: (group, i, 0))
    shape = (half, rows, 2, levs, BLOCK)
    piece = [jax.ShapeDtypeStruct((4, *shape), F32)] if stacked else [jax.ShapeDtypeStruct(shape, F32)] * 4
    return pl.pallas_call(
        advect_kernel,
        grid=(steps,),
        in_specs=[pl.BlockSpec((half, rows, 8, lon), lambda i: (group, 0, i, 0)), cspec, cspec, hspec, hspec, ANY],
        out_specs=[ANY] * len(piece),
        out_shape=piece,
        scratch_shapes=[pltpu.VMEM((steps, half, rows, 8, lon), F32), pltpu.SemaphoreType.DMA((steps, 4, 2))],
        compiler_params=params(58),
        cost_estimate=COST,
        name="advect",
    )(fields, c_lon, c_lat, prev, nxt, after)


def edges_kernel(thick, e_ref, lo_ref, n_ref, col):
    quarter = thick.shape[3]
    levels = 4 * quarter
    span = levels // 8
    row = lax.broadcasted_iota(jnp.int32, (levels, levels), 0)
    level = (row & 7) * span + lax.shift_right_logical(row, 3)
    j = lax.broadcasted_iota(jnp.int32, (levels, levels), 1)
    lower = (level >= j).astype(F32)
    at_level = level[:, :BLOCK].astype(F32) + 1.0
    low = jnp.zeros((1, 1), F32)
    high = jnp.zeros((1, 1), F32)
    for h in range(2):
        for s in range(4):
            col[h, s * quarter : (s + 1) * quarter, :] = thick[s, 0, h]
        upper = jnp.dot(lower, col[h], precision=HIGH, preferred_element_type=F32)
        e = upper * (levels / upper[levels - 1 :, :])
        e_ref[0, h] = e
        shift = e - at_level
        low = jnp.minimum(low, jnp.min(jnp.min(shift, axis=0, keepdims=True), axis=1, keepdims=True))
        high = jnp.maximum(high, jnp.max(jnp.max(shift, axis=0, keepdims=True), axis=1, keepdims=True))
    lo = jnp.maximum(-jnp.ceil(high), 1.0 - PAD).astype(jnp.int32)
    hi = jnp.minimum(-jnp.floor(low), PAD - 2.0 * RUN).astype(jnp.int32)
    n = lax.shift_right_logical(hi - lo + RUN, RUN.bit_length() - 1)
    lo_ref[0] = jnp.broadcast_to(lo, (1, BLOCK))
    n_ref[0] = jnp.broadcast_to(n, (1, BLOCK))


def edges(thick):
    _, rows, _, quarter, _ = thick.shape
    levels = 4 * quarter
    spec = pl.BlockSpec((4, 1, 2, quarter, BLOCK), lambda r: (0, r, 0, 0, 0))
    bound = jax.ShapeDtypeStruct((rows, 1, BLOCK), jnp.int32)
    bspec = pl.BlockSpec((1, 1, BLOCK), lambda r: (r, 0, 0))
    return pl.pallas_call(
        edges_kernel,
        grid=(rows,),
        in_specs=[spec],
        out_specs=[pl.BlockSpec((1, 2, levels, BLOCK), lambda r: (r, 0, 0, 0)), bspec, bspec],
        out_shape=[jax.ShapeDtypeStruct((rows, 2, levels, BLOCK), F32), bound, bound],
        scratch_shapes=[pltpu.VMEM((2, levels, BLOCK), F32)],
        compiler_params=params(24),
        cost_estimate=COST,
        name="edges",
    )(thick)


def remap_row(r, lo_ref, n_ref, e_ref, pieces, edge, cols, back, out):
    nf = cols.shape[0]
    quarter = pieces[0].shape[-2]
    levels = 4 * quarter
    span = levels // 8
    sub = lax.broadcasted_iota(jnp.int32, (8, BLOCK), 0)
    d0 = lo_ref[r, 0, 0]
    n = n_ref[r, 0, 0]

    def tile(ref, i):
        return ref[pl.ds(pl.multiple_of(i * 8, 8), 8), :]

    for h in range(2):
        edge[h, pl.ds(PAD * 8, levels), :] = e_ref[0, h]
        for k in range(4):
            src, s = (pieces[0].at[k], k) if len(pieces) == 1 else (pieces[k], lax.rem(lax.axis_index("lev") + 4 - k, 4))
            for m in range(quarter // 8):
                at = (PAD + 8 * (m % 2)) * 8 + m // 2 + s * (quarter // span)
                for f in range(nf):
                    cols[f, h, pl.ds(at, 8, stride=8), :] = src[f, 0, h, 8 * m : 8 * m + 8, :]

    def extend(i0, frm, turn, stop, fill):
        edge_row = sub == stop
        for t in range(RUN):
            i = i0 + t
            at = pl.ds(pl.multiple_of(i * 8, 8), 8)
            for h in range(2):
                edge[h, at, :] = jnp.where(edge_row, fill, pltpu.roll(tile(edge.at[h], i + frm), turn, 0))
                for f in range(nf):
                    cols[f, h, at, :] = jnp.where(edge_row, 0.0, pltpu.roll(tile(cols.at[f, h], i + frm), turn, 0))

    def above(k, c):
        extend(PAD + span + k * RUN, -span, 7, 7, 4.0 * levels)
        return c

    def below(k, c):
        extend(PAD - (k + 1) * RUN, span, 1, 0, 0.0)
        return c

    most = lax.shift_right_logical(jnp.maximum(d0 + n * RUN - 1, 0) + RUN - 1, RUN.bit_length() - 1)
    least = lax.shift_right_logical(jnp.maximum(-d0, 0) + RUN - 1, RUN.bit_length() - 1)
    lax.fori_loop(0, most, above, 0)
    lax.fori_loop(0, least, below, 0)

    spots = [(h, t) for h in range(2) for t in range(BUNCH)]
    many = len(spots)
    zero = jnp.zeros((8, BLOCK), F32)
    for g0 in range(0, span, BUNCH):
        lows = [(sub * span + (g0 + t)).astype(F32) for t in range(BUNCH)]
        highs = [x + 1.0 for x in lows]

        def some(k, carry):
            olds = list(carry[:many])
            accs = [list(carry[many * (f + 1) : many * (f + 2)]) for f in range(nf)]
            b = PAD + g0 + d0 + k * RUN
            for h in range(2):
                es = [tile(edge.at[h], b + x) for x in range(BUNCH + RUN - 1)]
                qs = [[tile(cols.at[f, h], b + x) for x in range(BUNCH + RUN - 1)] for f in range(nf)]
                for v in range(RUN):
                    for t in range(BUNCH):
                        i = h * BUNCH + t
                        p = jnp.minimum(jnp.maximum(es[v + t], lows[t]), highs[t])
                        w = p - olds[i]
                        olds[i] = p
                        for f in range(nf):
                            accs[f][i] = accs[f][i] + w * qs[f][v + t]
            return (*olds, *sum(accs, []))

        res = lax.fori_loop(0, n, some, (*lows, *lows) + (zero,) * (nf * many))
        for f in range(nf):
            for i, (h, t) in enumerate(spots):
                back[f, h, pl.ds(g0 + t, 8, stride=span), :] = res[many * (f + 1) + i]
    for f in range(nf):
        for h in range(2):
            out[f, 0, :, h * BLOCK : (h + 1) * BLOCK] = back[f, h]


def heat_kernel(lo_ref, n_ref, own_ref, day_ref, e_ref, exch, solar, *rest):
    *pieces, out, heating, shares, edge, cols, back = rest
    r = pl.program_id(0)
    remap_row(r, lo_ref, n_ref, e_ref, pieces, edge, cols, back, out)
    temp = out[0, 0]
    hum = out[1, 0]
    levels, width = temp.shape
    square = hum * hum
    clear = 1.0 / (1.0 + square)
    absorb = square * clear
    heat = jnp.dot(exch[0], absorb * temp, precision=HIGH, preferred_element_type=F32)
    heat = heat + jnp.dot(exch[1], clear * temp, precision=HIGH, preferred_element_type=F32)
    lane = lax.broadcasted_iota(jnp.int32, (1, width), 1)
    d0 = jnp.full((1, width), day_ref[2 * r], jnp.int32)
    d1 = jnp.full((1, width), day_ref[2 * r + 1], jnp.int32)
    day = jnp.where(lane < BLOCK, d0, d1).astype(F32)
    heat = heat + (day * solar[...]) * clear
    heating[0] = heat
    total = jnp.sum(heat, axis=0, keepdims=True)
    line = lax.broadcasted_iota(jnp.int32, (1, BLOCK), 1)

    @pl.when(r == 0)
    def _():
        shares[...] = jnp.zeros_like(shares)

    acc = shares[...]
    for b in range(2):
        mean = jnp.sum(total[:, b * BLOCK : (b + 1) * BLOCK], axis=1, keepdims=True) * (1.0 / (levels * BLOCK))
        acc = acc + jnp.where(line == own_ref[2 * r + b], mean, 0.0)
    shares[...] = acc


def remap_kernel(lo_ref, n_ref, e_ref, base, *rest):
    *pieces, out, edge, cols, back = rest
    remap_row(pl.program_id(0), lo_ref, n_ref, e_ref, pieces, edge, cols, back, out)


def remap(group, lo, n, e, pieces, base=None, heat_args=None):
    half, rows, _, quarter, _ = pieces[0].shape[-5:]
    levels = 4 * quarter
    width = 2 * BLOCK
    tall = levels + 2 * PAD * 8
    espec = pl.BlockSpec((1, 2, levels, BLOCK), lambda r: (r, 0, 0, 0))
    shape = (half, 1, 2, quarter, BLOCK)
    pspec = pl.BlockSpec(shape, lambda r: (0, r, 0, 0, 0))
    if len(pieces) == 1:
        pspec = pl.BlockSpec((4, *shape), lambda r: (0, 0, r, 0, 0, 0))
    pspecs = [pspec] * len(pieces)
    ospec = pl.BlockSpec((half, 1, levels, width), lambda r: (group, r, 0, 0))
    full = jax.ShapeDtypeStruct((2 * half, rows, levels, width), F32)
    common = dict(
        grid=(rows,),
        scratch_shapes=[
            pltpu.VMEM((2, tall, BLOCK), F32),
            pltpu.VMEM((half, 2, tall, BLOCK), F32),
            pltpu.VMEM((half, 2, levels, BLOCK), F32),
        ],
        compiler_params=params(24),
        cost_estimate=COST,
    )
    if heat_args is None:
        return pl.pallas_call(
            remap_kernel,
            in_specs=[SMEM, SMEM, espec, ANY] + pspecs,
            out_specs=ospec,
            out_shape=full,
            input_output_aliases={3: 0},
                name="remap",
            **common,
        )(lo, n, e, base, *pieces)
    owners, day, exchange, solar = heat_args
    hspec = pl.BlockSpec((1, levels, width), lambda r: (r, 0, 0))
    return pl.pallas_call(
        heat_kernel,
        in_specs=[SMEM, SMEM, SMEM, SMEM, espec]
        + [pl.BlockSpec((2, levels, levels), lambda r: (0, 0, 0)), pl.BlockSpec((levels, 1), lambda r: (0, 0))]
        + pspecs,
        out_specs=[ospec, hspec, pl.BlockSpec((1, BLOCK), lambda r: (0, 0))],
        out_shape=[full, jax.ShapeDtypeStruct((rows, levels, width), F32), jax.ShapeDtypeStruct((1, BLOCK), F32)],
        name="heat",
        **common,
    )(lo, n, owners, day, e, exchange, solar, *pieces)


def per_device(fields, thickness, courant_lon, courant_lat, exchange, solar_profile, owners, daylight):
    count = lax.axis_size("lat")
    ends = count - 1
    turn = lambda s: [(i, (i + s) % 4) for i in range(4)]
    around = lambda ps: [ps[0]] + [lax.ppermute(p, "lev", turn(s + 1)) for s, p in enumerate(ps[1:])]
    regroup = lambda x: lax.all_to_all(x, "lev", split_axis=0, concat_axis=0, tiled=True)

    head, tail, thick = prep(fields, courant_lon, thickness)
    prev = lax.ppermute(tail, "lat", [(i, i + 1) for i in range(ends)])
    nxt = lax.ppermute(head, "lat", [(i + 1, i) for i in range(ends)])
    e, lo, n = edges(regroup(thick))
    first = advect(0, fields, courant_lon, courant_lat, prev, nxt, True, head)
    second = around(advect(1, fields, courant_lon, courant_lat, prev, nxt, False, first[0]))
    first = [regroup(first[0])]
    heat_args = (owners[:, 0], daylight, exchange, solar_profile[:, None])
    remapped, heating, shares = remap(0, lo, n, e, first, heat_args=heat_args)
    remapped = remap(1, lo, n, e, second, base=remapped)
    shares = shares[0, :count].reshape(count, 1, 1)
    owner_heat = jnp.sum(lax.all_to_all(shares, "lat", split_axis=0, concat_axis=0, tiled=True)).reshape(1, 1)
    return (remapped, heating, owner_heat)


def solution(mesh):
    placed = (
        P(None, "lat", "lev", None),
        P("lat", "lev", None),
        P("lat", "lev", None),
        P("lat", "lev", None),
        P(),
        P(),
        P(("lat", "lev"), None),
        P(("lat", "lev")),
    )
    return jax.shard_map(
        per_device,
        mesh=mesh,
        in_specs=placed,
        out_specs=(P(None, "lat", None, "lev"), P("lat", None, "lev"), P("lat", "lev")),
        check_vma=False,
    )
```

time: 120 us -> 137 us (1.14)
  the two profiles are of different devices: /device:TPU:1 before, /device:TPU:13 now
where the time goes in v2:
time: 137 us
  Pallas kernels  72.8 us (53%)
  starting transfers between devices  38.4 us (28%)
  waiting for transfers between devices  19.3 us (14%)
  local copies, waits for them, and re-layouts  4.84 us (4%)
    pallas_call x1, Pallas kernels, prep(): pl.pallas_call(prep_kernel, grid=(levs // 8,), in_specs=[edge(0), edge(ro...  34.6 us
    all_to_all x1, starting transfers between devices, per_device(): lax.all_to_all(shares, 'lat', split_axis=0, concat_axis=0, tiled=True)  19.3 us
    pallas_call x1, Pallas kernels, remap(): pl.pallas_call(heat_kernel, in_specs=[SMEM, SMEM, SMEM, SMEM, espec] + [p...  13.8 us
    pallas_call x2, Pallas kernels, advect(): pl.pallas_call(advect_kernel, grid=(steps,), in_specs=[pl.BlockSpec((half...  10.7 us
    all_to_all x2, waiting for transfers between devices, per_device(): lax.all_to_all(x, 'lev', split_axis=0, concat_axis=0, tiled=True)  10.5 us
    pallas_call x1, Pallas kernels, remap(): pl.pallas_call(remap_kernel, in_specs=[SMEM, SMEM, espec, ANY] + pspecs,...  10.4 us
    all_to_all x2, starting transfers between devices, per_device(): lax.all_to_all(x, 'lev', split_axis=0, concat_axis=0, tiled=True)  8.59 us
    ppermute x1, starting transfers between devices, per_device(): prev = lax.ppermute(tail, 'lat', [(i, i + 1) for i in range(ends)])  4.65 us
  transfers between devices with their start and end apart: 8, of which 3 were waited for; matrix products, arithmetic and copies ran while one was open for 1% of the time, Pallas kernels for 28%

profile of v2, /device:TPU:13, one launch (start us, length us, event | category | flops | bytes accessed | tf_op | source)
XLA Modules:
  0.0 136.7 jit_solution(279792562867130149)
XLA Ops:
  0.6 34.6 %prep.1 = (f32[4,32,1024]{2,1,0:T(8,128)}, f32[4,32,1024]{2,1,0:T(8,128)}, f32[4,8,2,32,128]{4,3,2,1,0:T(8,128)}) custom-call(f32[4,8,32,1024]{3,2,1,0:T(8,128)} %q.3, f32[4,8,32,1024]{3,2,1,0:T(8,128)} %q.3, f32[8,32,1024]{2,1,0:T(8,128)} %c_lon.3, f32[8,32,1024]{2,1,0:T(8,128)} %c_lon.3, f32[8,32,1024]{2,1,0:T(8,128)} %thick.1), custom_call_target="tpu_custom_call" | custom-call | flops 1 | bytes 1 | tf_op jit(solution)/shard_map/prep/pallas_call | solution.py:72
  35.3 4.4 %all-to-all-start = ((f32[4,8,2,32,128]{4,3,2,1,0:T(8,128)}), f32[4,8,2,32,128]{4,3,2,1,0:T(8,128)S(1)}, u32[]{:S(2)}, u32[]{:S(2)}) async-start(f32[4,8,2,32,128]{4,3,2,1,0:T(8,128)} %get-tuple-element.16), calls=%async_computation | async-start | bytes 2097152 | tf_op jit(solution)/shard_map/all_to_all | solution.py:362
  39.6 4.7 %collective-permute-start = (f32[4,32,1024]{2,1,0:T(8,128)}, f32[4,32,1024]{2,1,0:T(8,128)S(1)}, u32[]{:S(2)}, u32[]{:S(2)}) collective-permute-start(f32[4,32,1024]{2,1,0:T(8,128)} %get-tuple-element.20), channel_id=1, source_target_pairs={{0,4},{4,8},{8,12},{12,16},{16,20},{20,24},{24,28},{28,32},{32,36}... | collective-permute-start | bytes 1572872 | tf_op jit(solution)/shard_map/ppermute | solution.py:365
  44.3 1.9 %collective-permute-start.1 = (f32[4,32,1024]{2,1,0:T(8,128)}, f32[4,32,1024]{2,1,0:T(8,128)S(1)}, u32[]{:S(2)}, u32[]{:S(2)}) collective-permute-start(f32[4,32,1024]{2,1,0:T(8,128)} %get-tuple-element.21.after), channel_id=1, source_target_pairs={{4,0},{8,4},{12,8},{16,12},{20,16},{24,20},{28,24},{32,28},{36,32}... | collective-permute-start | bytes 1572872 | tf_op jit(solution)/shard_map/ppermute | solution.py:366
  46.2 4.5 %collective-permute-done.prev = f32[4,32,1024]{2,1,0:T(8,128)S(1)} collective-permute-done((f32[4,32,1024]{2,1,0:T(8,128)}, f32[4,32,1024]{2,1,0:T(8,128)S(1)}, u32[]{:S(2)}, u32[]{:S(2)}) %collective-permute-start) | collective-permute-done | bytes 524320 | tf_op jit(solution)/shard_map/ppermute | solution.py:365
  50.7 0.0 copy-start.6
  50.7 4.3 %collective-permute-done.1.nxt = f32[4,32,1024]{2,1,0:T(8,128)S(1)} collective-permute-done((f32[4,32,1024]{2,1,0:T(8,128)}, f32[4,32,1024]{2,1,0:T(8,128)S(1)}, u32[]{:S(2)}, u32[]{:S(2)}) %collective-permute-start.1) | collective-permute-done | bytes 524320 | tf_op jit(solution)/shard_map/ppermute | solution.py:366
  55.0 0.0 copy-done.6
  55.0 0.0 copy-start.7
  55.0 0.8 copy-done.7
  55.8 5.2 %advect.2.after = f32[4,2,8,2,32,128]{5,4,3,2,1,0:T(8,128)} custom-call(f32[4,8,32,1024]{3,2,1,0:T(8,128)} %q.3, f32[8,32,1024]{2,1,0:T(8,128)} %c_lon.3, f32[8,32,1024]{2,1,0:T(8,128)} %c_lat.3, f32[4,32,1024]{2,1,0:T(8,128)} %copy-done.6, f32[4,32,1024]{2,1,0:T(8,128)} %copy-done.7, f32[4,32,1024]{2,1,0:T(8,128)} %get-tuple-element.21.after), custom_call_target="tpu_custom_call" | custom-call | flops 1 | bytes 1 | tf_op jit(solution)/shard_map/advect/pallas_call | solution.py:137
  61.0 0.0 all-to-all-done.thick
  61.1 0.0 copy-start
  61.1 1.0 copy-done
  62.0 4.2 %all-to-all-start.1 = ((f32[4,2,8,2,32,128]{5,4,3,2,1,0:T(8,128)}), f32[4,2,8,2,32,128]{5,4,3,2,1,0:T(8,128)S(1)}, u32[]{:S(2)}, u32[]{:S(2)}) async-start(f32[4,2,8,2,32,128]{5,4,3,2,1,0:T(8,128)} %advect.2.after), calls=%async_computation.1 | async-start | bytes 4194304 | tf_op jit(solution)/shard_map/all_to_all | solution.py:362
  66.3 0.0 copy-start.8
  66.3 0.0 copy-start.3
  66.3 0.0 copy-start.4
  66.3 0.0 copy-start.5
  66.3 5.4 %advect.3 = (f32[2,8,2,32,128]{4,3,2,1,0:T(8,128)}, f32[2,8,2,32,128]{4,3,2,1,0:T(8,128)}, f32[2,8,2,32,128]{4,3,2,1,0:T(8,128)}, f32[2,8,2,32,128]{4,3,2,1,0:T(8,128)}) custom-call(f32[4,8,32,1024]{3,2,1,0:T(8,128)} %q.3, f32[8,32,1024]{2,1,0:T(8,128)} %c_lon.3, f32[8,32,1024]{2,1,0:T(8,128)} %c_lat.3, f32[4,32,1024]{2,1,0:T(8,128)} %copy-done.6, ...), custom_call_target="tpu_custom_call" | custom-call | flops 1 | bytes 1 | tf_op jit(solution)/shard_map/advect/pallas_call | solution.py:137
  71.7 1.3 collective-permute-start.2
  73.0 0.7 collective-permute-start.3
  73.7 2.0 %collective-permute-start.4 = (f32[2,8,2,32,128]{4,3,2,1,0:T(8,128)}, f32[2,8,2,32,128]{4,3,2,1,0:T(8,128)}, u32[]{:S(2)}, u32[]{:S(2)}) collective-permute-start(f32[2,8,2,32,128]{4,3,2,1,0:T(8,128)} %get-tuple-element.26), channel_id=1, source_target_pairs={{0,3},{1,0},{2,1},{3,2},{4,7},{5,4},{6,5},{7,6},{8,11},{9,8},{10,9... | collective-permute-start | bytes 1572872 | tf_op jit(solution)/shard_map/ppermute | solution.py:361
  75.6 0.0 copy-done.8
  75.6 0.1 copy.13.solar
  75.7 0.0 copy-start.1
  75.7 1.2 copy-done.1
  77.0 3.2 %edges.1 = (f32[8,2,128,128]{3,2,1,0:T(8,128)S(1)}, s32[8,1,128]{2,1,0:T(1,128)S(1)}, s32[8,1,128]{2,1,0:T(1,128)S(1)}) custom-call(f32[4,8,2,32,128]{4,3,2,1,0:T(8,128)S(1)} %copy-done.1), custom_call_target="tpu_custom_call" | custom-call | flops 1 | bytes 1 | tf_op jit(solution)/shard_map/edges/pallas_call | solution.py:183
  80.2 10.5 %all-to-all-done.1.rest_0_ = f32[4,2,8,2,32,128]{5,4,3,2,1,0:T(8,128)S(1)} async-done(((f32[4,2,8,2,32,128]{5,4,3,2,1,0:T(8,128)}), f32[4,2,8,2,32,128]{5,4,3,2,1,0:T(8,128)S(1)}, u32[]{:S(2)}, u32[]{:S(2)}) %all-to-all-start.1) | async-done | bytes 2097184 | tf_op jit(solution)/shard_map/all_to_all | solution.py:362
  90.7 0.0 copy-done.3
  90.7 0.0 copy-done.4
  90.7 0.0 copy-done.5
  90.7 13.8 %heat.1 = (f32[4,8,128,256]{3,2,1,0:T(8,128)}, f32[8,128,256]{2,1,0:T(8,128)}, f32[1,128]{1,0:T(1,128)S(1)}) custom-call(s32[8,1,128]{2,1,0:T(1,128)S(1)} %get-tuple-element.17.lo_ref, s32[8,1,128]{2,1,0:T(1,128)S(1)} %get-tuple-element.18.n_ref, s32[16]{0:T(128)S(1)} %bitcast.5, s32[16]{0:T(128)S(1)} %copy-done.5, ...), custom_call_target="tpu_custom_call" | custom-call | flops 1 | bytes 1 | tf_op jit(solution)/shard_map/heat/pallas_call | solution.py:345
  104.6 0.7 copy.14
  105.2 19.3 %all-to-all-start.2 = ((f32[32,1,1]{2,1,0:T(1,128)}), f32[32,1,1]{2,1,0:T(1,128)S(1)}, u32[]{:S(2)}, u32[]{:S(2)}) async-start(f32[32,1,1]{2,1,0:T(1,128)} %copy.14), calls=%async_computation.2 | async-start | bytes 32768 | tf_op jit(solution)/shard_map/all_to_all | solution.py:375
  124.6 0.0 collective-permute-done.2.rest_1_
  124.6 0.0 collective-permute-done.3.rest_2_
  124.6 0.0 collective-permute-done.4.rest_3_
  124.6 0.0 copy-start.2
  124.6 1.0 copy-done.2
  125.7 10.4 %remap.1 = f32[4,8,128,256]{3,2,1,0:T(8,128)} custom-call(s32[8,1,128]{2,1,0:T(1,128)S(1)} %get-tuple-element.17.lo_ref, s32[8,1,128]{2,1,0:T(1,128)S(1)} %get-tuple-element.18.n_ref, f32[8,2,128,128]{3,2,1,0:T(8,128)S(1)} %get-tuple-element.19.e_ref, f32[4,8,128,256]{3,2,1,0:T(8,128)} %get-tuple-element.22.base, ...), custom_call_target="tpu_custom_call", output_to_operand_aliasing={{}: (3, {})} | custom-call | flops 1 | bytes 1 | tf_op jit(solution)/shard_map/remap/pallas_call | solution.py:334
  136.1 0.0 all-to-all-done.2
  136.1 0.6 reduce_sum.9
  (1 shorter events, 0.0 us)
Async XLA Ops:
  35.3 25.8 %all-to-all-start = ((f32[4,8,2,32,128]{4,3,2,1,0:T(8,128)}), f32[4,8,2,32,128]{4,3,2,1,0:T(8,128)S(1)}, u32[]{:S(2)}, u32[]{:S(2)}) async-start(f32[4,8,2,32,128]{4,3,2,1,0:T(8,128)} %get-tuple-element.16), calls=%async_computation | async-start | bytes 2097152 | tf_op jit(solution)/shard_map/all_to_all | solution.py:362
  39.6 11.1 %collective-permute-start = (f32[4,32,1024]{2,1,0:T(8,128)}, f32[4,32,1024]{2,1,0:T(8,128)S(1)}, u32[]{:S(2)}, u32[]{:S(2)}) collective-permute-start(f32[4,32,1024]{2,1,0:T(8,128)} %get-tuple-element.20), channel_id=1, source_target_pairs={{0,4},{4,8},{8,12},{12,16},{16,20},{20,24},{24,28},{28,32},{32,36}... | collective-permute-start | bytes 1572872 | tf_op jit(solution)/shard_map/ppermute | solution.py:365
  44.3 10.7 %collective-permute-start.1 = (f32[4,32,1024]{2,1,0:T(8,128)}, f32[4,32,1024]{2,1,0:T(8,128)S(1)}, u32[]{:S(2)}, u32[]{:S(2)}) collective-permute-start(f32[4,32,1024]{2,1,0:T(8,128)} %get-tuple-element.21.after), channel_id=1, source_target_pairs={{4,0},{8,4},{12,8},{16,12},{20,16},{24,20},{28,24},{32,28},{36,32}... | collective-permute-start | bytes 1572872 | tf_op jit(solution)/shard_map/ppermute | solution.py:366
  50.7 4.3 %copy-start.6 = (f32[4,32,1024]{2,1,0:T(8,128)}, f32[4,32,1024]{2,1,0:T(8,128)S(1)}, u32[]{:S(2)}) copy-start(f32[4,32,1024]{2,1,0:T(8,128)S(1)} %collective-permute-done.prev) | copy-start | bytes 1572868
  55.0 0.8 copy-start.7
  61.1 1.0 copy-start
  62.0 28.7 %all-to-all-start.1 = ((f32[4,2,8,2,32,128]{5,4,3,2,1,0:T(8,128)}), f32[4,2,8,2,32,128]{5,4,3,2,1,0:T(8,128)S(1)}, u32[]{:S(2)}, u32[]{:S(2)}) async-start(f32[4,2,8,2,32,128]{5,4,3,2,1,0:T(8,128)} %advect.2.after), calls=%async_computation.1 | async-start | bytes 4194304 | tf_op jit(solution)/shard_map/all_to_all | solution.py:362
  66.3 9.4 %copy-start.8 = (f32[128]{0:T(128)S(1)}, f32[128]{0:T(128)}, u32[]{:S(2)}) copy-start(f32[128]{0:T(128)} %param.13) | copy-start | bytes 1540
  66.3 24.4 %copy-start.3 = (f32[2,128,128]{2,1,0:T(8,128)S(1)}, f32[2,128,128]{2,1,0:T(8,128)}, u32[]{:S(2)}) copy-start(f32[2,128,128]{2,1,0:T(8,128)} %exch.1) | copy-start | bytes 393220
  66.3 24.4 %copy-start.4 = (s32[16,1]{0,1:T(1,128)S(1)}, s32[16,1]{0,1:T(1,128)}, u32[]{:S(2)}) copy-start(s32[16,1]{0,1:T(1,128)} %param.14) | copy-start | bytes 196
  66.3 24.4 %copy-start.5 = (s32[16]{0:T(128)S(1)}, s32[16]{0:T(128)}, u32[]{:S(2)}) copy-start(s32[16]{0:T(128)} %day_ref.1) | copy-start | bytes 196
  71.7 52.9 %collective-permute-start.2 = (f32[2,8,2,32,128]{4,3,2,1,0:T(8,128)}, f32[2,8,2,32,128]{4,3,2,1,0:T(8,128)}, u32[]{:S(2)}, u32[]{:S(2)}) collective-permute-start(f32[2,8,2,32,128]{4,3,2,1,0:T(8,128)} %get-tuple-element.24), channel_id=1, source_target_pairs={{0,1},{1,2},{2,3},{3,0},{4,5},{5,6},{6,7},{7,4},{8,9},{9,10},{10,1... | collective-permute-start | bytes 1572872 | tf_op jit(solution)/shard_map/ppermute | solution.py:361
  73.0 51.7 %collective-permute-start.3 = (f32[2,8,2,32,128]{4,3,2,1,0:T(8,128)}, f32[2,8,2,32,128]{4,3,2,1,0:T(8,128)}, u32[]{:S(2)}, u32[]{:S(2)}) collective-permute-start(f32[2,8,2,32,128]{4,3,2,1,0:T(8,128)} %get-tuple-element.25), channel_id=1, source_target_pairs={{0,2},{1,3},{2,0},{3,1},{4,6},{5,7},{6,4},{7,5},{8,10},{9,11},{10,... | collective-permute-start | bytes 1572872 | tf_op jit(solution)/shard_map/ppermute | solution.py:361
  73.7 51.0 %collective-permute-start.4 = (f32[2,8,2,32,128]{4,3,2,1,0:T(8,128)}, f32[2,8,2,32,128]{4,3,2,1,0:T(8,128)}, u32[]{:S(2)}, u32[]{:S(2)}) collective-permute-start(f32[2,8,2,32,128]{4,3,2,1,0:T(8,128)} %get-tuple-element.26), channel_id=1, source_target_pairs={{0,3},{1,0},{2,1},{3,2},{4,7},{5,4},{6,5},{7,6},{8,11},{9,8},{10,9... | collective-permute-start | bytes 1572872 | tf_op jit(solution)/shard_map/ppermute | solution.py:361
  75.7 1.2 copy-start.1
  105.2 30.9 %all-to-all-start.2 = ((f32[32,1,1]{2,1,0:T(1,128)}), f32[32,1,1]{2,1,0:T(1,128)S(1)}, u32[]{:S(2)}, u32[]{:S(2)}) async-start(f32[32,1,1]{2,1,0:T(1,128)} %copy.14), calls=%async_computation.2 | async-start | bytes 32768 | tf_op jit(solution)/shard_map/all_to_all | solution.py:375
  124.6 1.0 copy-start.2

commit v3 on v2

v3 whole, which is shorter than its diff:
```python
import functools

import jax
import jax.numpy as jnp
from jax import lax
from jax.experimental import pallas as pl
from jax.experimental.pallas import tpu as pltpu
from jax.sharding import PartitionSpec as P

F32 = jnp.float32
HIGH = lax.Precision.HIGHEST
ANY = pl.BlockSpec(memory_space=pl.ANY)
SMEM = pl.BlockSpec(memory_space=pltpu.SMEM)
BLOCK = 128
PAD = 48
RUN = 4
BUNCH = 4
MIB = 1024 * 1024


COST = pl.CostEstimate(flops=1, bytes_accessed=1, transcendentals=0)


def params(mib):
    return pltpu.CompilerParams(vmem_limit_bytes=mib * MIB)


def coefs(c):
    sq = 0.5 * c * c
    half = 0.5 * c
    return 1.0 - 2.0 * sq, sq - half, sq + half


def lon_step(x, w):
    n = x.shape[-1]
    mid, up, down = w
    return mid * x + up * pltpu.roll(x, n - 1, 1) + down * pltpu.roll(x, 1, 1)


def put(sent, k, r, value):
    for d in range(4):
        for h in range(2):
            at = (2 * d + h) * BLOCK
            sent[d, k, r, h] = value[:, at : at + BLOCK]


def inner_kernel(q, head_in, tail_in, c_lon, c_lat, thick, head, tail, *rest):
    *sent, keep, sems = rest
    step = pl.program_id(0)
    last = pl.num_programs(0) - 1
    nf, rows = q.shape[0], q.shape[1]

    def copies(k):
        return turned(sent, lambda cols: keep.at[k, :, :, :, cols], sems, k)

    before = here = None
    for r in range(rows):
        w = coefs(c_lon[r])
        ahead = [lon_step(q[f, r], w) for f in range(nf)]
        if r in (0, rows - 1):
            src, dst = (head_in, head) if r == 0 else (tail_in, tail)
            for f in range(nf):
                dst[f] = ahead[f]
                dst[nf + f] = lon_step(src[f, 0], w)
        else:
            keep[step, 0, r - 1] = thick[r]
        if r > 1:
            mid, up, down = coefs(c_lat[r - 1])
            for f in range(nf):
                keep[step, 1 + f, r - 2] = mid * here[f] + up * ahead[f] + down * before[f]
        before, here = here, ahead
    for c in copies(step):
        c.start()

    @pl.when(step == last)
    def _():
        for k in range(4):
            for c in copies(k):
                c.wait()


def inner(fields, c_lon, c_lat, thickness):
    nf, rows, levs, lon = fields.shape
    half = nf // 2
    cspec = pl.BlockSpec((rows, 8, lon), lambda i: (0, i, 0))
    edge = lambda r: pl.BlockSpec((half, 1, 8, lon), lambda i: (1, r, i, 0))
    ospec = pl.BlockSpec((nf, 8, lon), lambda i: (0, i, 0))
    side = pltpu.HBM((nf, levs, lon), F32)
    return pl.pallas_call(
        inner_kernel,
        grid=(levs // 8,),
        in_specs=[pl.BlockSpec((half, rows, 8, lon), lambda i: (0, 0, i, 0)), edge(0), edge(rows - 1)] + [cspec] * 3,
        out_specs=[ospec, ospec] + [ANY] * 4,
        out_shape=[side, side] + [pltpu.HBM((1 + half, rows - 2, 2, levs, BLOCK), F32)] * 4,
        scratch_shapes=[
            pltpu.VMEM((levs // 8, 1 + half, rows - 2, 8, lon), F32),
            pltpu.SemaphoreType.DMA((levs // 8, 4, 2)),
        ],
        compiler_params=params(12),
        cost_estimate=COST,
        name="inner",
    )(fields, fields, fields, c_lon, c_lat, thickness)


def outer_kernel(head, tail, q1, q2, c1, c2, l1, l2, th1, th2, prev, nxt, sent):
    nf = head.shape[0]
    for e, (here, q, c, lat, th) in enumerate(((head, q1, c1, l1, th1), (tail, q2, c2, l2, th2))):
        put(sent, 0, e, th[0])
        w = coefs(c[0])
        mid, up, down = coefs(lat[0])
        for f in range(nf):
            beside = lon_step(q[f, 0], w)
            before, ahead = (prev[f], beside) if e == 0 else (beside, nxt[f])
            put(sent, 1 + f, e, mid * here[f] + up * ahead + down * before)


def outer(head, tail, fields, c_lon, c_lat, thickness, prev, nxt):
    nf, rows, levs, lon = fields.shape
    half = nf // 2
    steps = levs // 8
    sspec = pl.BlockSpec((half, 8, lon), lambda i: (0, i, 0))
    qrow = lambda r: pl.BlockSpec((half, 1, 8, lon), lambda i: (0, r, i, 0))
    crow = lambda r: pl.BlockSpec((1, 8, lon), lambda i: (r, i, 0))
    end = rows - 1
    return pl.pallas_call(
        outer_kernel,
        grid=(steps,),
        in_specs=[sspec, sspec, qrow(1), qrow(end - 1), crow(1), crow(end - 1)]
        + [crow(0), crow(end)] * 2
        + [sspec, sspec],
        out_specs=pl.BlockSpec((4, 1 + half, 2, 2, 8, BLOCK), lambda i: (0, 0, 0, 0, i, 0)),
        out_shape=pltpu.HBM((4, 1 + half, 2, 2, levs, BLOCK), F32),
        compiler_params=params(12),
        cost_estimate=COST,
        name="outer",
    )(head, tail, fields, fields, c_lon, c_lon, c_lat, c_lat, thickness, thickness, prev, nxt)


def turned(sent, part, sems, k):
    out = []
    for s, dst in enumerate(sent):
        for h in range(2):
            at = pl.multiple_of(lax.rem(lax.axis_index("lev") + s, 4) * (2 * BLOCK) + h * BLOCK, BLOCK)
            lev = pl.multiple_of(k * 8, 8)
            out.append(
                pltpu.make_async_copy(part(pl.ds(at, BLOCK)), dst.at[:, :, h, pl.ds(lev, 8), :], sems.at[k, s, h])
            )
    return out


def advect_kernel(q, c_lon, c_lat, prev, nxt, *rest):
    *sent, keep, sems = rest
    step = pl.program_id(0)
    last = pl.num_programs(0) - 1
    nf, rows = q.shape[0], q.shape[1]

    def copies(k):
        return turned(sent, lambda cols: keep.at[k, :, :, :, cols], sems, k)

    before = [prev[f] for f in range(nf)]
    w = coefs(c_lon[0])
    here = [lon_step(q[f, 0], w) for f in range(nf)]
    for r in range(rows):
        if r + 1 < rows:
            w = coefs(c_lon[r + 1])
            ahead = [lon_step(q[f, r + 1], w) for f in range(nf)]
        else:
            ahead = [nxt[f] for f in range(nf)]
        mid, up, down = coefs(c_lat[r])
        for f in range(nf):
            keep[step, f, r] = mid * here[f] + up * ahead[f] + down * before[f]
        before, here = here, ahead
    for c in copies(step):
        c.start()

    @pl.when(step == last)
    def _():
        for k in range(4):
            for c in copies(k):
                c.wait()


def advect(group, fields, c_lon, c_lat, prev, nxt):
    nf, rows, levs, lon = fields.shape
    half = nf // 2
    steps = levs // 8
    cspec = pl.BlockSpec((rows, 8, lon), lambda i: (0, i, 0))
    hspec = pl.BlockSpec((half, 8, lon), lambda i: (group, i, 0))
    shape = (half, rows, 2, levs, BLOCK)
    piece = [pltpu.HBM(shape, F32)] * 4
    return pl.pallas_call(
        advect_kernel,
        grid=(steps,),
        in_specs=[pl.BlockSpec((half, rows, 8, lon), lambda i: (group, 0, i, 0)), cspec, cspec, hspec, hspec],
        out_specs=[ANY] * len(piece),
        out_shape=piece,
        scratch_shapes=[pltpu.VMEM((steps, half, rows, 8, lon), F32), pltpu.SemaphoreType.DMA((steps, 4, 2))],
        compiler_params=params(12),
        cost_estimate=COST,
        name="advect",
    )(fields, c_lon, c_lat, prev, nxt)


def source(pieces, k):
    if len(pieces) == 1:
        return pieces[0].at[k], k
    return pieces[k], lax.rem(lax.axis_index("lev") + 4 - k, 4)


def remap_row(d0, n, e_ref, pieces, first, edge, cols, back, out):
    nf = cols.shape[0]
    quarter = pieces[0].shape[-2]
    levels = 4 * quarter
    span = levels // 8
    sub = lax.broadcasted_iota(jnp.int32, (8, BLOCK), 0)

    def tile(ref, i):
        return ref[pl.ds(pl.multiple_of(i * 8, 8), 8), :]

    for h in range(2):
        edge[h, pl.ds(PAD * 8, levels), :] = e_ref[0, h]
        for k in range(4):
            src, s = source(pieces, k)
            for m in range(quarter // 8):
                at = (PAD + 8 * (m % 2)) * 8 + m // 2 + s * (quarter // span)
                for f in range(nf):
                    cols[f, h, pl.ds(at, 8, stride=8), :] = src[first + f, 0, h, 8 * m : 8 * m + 8, :]

    def extend(i0, frm, turn, stop, fill):
        edge_row = sub == stop
        for t in range(RUN):
            i = i0 + t
            at = pl.ds(pl.multiple_of(i * 8, 8), 8)
            for h in range(2):
                edge[h, at, :] = jnp.where(edge_row, fill, pltpu.roll(tile(edge.at[h], i + frm), turn, 0))
                for f in range(nf):
                    cols[f, h, at, :] = jnp.where(edge_row, 0.0, pltpu.roll(tile(cols.at[f, h], i + frm), turn, 0))

    def above(k, c):
        extend(PAD + span + k * RUN, -span, 7, 7, 4.0 * levels)
        return c

    def below(k, c):
        extend(PAD - (k + 1) * RUN, span, 1, 0, 0.0)
        return c

    most = lax.shift_right_logical(jnp.maximum(d0 + n * RUN - 1, 0) + RUN - 1, RUN.bit_length() - 1)
    least = lax.shift_right_logical(jnp.maximum(-d0, 0) + RUN - 1, RUN.bit_length() - 1)
    lax.fori_loop(0, most, above, 0)
    lax.fori_loop(0, least, below, 0)

    spots = [(h, t) for h in range(2) for t in range(BUNCH)]
    many = len(spots)
    zero = jnp.zeros((8, BLOCK), F32)
    for g0 in range(0, span, BUNCH):
        lows = [(sub * span + (g0 + t)).astype(F32) for t in range(BUNCH)]
        highs = [x + 1.0 for x in lows]

        def some(k, carry):
            olds = list(carry[:many])
            accs = [list(carry[many * (f + 1) : many * (f + 2)]) for f in range(nf)]
            b = PAD + g0 + d0 + k * RUN
            for h in range(2):
                es = [tile(edge.at[h], b + x) for x in range(BUNCH + RUN - 1)]
                qs = [[tile(cols.at[f, h], b + x) for x in range(BUNCH + RUN - 1)] for f in range(nf)]
                for v in range(RUN):
                    for t in range(BUNCH):
                        i = h * BUNCH + t
                        p = jnp.minimum(jnp.maximum(es[v + t], lows[t]), highs[t])
                        w = p - olds[i]
                        olds[i] = p
                        for f in range(nf):
                            accs[f][i] = accs[f][i] + w * qs[f][v + t]
            return (*olds, *sum(accs, []))

        res = lax.fori_loop(0, n, some, (*lows, *lows) + (zero,) * (nf * many))
        for f in range(nf):
            for i, (h, t) in enumerate(spots):
                back[f, h, pl.ds(g0 + t, 8, stride=span), :] = res[many * (f + 1) + i]
    for f in range(nf):
        for h in range(2):
            out[f, 0, :, h * BLOCK : (h + 1) * BLOCK] = back[f, h]


def edges_row(pieces, col, e_ref):
    quarter = pieces[0].shape[-2]
    levels = 4 * quarter
    row = lax.broadcasted_iota(jnp.int32, (levels, levels), 0)
    level = (row & 7) * (levels // 8) + lax.shift_right_logical(row, 3)
    j = lax.broadcasted_iota(jnp.int32, (levels, levels), 1)
    lower = (level >= j).astype(F32)
    at_level = level[:, :BLOCK].astype(F32) + 1.0
    low = jnp.zeros((1, 1), F32)
    high = jnp.zeros((1, 1), F32)
    for h in range(2):
        for k in range(4):
            src, s = source(pieces, k)
            at = s * quarter if isinstance(s, int) else pl.multiple_of(s * quarter, quarter)
            col[h, pl.ds(at, quarter), :] = src[0, 0, h]
        upper = jnp.dot(lower, col[h], precision=HIGH, preferred_element_type=F32)
        e = upper * (levels / upper[levels - 1 :, :])
        e_ref[0, h] = e
        shift = e - at_level
        low = jnp.minimum(low, jnp.min(jnp.min(shift, axis=0, keepdims=True), axis=1, keepdims=True))
        high = jnp.maximum(high, jnp.max(jnp.max(shift, axis=0, keepdims=True), axis=1, keepdims=True))
    lo = jnp.maximum(-jnp.ceil(high), 1.0 - PAD).astype(jnp.int32)
    hi = jnp.minimum(-jnp.floor(low), PAD - 2.0 * RUN).astype(jnp.int32)
    n = lax.shift_right_logical(hi - lo + RUN, RUN.bit_length() - 1)
    return lo[0, 0], n[0, 0]


def halves(x):
    top = x.astype(jnp.bfloat16)
    return top, (x - top.astype(F32)).astype(jnp.bfloat16)


def heat_kernel(row_of, skip, own_ref, day_ref, exch, solar, so_far, *rest):
    *pieces, out, heating, shares, e_ref, lo_ref, n_ref, edge, cols, back, col, mats = rest
    pieces = pieces[skip:]
    step = pl.program_id(0)
    r = row_of(step)

    @pl.when(step == 0)
    def _():
        shares[...] = so_far[...]
        both = jnp.concatenate([exch[0], exch[1]], axis=1)
        mats[0], mats[1] = halves(both)

    d0, n = edges_row(pieces, col, e_ref)
    lo_ref[step] = d0
    n_ref[step] = n
    remap_row(d0, n, e_ref, pieces, 1, edge, cols, back, out)
    temp = out[0, 0]
    hum = out[1, 0]
    levels, width = temp.shape
    square = hum * hum
    clear = 1.0 / (1.0 + square)
    absorb = square * clear
    top, rest_of = halves(jnp.concatenate([absorb * temp, clear * temp], axis=0))
    heat = jnp.dot(mats[0], rest_of, preferred_element_type=F32) + jnp.dot(mats[1], top, preferred_element_type=F32)
    heat = heat + jnp.dot(mats[0], top, preferred_element_type=F32)
    lane = lax.broadcasted_iota(jnp.int32, (1, width), 1)
    d0 = jnp.full((1, width), day_ref[2 * r], jnp.int32)
    d1 = jnp.full((1, width), day_ref[2 * r + 1], jnp.int32)
    day = jnp.where(lane < BLOCK, d0, d1).astype(F32)
    heat = heat + (day * solar[...]) * clear
    heating[0] = heat
    total = jnp.sum(heat, axis=0, keepdims=True)
    line = lax.broadcasted_iota(jnp.int32, (1, BLOCK), 1)
    acc = shares[...]
    for b in range(2):
        mean = jnp.sum(total[:, b * BLOCK : (b + 1) * BLOCK], axis=1, keepdims=True) * (1.0 / (levels * BLOCK))
        acc = acc + jnp.where(line == own_ref[2 * r + b], mean, 0.0)
    shares[...] = acc


def piece_spec(pieces):
    many, _, _, quarter, _ = pieces[0].shape[-5:]
    shape = (many, 1, 2, quarter, BLOCK)
    if len(pieces) == 1:
        return [pl.BlockSpec((4, *shape), lambda r: (0, 0, r, 0, 0, 0))]
    return [pl.BlockSpec(shape, lambda r: (0, r, 0, 0, 0))] * 4


def row_scratch(levels, half):
    tall = levels + 2 * PAD * 8
    return [
        pltpu.VMEM((2, tall, BLOCK), F32),
        pltpu.VMEM((half, 2, tall, BLOCK), F32),
        pltpu.VMEM((half, 2, levels, BLOCK), F32),
    ]


def heat(pieces, rows, row_of, owners, day, exchange, solar, shares, made=()):
    many, count, _, quarter, _ = pieces[0].shape[-5:]
    half = many - 1
    levels = 4 * quarter
    width = 2 * BLOCK
    bound = jax.ShapeDtypeStruct((count,), jnp.int32)
    whole = pl.BlockSpec((1, BLOCK), lambda r: (0, 0))
    return pl.pallas_call(
        functools.partial(heat_kernel, row_of, len(made)),
        grid=(count,),
        in_specs=[
            SMEM,
            SMEM,
            pl.BlockSpec((2, levels, levels), lambda r: (0, 0, 0)),
            pl.BlockSpec((levels, 1), lambda r: (0, 0)),
            whole,
        ]
        + [ANY] * len(made)
        + piece_spec(pieces),
        out_specs=[
            pl.BlockSpec((half, 1, levels, width), lambda r: (0, row_of(r), 0, 0)),
            pl.BlockSpec((1, levels, width), lambda r: (row_of(r), 0, 0)),
            whole,
            pl.BlockSpec((1, 2, levels, BLOCK), lambda r: (row_of(r), 0, 0, 0)),
            SMEM,
            SMEM,
        ],
        out_shape=[
            jax.ShapeDtypeStruct((2 * half, rows, levels, width), F32),
            jax.ShapeDtypeStruct((rows, levels, width), F32),
            jax.ShapeDtypeStruct((1, BLOCK), F32),
            jax.ShapeDtypeStruct((rows, 2, levels, BLOCK), F32),
            bound,
            bound,
        ],
        input_output_aliases={5: 0, 6: 1, 7: 3} if made else {},
        scratch_shapes=row_scratch(levels, half)
        + [pltpu.VMEM((2, levels, BLOCK), F32), pltpu.VMEM((2, levels, 2 * levels), jnp.bfloat16)],
        compiler_params=params(12),
        cost_estimate=COST,
        name="heat",
    )(owners, day, exchange, solar, shares, *made, *pieces)


def remap_kernel(lo_in, n_in, lo_out, n_out, e_ref, base, *rest):
    *pieces, out, edge, cols, back = rest
    r = pl.program_id(0)
    end = pl.num_programs(0) - 1
    rim = jnp.logical_or(r == 0, r == end)
    at = jnp.clip(r - 1, 0, end - 2)
    side = jnp.minimum(r, 1)
    d0 = jnp.where(rim, lo_out[side], lo_in[at])
    n = jnp.where(rim, n_out[side], n_in[at])
    remap_row(d0, n, e_ref, pieces, 0, edge, cols, back, out)


def remap(inside, outside, e, pieces, base):
    half, rows, _, quarter, _ = pieces[0].shape[-5:]
    levels = 4 * quarter
    width = 2 * BLOCK
    return pl.pallas_call(
        remap_kernel,
        grid=(rows,),
        in_specs=[SMEM] * 4 + [pl.BlockSpec((1, 2, levels, BLOCK), lambda r: (r, 0, 0, 0)), ANY] + piece_spec(pieces),
        out_specs=pl.BlockSpec((half, 1, levels, width), lambda r: (1, r, 0, 0)),
        out_shape=jax.ShapeDtypeStruct((2 * half, rows, levels, width), F32),
        input_output_aliases={5: 0},
        scratch_shapes=row_scratch(levels, half),
        compiler_params=params(12),
        cost_estimate=COST,
        name="remap",
    )(*inside, *outside, e, base, *pieces)


def per_device(fields, thickness, courant_lon, courant_lat, exchange, solar_profile, owners, daylight):
    count = lax.axis_size("lat")
    rows = fields.shape[1]
    ends = count - 1
    hbm = lambda xs: [pltpu.with_memory_space_constraint(x, pltpu.HBM) for x in xs]
    turn = lambda s: [(i, (i + s) % 4) for i in range(4)]
    around = lambda ps: hbm(ps[:1]) + [lax.ppermute(p, "lev", turn(s + 1)) for s, p in enumerate(ps[1:])]
    regroup = lambda x: lax.all_to_all(x, "lev", split_axis=0, concat_axis=0, tiled=True)

    fields, thickness, courant_lon, courant_lat = hbm([fields, thickness, courant_lon, courant_lat])
    head, tail, *inside = inner(fields, courant_lon, courant_lat, thickness)
    prev = lax.ppermute(tail, "lat", [(i, i + 1) for i in range(ends)])
    nxt = lax.ppermute(head, "lat", [(i + 1, i) for i in range(ends)])
    inside = around(inside)
    head, tail = hbm([head, tail])
    outside = [regroup(outer(head, tail, fields, courant_lon, courant_lat, thickness, prev, nxt))]
    second = around(advect(1, fields, courant_lon, courant_lat, prev, nxt))

    other = (owners[:, 0], daylight, exchange, solar_profile[:, None])
    shares = jnp.zeros((1, BLOCK), F32)
    remapped, heating, shares, e, *inside = heat(inside, rows, lambda r: r + 1, *other, shares)
    made = (remapped, heating, e)
    remapped, heating, shares, e, *outside = heat(outside, rows, lambda r: r * (rows - 1), *other, shares, made)
    remapped = remap(inside, outside, e, second, remapped)
    shares = shares[0, :count].reshape(count, 1, 1)
    owner_heat = jnp.sum(lax.all_to_all(shares, "lat", split_axis=0, concat_axis=0, tiled=True)).reshape(1, 1)
    return (remapped, heating, owner_heat)


def solution(mesh):
    placed = (
        P(None, "lat", "lev", None),
        P("lat", "lev", None),
        P("lat", "lev", None),
        P("lat", "lev", None),
        P(),
        P(),
        P(("lat", "lev"), None),
        P(("lat", "lev")),
    )
    return jax.shard_map(
        per_device,
        mesh=mesh,
        in_specs=placed,
        out_specs=(P(None, "lat", None, "lev"), P("lat", None, "lev"), P("lat", "lev")),
        check_vma=False,
    )
```

time: 137 us -> 86.7 us (0.63)
  the two profiles are of different devices: /device:TPU:13 before, /device:TPU:2 now
where the time goes in v3:
time: 86.7 us; the launch traced here: 85.1 us
  Pallas kernels  42.2 us (49%)
  starting transfers between devices  31.2 us (36%)
  waiting for transfers between devices  9.45 us (11%)
    pallas_call x2, Pallas kernels, heat(): pl.pallas_call(functools.partial(heat_kernel, row_of, len(made)), grid=(c...  17.1 us
    ppermute x6, starting transfers between devices, per_device(): lax.ppermute(p, 'lev', turn(s + 1))  12.1 us
    pallas_call x1, Pallas kernels, remap(): pl.pallas_call(remap_kernel, grid=(rows,), in_specs=[SMEM] * 4 + [pl.Bloc...  9.69 us
    ppermute x6, waiting for transfers between devices, per_device(): lax.ppermute(p, 'lev', turn(s + 1))  8.34 us
    all_to_all x1, starting transfers between devices, per_device(): lax.all_to_all(shares, 'lat', split_axis=0, concat_axis=0, tiled=True)  6.83 us
    pallas_call x1, Pallas kernels, inner(): pl.pallas_call(inner_kernel, grid=(levs // 8,), in_specs=[pl.BlockSpec((h...  6.59 us
    ppermute x1, starting transfers between devices, per_device(): nxt = lax.ppermute(head, 'lat', [(i + 1, i) for i in range(ends)])  5.75 us
    pallas_call x1, Pallas kernels, advect(): pl.pallas_call(advect_kernel, grid=(steps,), in_specs=[pl.BlockSpec((half...  5.2 us
  transfers between devices with their start and end apart: 10, of which 3 were waited for; matrix products, arithmetic and copies ran while one was open for 1% of the time, Pallas kernels for 42%

profile of v3, /device:TPU:2, one launch (start us, length us, event | category | flops | bytes accessed | tf_op | source)
XLA Modules:
  0.0 85.1 jit_solution(11221579892584163891)
XLA Ops:
  0.6 6.6 %inner.1 = (f32[4,32,1024]{2,1,0:T(8,128)}, f32[4,32,1024]{2,1,0:T(8,128)}, f32[3,6,2,32,128]{4,3,2,1,0:T(8,128)}, f32[3,6,2,32,128]{4,3,2,1,0:T(8,128)}, f32[3,...) custom-call(f32[4,8,32,1024]{3,2,1,0:T(8,128)} %q.3, f32[4,8,32,1024]{3,2,1,0:T(8,128)} %q.3, ...), custom_call_target="tpu_custom_call" | custom-call | flops 1 | bytes 1 | tf_op jit(solution)/shard_map/inner/pallas_call | solution.py:89
  7.2 1.9 %collective-permute-start.3 = (f32[4,32,1024]{2,1,0:T(8,128)}, f32[4,32,1024]{2,1,0:T(8,128)S(1)}, u32[]{:S(2)}, u32[]{:S(2)}) collective-permute-start(f32[4,32,1024]{2,1,0:T(8,128)} %get-tuple-element.36.tail), channel_id=1, source_target_pairs={{0,4},{4,8},{8,12},{12,16},{16,20},{20,24},{24,28},{28,32},{32,36}... | collective-permute-start | bytes 1572872 | tf_op jit(solution)/shard_map/ppermute | solution.py:459
  9.2 5.8 %collective-permute-start.4 = (f32[4,32,1024]{2,1,0:T(8,128)}, f32[4,32,1024]{2,1,0:T(8,128)S(1)}, u32[]{:S(2)}, u32[]{:S(2)}) collective-permute-start(f32[4,32,1024]{2,1,0:T(8,128)} %get-tuple-element.35.head), channel_id=1, source_target_pairs={{4,0},{8,4},{12,8},{16,12},{20,16},{24,20},{28,24},{32,28},{36,32}... | collective-permute-start | bytes 1572872 | tf_op jit(solution)/shard_map/ppermute | solution.py:460
  14.9 1.6 %collective-permute-start = (f32[3,6,2,32,128]{4,3,2,1,0:T(8,128)}, f32[3,6,2,32,128]{4,3,2,1,0:T(8,128)S(1)}, u32[]{:S(2)}, u32[]{:S(2)}) collective-permute-start(f32[3,6,2,32,128]{4,3,2,1,0:T(8,128)} %get-tuple-element.26), channel_id=1, source_target_pairs={{0,1},{1,2},{2,3},{3,0},{4,5},{5,6},{6,7},{7,4},{8,9},{9,10},{10,1... | collective-permute-start | bytes 1769480 | tf_op jit(solution)/shard_map/ppermute | solution.py:454
  16.6 2.9 %collective-permute-start.1 = (f32[3,6,2,32,128]{4,3,2,1,0:T(8,128)}, f32[3,6,2,32,128]{4,3,2,1,0:T(8,128)S(1)}, u32[]{:S(2)}, u32[]{:S(2)}) collective-permute-start(f32[3,6,2,32,128]{4,3,2,1,0:T(8,128)} %get-tuple-element.27), channel_id=1, source_target_pairs={{0,2},{1,3},{2,0},{3,1},{4,6},{5,7},{6,4},{7,5},{8,10},{9,11},{10,... | collective-permute-start | bytes 1769480 | tf_op jit(solution)/shard_map/ppermute | solution.py:454
  19.5 1.3 %collective-permute-start.2 = (f32[3,6,2,32,128]{4,3,2,1,0:T(8,128)}, f32[3,6,2,32,128]{4,3,2,1,0:T(8,128)}, u32[]{:S(2)}, u32[]{:S(2)}) collective-permute-start(f32[3,6,2,32,128]{4,3,2,1,0:T(8,128)} %get-tuple-element.28), channel_id=1, source_target_pairs={{0,3},{1,0},{2,1},{3,2},{4,7},{5,4},{6,5},{7,6},{8,11},{9,8},{10,9... | collective-permute-start | bytes 1769480 | tf_op jit(solution)/shard_map/ppermute | solution.py:454
  20.8 0.0 collective-permute-done.3.prev
  20.8 1.1 %collective-permute-done.4.nxt = f32[4,32,1024]{2,1,0:T(8,128)S(1)} collective-permute-done((f32[4,32,1024]{2,1,0:T(8,128)}, f32[4,32,1024]{2,1,0:T(8,128)S(1)}, u32[]{:S(2)}, u32[]{:S(2)}) %collective-permute-start.4) | collective-permute-done | bytes 524320 | tf_op jit(solution)/shard_map/ppermute | solution.py:460
  21.9 3.7 %outer.1 = f32[4,3,2,2,32,128]{5,4,3,2,1,0:T(8,128)} custom-call(f32[4,32,1024]{2,1,0:T(8,128)} %get-tuple-element.35.head, f32[4,32,1024]{2,1,0:T(8,128)} %get-tuple-element.36.tail, f32[4,8,32,1024]{3,2,1,0:T(8,128)} %q.3, f32[4,8,32,1024]{3,2,1,0:T(8,128)} %q.3, f32[8,32,1024]{2,1,0:T(8,128)} %c_lon.3, f32[8,32,1024]{2,1,0:T(8,128)} %c_lon.3, ...), custom_call_target="tpu_custom_call" | custom-call | flops 1 | bytes 1 | tf_op jit(solution)/shard_map/outer/pallas_call | solution.py:125
  25.6 0.0 copy-start.3
  25.6 0.0 copy-start
  25.6 0.0 copy-start.1
  25.6 0.0 copy-start.2
  25.6 4.6 %all-to-all-start = ((f32[4,3,2,2,32,128]{5,4,3,2,1,0:T(8,128)}), f32[4,3,2,2,32,128]{5,4,3,2,1,0:T(8,128)S(1)}, u32[]{:S(2)}, u32[]{:S(2)}) async-start(f32[4,3,2,2,32,128]{5,4,3,2,1,0:T(8,128)} %outer.1), calls=%async_computation | async-start | bytes 1572864 | tf_op jit(solution)/shard_map/all_to_all | solution.py:455
  30.2 5.2 %advect.1 = (f32[2,8,2,32,128]{4,3,2,1,0:T(8,128)}, f32[2,8,2,32,128]{4,3,2,1,0:T(8,128)}, f32[2,8,2,32,128]{4,3,2,1,0:T(8,128)}, f32[2,8,2,32,128]{4,3,2,1,0:T(8,128)}) custom-call(f32[4,8,32,1024]{3,2,1,0:T(8,128)} %q.3, f32[8,32,1024]{2,1,0:T(8,128)} %c_lon.3, f32[8,32,1024]{2,1,0:T(8,128)} %c_lat.3, f32[4,32,1024]{2,1,0:T(8,128)S(1)} %collective-permute-done.3.prev, ...), custom_call_target="tpu_custom_call" | custom-call | flops 1 | bytes 1 | tf_op jit(solution)/shard_map/advect/pallas_call | solution.py:191
  35.4 2.1 %collective-permute-start.5 = (f32[2,8,2,32,128]{4,3,2,1,0:T(8,128)}, f32[2,8,2,32,128]{4,3,2,1,0:T(8,128)}, u32[]{:S(2)}, u32[]{:S(2)}) collective-permute-start(f32[2,8,2,32,128]{4,3,2,1,0:T(8,128)} %get-tuple-element.42), channel_id=1, source_target_pairs={{0,1},{1,2},{2,3},{3,0},{4,5},{5,6},{6,7},{7,4},{8,9},{9,10},{10,1... | collective-permute-start | bytes 1572872 | tf_op jit(solution)/shard_map/ppermute | solution.py:454
  37.5 2.7 %collective-permute-start.6 = (f32[2,8,2,32,128]{4,3,2,1,0:T(8,128)}, f32[2,8,2,32,128]{4,3,2,1,0:T(8,128)}, u32[]{:S(2)}, u32[]{:S(2)}) collective-permute-start(f32[2,8,2,32,128]{4,3,2,1,0:T(8,128)} %get-tuple-element.43), channel_id=1, source_target_pairs={{0,2},{1,3},{2,0},{3,1},{4,6},{5,7},{6,4},{7,5},{8,10},{9,11},{10,... | collective-permute-start | bytes 1572872 | tf_op jit(solution)/shard_map/ppermute | solution.py:454
  40.2 0.0 collective-permute-done.rest_1_
  40.2 1.5 %collective-permute-start.7 = (f32[2,8,2,32,128]{4,3,2,1,0:T(8,128)}, f32[2,8,2,32,128]{4,3,2,1,0:T(8,128)}, u32[]{:S(2)}, u32[]{:S(2)}) collective-permute-start(f32[2,8,2,32,128]{4,3,2,1,0:T(8,128)} %get-tuple-element.44), channel_id=1, source_target_pairs={{0,3},{1,0},{2,1},{3,2},{4,7},{5,4},{6,5},{7,6},{8,11},{9,8},{10,9... | collective-permute-start | bytes 1572872 | tf_op jit(solution)/shard_map/ppermute | solution.py:454
  41.7 0.0 copy-done.3
  41.7 0.1 copy.17.solar
  41.8 4.9 %collective-permute-done.1.rest_2_ = f32[3,6,2,32,128]{4,3,2,1,0:T(8,128)S(1)} collective-permute-done((f32[3,6,2,32,128]{4,3,2,1,0:T(8,128)}, f32[3,6,2,32,128]{4,3,2,1,0:T(8,128)S(1)}, u32[]{:S(2)}, u32[]{:S(2)}) %collective-permute-start.1) | collective-permute-done | bytes 589856 | tf_op jit(solution)/shard_map/ppermute | solution.py:454
  46.6 0.0 collective-permute-done.2.rest_3_
  46.7 0.0 copy-done
  46.7 0.0 copy-done.1
  46.7 0.0 copy-done.2
  46.7 12.4 %heat.2 = (f32[4,8,128,256]{3,2,1,0:T(8,128)}, f32[8,128,256]{2,1,0:T(8,128)}, f32[1,128]{1,0:T(1,128)S(1)}, f32[8,2,128,128]{3,2,1,0:T(8,128)S(1)}, s32[6]{0:T(128)S(1)}, /*index=5*/s32[6]{0:T(128)S(1)}) custom-call(s32[16]{0:T(128)S(1)} %bitcast.5, s32[16]{0:T(128)S(1)} %copy-done.2, f32[2,128,128]{2,1,0:T(8,128)S(1)} %copy-done, ...), custom_call_target="tpu_custom_call" | custom-call | flops 1 | bytes 1 | tf_op jit(solution)/shard_map/heat/pallas_call | solution.py:381
  59.0 0.0 all-to-all-done.rest_3_
  59.1 4.7 %heat.3 = (f32[4,8,128,256]{3,2,1,0:T(8,128)}, f32[8,128,256]{2,1,0:T(8,128)}, f32[1,128]{1,0:T(1,128)S(1)}, f32[8,2,128,128]{3,2,1,0:T(8,128)S(1)}, s32[2]{0:T(128)S(1)}, /*index=5*/s32[2]{0:T(128)S(1)}) custom-call(s32[16]{0:T(128)S(1)} %bitcast.6, s32[16]{0:T(128)S(1)} %copy-done.2, ...), custom_call_target="tpu_custom_call", output_to_operand_aliasing={{0}: (5, {}), {1}: (6, {}), {3}: (7, {})} | custom-call | flops 1 | bytes 1 | tf_op jit(solution)/shard_map/heat/pallas_call | solution.py:381
  63.7 0.7 copy.19
  64.4 6.8 %all-to-all-start.1 = ((f32[32,1,1]{2,1,0:T(1,128)}), f32[32,1,1]{2,1,0:T(1,128)S(1)}, u32[]{:S(2)}, u32[]{:S(2)}) async-start(f32[32,1,1]{2,1,0:T(1,128)} %copy.19), calls=%async_computation.1 | async-start | bytes 32768 | tf_op jit(solution)/shard_map/all_to_all | solution.py:473
  71.3 0.0 collective-permute-done.5.rest_1_
  71.3 3.5 %collective-permute-done.6.rest_2_ = f32[2,8,2,32,128]{4,3,2,1,0:T(8,128)} collective-permute-done((f32[2,8,2,32,128]{4,3,2,1,0:T(8,128)}, f32[2,8,2,32,128]{4,3,2,1,0:T(8,128)}, u32[]{:S(2)}, u32[]{:S(2)}) %collective-permute-start.6) | collective-permute-done | bytes 524320 | tf_op jit(solution)/shard_map/ppermute | solution.py:454
  74.8 0.0 collective-permute-done.7.rest_3_
  74.8 9.7 %remap.1 = f32[4,8,128,256]{3,2,1,0:T(8,128)} custom-call(s32[6]{0:T(128)S(1)} %get-tuple-element.29.lo_in, s32[6]{0:T(128)S(1)} %get-tuple-element.30.n_in, s32[2]{0:T(128)S(1)} %get-tuple-element.37.lo_out, s32[2]{0:T(128)S(1)} %get-tuple-element.38.n_out, f32[8,2,128,128]{3,2,1,0:T(8,128)S(1)} %get-tuple-element.39.e_ref, ...), custom_call_target="tpu_custom_call", output_to_operand_aliasing={{}: (5, {})} | custom-call | flops 1 | bytes 1 | tf_op jit(solution)/shard_map/remap/pallas_call | solution.py:434
  84.5 0.0 all-to-all-done.1
  84.5 0.6 reduce_sum.9
  (2 shorter events, 0.0 us)
Async XLA Ops:
  7.2 13.6 %collective-permute-start.3 = (f32[4,32,1024]{2,1,0:T(8,128)}, f32[4,32,1024]{2,1,0:T(8,128)S(1)}, u32[]{:S(2)}, u32[]{:S(2)}) collective-permute-start(f32[4,32,1024]{2,1,0:T(8,128)} %get-tuple-element.36.tail), channel_id=1, source_target_pairs={{0,4},{4,8},{8,12},{12,16},{16,20},{20,24},{24,28},{28,32},{32,36}... | collective-permute-start | bytes 1572872 | tf_op jit(solution)/shard_map/ppermute | solution.py:459
  9.2 12.8 %collective-permute-start.4 = (f32[4,32,1024]{2,1,0:T(8,128)}, f32[4,32,1024]{2,1,0:T(8,128)S(1)}, u32[]{:S(2)}, u32[]{:S(2)}) collective-permute-start(f32[4,32,1024]{2,1,0:T(8,128)} %get-tuple-element.35.head), channel_id=1, source_target_pairs={{4,0},{8,4},{12,8},{16,12},{20,16},{24,20},{28,24},{32,28},{36,32}... | collective-permute-start | bytes 1572872 | tf_op jit(solution)/shard_map/ppermute | solution.py:460
  14.9 25.3 %collective-permute-start = (f32[3,6,2,32,128]{4,3,2,1,0:T(8,128)}, f32[3,6,2,32,128]{4,3,2,1,0:T(8,128)S(1)}, u32[]{:S(2)}, u32[]{:S(2)}) collective-permute-start(f32[3,6,2,32,128]{4,3,2,1,0:T(8,128)} %get-tuple-element.26), channel_id=1, source_target_pairs={{0,1},{1,2},{2,3},{3,0},{4,5},{5,6},{6,7},{7,4},{8,9},{9,10},{10,1... | collective-permute-start | bytes 1769480 | tf_op jit(solution)/shard_map/ppermute | solution.py:454
  16.6 30.1 %collective-permute-start.1 = (f32[3,6,2,32,128]{4,3,2,1,0:T(8,128)}, f32[3,6,2,32,128]{4,3,2,1,0:T(8,128)S(1)}, u32[]{:S(2)}, u32[]{:S(2)}) collective-permute-start(f32[3,6,2,32,128]{4,3,2,1,0:T(8,128)} %get-tuple-element.27), channel_id=1, source_target_pairs={{0,2},{1,3},{2,0},{3,1},{4,6},{5,7},{6,4},{7,5},{8,10},{9,11},{10,... | collective-permute-start | bytes 1769480 | tf_op jit(solution)/shard_map/ppermute | solution.py:454
  19.5 27.2 %collective-permute-start.2 = (f32[3,6,2,32,128]{4,3,2,1,0:T(8,128)}, f32[3,6,2,32,128]{4,3,2,1,0:T(8,128)}, u32[]{:S(2)}, u32[]{:S(2)}) collective-permute-start(f32[3,6,2,32,128]{4,3,2,1,0:T(8,128)} %get-tuple-element.28), channel_id=1, source_target_pairs={{0,3},{1,0},{2,1},{3,2},{4,7},{5,4},{6,5},{7,6},{8,11},{9,8},{10,9... | collective-permute-start | bytes 1769480 | tf_op jit(solution)/shard_map/ppermute | solution.py:454
  25.6 16.1 %copy-start.3 = (f32[128]{0:T(128)S(1)}, f32[128]{0:T(128)}, u32[]{:S(2)}) copy-start(f32[128]{0:T(128)} %param.13) | copy-start | bytes 1540
  25.6 21.1 %copy-start = (f32[2,128,128]{2,1,0:T(8,128)S(1)}, f32[2,128,128]{2,1,0:T(8,128)}, u32[]{:S(2)}) copy-start(f32[2,128,128]{2,1,0:T(8,128)} %exch.3) | copy-start | bytes 393220
  25.6 21.1 %copy-start.1 = (s32[16,1]{0,1:T(1,128)S(1)}, s32[16,1]{0,1:T(1,128)}, u32[]{:S(2)}) copy-start(s32[16,1]{0,1:T(1,128)} %param.14) | copy-start | bytes 196
  25.6 21.1 %copy-start.2 = (s32[16]{0:T(128)S(1)}, s32[16]{0:T(128)}, u32[]{:S(2)}) copy-start(s32[16]{0:T(128)} %day_ref.3) | copy-start | bytes 196
  25.6 33.4 %all-to-all-start = ((f32[4,3,2,2,32,128]{5,4,3,2,1,0:T(8,128)}), f32[4,3,2,2,32,128]{5,4,3,2,1,0:T(8,128)S(1)}, u32[]{:S(2)}, u32[]{:S(2)}) async-start(f32[4,3,2,2,32,128]{5,4,3,2,1,0:T(8,128)} %outer.1), calls=%async_computation | async-start | bytes 1572864 | tf_op jit(solution)/shard_map/all_to_all | solution.py:455
  35.4 35.8 %collective-permute-start.5 = (f32[2,8,2,32,128]{4,3,2,1,0:T(8,128)}, f32[2,8,2,32,128]{4,3,2,1,0:T(8,128)}, u32[]{:S(2)}, u32[]{:S(2)}) collective-permute-start(f32[2,8,2,32,128]{4,3,2,1,0:T(8,128)} %get-tuple-element.42), channel_id=1, source_target_pairs={{0,1},{1,2},{2,3},{3,0},{4,5},{5,6},{6,7},{7,4},{8,9},{9,10},{10,1... | collective-permute-start | bytes 1572872 | tf_op jit(solution)/shard_map/ppermute | solution.py:454
  37.5 37.2 %collective-permute-start.6 = (f32[2,8,2,32,128]{4,3,2,1,0:T(8,128)}, f32[2,8,2,32,128]{4,3,2,1,0:T(8,128)}, u32[]{:S(2)}, u32[]{:S(2)}) collective-permute-start(f32[2,8,2,32,128]{4,3,2,1,0:T(8,128)} %get-tuple-element.43), channel_id=1, source_target_pairs={{0,2},{1,3},{2,0},{3,1},{4,6},{5,7},{6,4},{7,5},{8,10},{9,11},{10,... | collective-permute-start | bytes 1572872 | tf_op jit(solution)/shard_map/ppermute | solution.py:454
  40.2 34.5 %collective-permute-start.7 = (f32[2,8,2,32,128]{4,3,2,1,0:T(8,128)}, f32[2,8,2,32,128]{4,3,2,1,0:T(8,128)}, u32[]{:S(2)}, u32[]{:S(2)}) collective-permute-start(f32[2,8,2,32,128]{4,3,2,1,0:T(8,128)} %get-tuple-element.44), channel_id=1, source_target_pairs={{0,3},{1,0},{2,1},{3,2},{4,7},{5,4},{6,5},{7,6},{8,11},{9,8},{10,9... | collective-permute-start | bytes 1572872 | tf_op jit(solution)/shard_map/ppermute | solution.py:454
  64.4 20.0 %all-to-all-start.1 = ((f32[32,1,1]{2,1,0:T(1,128)}), f32[32,1,1]{2,1,0:T(1,128)S(1)}, u32[]{:S(2)}, u32[]{:S(2)}) async-start(f32[32,1,1]{2,1,0:T(1,128)} %copy.19), calls=%async_computation.1 | async-start | bytes 32768 | tf_op jit(solution)/shard_map/all_to_all | solution.py:473

commit v4 on v3

v4 whole, which is shorter than its diff:
```python
import functools

import jax
import jax.numpy as jnp
from jax import lax
from jax.experimental import pallas as pl
from jax.experimental.pallas import tpu as pltpu
from jax.sharding import PartitionSpec as P

F32 = jnp.float32
HIGH = lax.Precision.HIGHEST
ANY = pl.BlockSpec(memory_space=pl.ANY)
SMEM = pl.BlockSpec(memory_space=pltpu.SMEM)
BLOCK = 128
PAD = 48
RUN = 4
BUNCH = 4
MIB = 1024 * 1024


COST = pl.CostEstimate(flops=1, bytes_accessed=1, transcendentals=0)


def params(mib):
    return pltpu.CompilerParams(vmem_limit_bytes=mib * MIB)


def coefs(c):
    sq = 0.5 * c * c
    half = 0.5 * c
    return 1.0 - 2.0 * sq, sq - half, sq + half


def lon_step(x, w):
    n = x.shape[-1]
    mid, up, down = w
    return mid * x + up * pltpu.roll(x, n - 1, 1) + down * pltpu.roll(x, 1, 1)


def put(sent, k, r, value):
    for d in range(4):
        for h in range(2):
            at = (2 * d + h) * BLOCK
            sent[d, k, r, h] = value[:, at : at + BLOCK]


def staged(ins, outs, sems, body):
    def reads(k):
        return [pltpu.make_async_copy(part(k), buf.at[k], sems.at[k, i]) for i, (part, buf) in enumerate(ins)]

    steps = ins[0][1].shape[0]
    for k in range(steps):
        for c in reads(k):
            c.start()

    def step(k, carry):
        for c in reads(k):
            c.wait()
        body(k, [buf.at[k] for _, buf in ins])
        for c in outs(k):
            c.start()
        return carry

    lax.fori_loop(0, steps, step, 0)
    for k in range(steps):
        for c in outs(k):
            c.wait()


def levs_of(k):
    return pl.ds(pl.multiple_of(k * 8, 8), 8)


def spread_kernel(thick, sent, buf, in_sems, sems):
    def outs(k):
        out = []
        for d in range(4):
            for h in range(2):
                at = (2 * d + h) * BLOCK
                out.append(
                    pltpu.make_async_copy(
                        buf.at[k, :, :, pl.ds(at, BLOCK)], sent.at[d, :, h, levs_of(k), :], sems.at[k, d, h]
                    )
                )
        return out

    staged([(lambda k: thick.at[:, levs_of(k), :], buf)], outs, in_sems, lambda k, bufs: None)


def spread(thickness):
    rows, levs, lon = thickness.shape
    steps = levs // 8
    return pl.pallas_call(
        spread_kernel,
        in_specs=[ANY],
        out_specs=ANY,
        out_shape=pltpu.HBM((4, rows, 2, levs, BLOCK), F32),
        scratch_shapes=[
            pltpu.VMEM((steps, rows, 8, lon), F32),
            pltpu.SemaphoreType.DMA((steps, 1)),
            pltpu.SemaphoreType.DMA((steps, 4, 2)),
        ],
        compiler_params=params(8),
        cost_estimate=COST,
        name="spread",
    )(thickness)


def inner_kernel(fields, c_lon, c_lat, after, head, tail, *rest):
    *sent, q_b, h_b, t_b, lon_b, lat_b, keep, ends, in_sems, sems, end_sems = rest
    nf, rows = q_b.shape[1], q_b.shape[2]
    ins = [
        (lambda k: fields.at[:nf, :, levs_of(k), :], q_b),
        (lambda k: c_lon.at[:, levs_of(k), :], lon_b),
        (lambda k: fields.at[nf:, 0, levs_of(k), :], h_b),
        (lambda k: fields.at[nf:, rows - 1, levs_of(k), :], t_b),
        (lambda k: c_lat.at[:, levs_of(k), :], lat_b),
    ]

    def outs(k):
        out = turned(sent, lambda cols: keep.at[k, :, :, :, cols], sems, k)
        for e, dst in enumerate((head, tail)):
            out.append(pltpu.make_async_copy(ends.at[k, e], dst.at[:, levs_of(k), :], end_sems.at[k, e]))
        return out

    def body(k, bufs):
        q, lon, head_in, tail_in, lat = bufs
        before = here = None
        for r in range(rows):
            w = coefs(lon[r])
            ahead = [lon_step(q[f, r], w) for f in range(nf)]
            if r in (0, rows - 1):
                e, src = (0, head_in) if r == 0 else (1, tail_in)
                for f in range(nf):
                    ends[k, e, f] = ahead[f]
                    ends[k, e, nf + f] = lon_step(src[f], w)
            if r > 1:
                mid, up, down = coefs(lat[r - 1])
                for f in range(nf):
                    keep[k, f, r - 2] = mid * here[f] + up * ahead[f] + down * before[f]
            before, here = here, ahead

    staged(ins, outs, in_sems, body)


def inner(fields, c_lon, c_lat, after):
    nf, rows, levs, lon = fields.shape
    half = nf // 2
    steps = levs // 8
    side = pltpu.HBM((nf, levs, lon), F32)
    sem = pltpu.SemaphoreType.DMA
    return pl.pallas_call(
        inner_kernel,
        in_specs=[ANY] * 4,
        out_specs=[ANY] * 6,
        out_shape=[side, side] + [pltpu.HBM((half, rows - 2, 2, levs, BLOCK), F32)] * 4,
        scratch_shapes=[
            pltpu.VMEM((steps, half, rows, 8, lon), F32),
            pltpu.VMEM((steps, half, 8, lon), F32),
            pltpu.VMEM((steps, half, 8, lon), F32),
            pltpu.VMEM((steps, rows, 8, lon), F32),
            pltpu.VMEM((steps, rows, 8, lon), F32),
            pltpu.VMEM((steps, half, rows - 2, 8, lon), F32),
            pltpu.VMEM((steps, 2, nf, 8, lon), F32),
            sem((steps, 5)),
            sem((steps, 4, 2)),
            sem((steps, 2)),
        ],
        compiler_params=params(20),
        cost_estimate=COST,
        name="inner",
    )(fields, c_lon, c_lat, after)


def outer_kernel(head, tail, q1, q2, c1, c2, l1, l2, prev, nxt, after, sent):
    nf = head.shape[0]
    for e, (here, q, c, lat) in enumerate(((head, q1, c1, l1), (tail, q2, c2, l2))):
        w = coefs(c[0])
        mid, up, down = coefs(lat[0])
        for f in range(nf):
            beside = lon_step(q[f, 0], w)
            before, ahead = (prev[f], beside) if e == 0 else (beside, nxt[f])
            put(sent, f, e, mid * here[f] + up * ahead + down * before)


def outer(head, tail, fields, c_lon, c_lat, prev, nxt, after):
    nf, rows, levs, lon = fields.shape
    half = nf // 2
    steps = levs // 8
    sspec = pl.BlockSpec((half, 8, lon), lambda i: (0, i, 0))
    qrow = lambda r: pl.BlockSpec((half, 1, 8, lon), lambda i: (0, r, i, 0))
    crow = lambda r: pl.BlockSpec((1, 8, lon), lambda i: (r, i, 0))
    end = rows - 1
    return pl.pallas_call(
        outer_kernel,
        grid=(steps,),
        in_specs=[sspec, sspec, qrow(1), qrow(end - 1), crow(1), crow(end - 1)]
        + [crow(0), crow(end), sspec, sspec, ANY],
        out_specs=pl.BlockSpec((4, half, 2, 2, 8, BLOCK), lambda i: (0, 0, 0, 0, i, 0)),
        out_shape=pltpu.HBM((4, half, 2, 2, levs, BLOCK), F32),
        compiler_params=params(12),
        cost_estimate=COST,
        name="outer",
    )(head, tail, fields, fields, c_lon, c_lon, c_lat, c_lat, prev, nxt, after)


def turned(sent, part, sems, k):
    out = []
    for s, dst in enumerate(sent):
        for h in range(2):
            at = pl.multiple_of(lax.rem(lax.axis_index("lev") + s, 4) * (2 * BLOCK) + h * BLOCK, BLOCK)
            lev = pl.multiple_of(k * 8, 8)
            out.append(
                pltpu.make_async_copy(part(pl.ds(at, BLOCK)), dst.at[:, :, h, pl.ds(lev, 8), :], sems.at[k, s, h])
            )
    return out


def advect_kernel(group, fields, c_lon, c_lat, prev, nxt, *rest):
    *sent, q_b, lon_b, lat_b, prev_b, nxt_b, keep, in_sems, sems = rest
    nf, rows = q_b.shape[1], q_b.shape[2]
    which = slice(group * nf, (group + 1) * nf)
    ins = [
        (lambda k: fields.at[which, :, levs_of(k), :], q_b),
        (lambda k: c_lon.at[:, levs_of(k), :], lon_b),
        (lambda k: c_lat.at[:, levs_of(k), :], lat_b),
        (lambda k: prev.at[which, levs_of(k), :], prev_b),
        (lambda k: nxt.at[which, levs_of(k), :], nxt_b),
    ]

    def outs(k):
        return turned(sent, lambda cols: keep.at[k, :, :, :, cols], sems, k)

    def body(k, bufs):
        q, lon, lat, prev_in, nxt_in = bufs
        before = [prev_in[f] for f in range(nf)]
        w = coefs(lon[0])
        here = [lon_step(q[f, 0], w) for f in range(nf)]
        for r in range(rows):
            if r + 1 < rows:
                w = coefs(lon[r + 1])
                ahead = [lon_step(q[f, r + 1], w) for f in range(nf)]
            else:
                ahead = [nxt_in[f] for f in range(nf)]
            mid, up, down = coefs(lat[r])
            for f in range(nf):
                keep[k, f, r] = mid * here[f] + up * ahead[f] + down * before[f]
            before, here = here, ahead

    staged(ins, outs, in_sems, body)


def advect(group, fields, c_lon, c_lat, prev, nxt):
    nf, rows, levs, lon = fields.shape
    half = nf // 2
    steps = levs // 8
    sem = pltpu.SemaphoreType.DMA
    return pl.pallas_call(
        functools.partial(advect_kernel, group),
        in_specs=[ANY] * 5,
        out_specs=[ANY] * 4,
        out_shape=[pltpu.HBM((half, rows, 2, levs, BLOCK), F32)] * 4,
        scratch_shapes=[
            pltpu.VMEM((steps, half, rows, 8, lon), F32),
            pltpu.VMEM((steps, rows, 8, lon), F32),
            pltpu.VMEM((steps, rows, 8, lon), F32),
            pltpu.VMEM((steps, half, 8, lon), F32),
            pltpu.VMEM((steps, half, 8, lon), F32),
            pltpu.VMEM((steps, half, rows, 8, lon), F32),
            sem((steps, 5)),
            sem((steps, 4, 2)),
        ],
        compiler_params=params(20),
        cost_estimate=COST,
        name="advect",
    )(fields, c_lon, c_lat, prev, nxt)


def source(pieces, k):
    if len(pieces) == 1:
        return pieces[0].at[k], k
    return pieces[k], lax.rem(lax.axis_index("lev") + 4 - k, 4)


def remap_row(d0, n, e_ref, pieces, edge, cols, back, out):
    nf = cols.shape[0]
    quarter = pieces[0].shape[-2]
    levels = 4 * quarter
    span = levels // 8
    sub = lax.broadcasted_iota(jnp.int32, (8, BLOCK), 0)

    def tile(ref, i):
        return ref[pl.ds(pl.multiple_of(i * 8, 8), 8), :]

    for h in range(2):
        edge[h, pl.ds(PAD * 8, levels), :] = e_ref[0, h]
        for k in range(4):
            src, s = source(pieces, k)
            for m in range(quarter // 8):
                at = (PAD + 8 * (m % 2)) * 8 + m // 2 + s * (quarter // span)
                for f in range(nf):
                    cols[f, h, pl.ds(at, 8, stride=8), :] = src[f, 0, h, 8 * m : 8 * m + 8, :]

    def extend(i0, frm, turn, stop, fill):
        edge_row = sub == stop
        for t in range(RUN):
            i = i0 + t
            at = pl.ds(pl.multiple_of(i * 8, 8), 8)
            for h in range(2):
                edge[h, at, :] = jnp.where(edge_row, fill, pltpu.roll(tile(edge.at[h], i + frm), turn, 0))
                for f in range(nf):
                    cols[f, h, at, :] = jnp.where(edge_row, 0.0, pltpu.roll(tile(cols.at[f, h], i + frm), turn, 0))

    def above(k, c):
        extend(PAD + span + k * RUN, -span, 7, 7, 4.0 * levels)
        return c

    def below(k, c):
        extend(PAD - (k + 1) * RUN, span, 1, 0, 0.0)
        return c

    most = lax.shift_right_logical(jnp.maximum(d0 + n * RUN - 1, 0) + RUN - 1, RUN.bit_length() - 1)
    least = lax.shift_right_logical(jnp.maximum(-d0, 0) + RUN - 1, RUN.bit_length() - 1)
    lax.fori_loop(0, most, above, 0)
    lax.fori_loop(0, least, below, 0)

    spots = [(h, t) for h in range(2) for t in range(BUNCH)]
    many = len(spots)
    zero = jnp.zeros((8, BLOCK), F32)
    for g0 in range(0, span, BUNCH):
        lows = [(sub * span + (g0 + t)).astype(F32) for t in range(BUNCH)]
        highs = [x + 1.0 for x in lows]

        def some(k, carry):
            olds = list(carry[:many])
            accs = [list(carry[many * (f + 1) : many * (f + 2)]) for f in range(nf)]
            b = PAD + g0 + d0 + k * RUN
            for h in range(2):
                es = [tile(edge.at[h], b + x) for x in range(BUNCH + RUN - 1)]
                qs = [[tile(cols.at[f, h], b + x) for x in range(BUNCH + RUN - 1)] for f in range(nf)]
                for v in range(RUN):
                    for t in range(BUNCH):
                        i = h * BUNCH + t
                        p = jnp.minimum(jnp.maximum(es[v + t], lows[t]), highs[t])
                        w = p - olds[i]
                        olds[i] = p
                        for f in range(nf):
                            accs[f][i] = accs[f][i] + w * qs[f][v + t]
            return (*olds, *sum(accs, []))

        res = lax.fori_loop(0, n, some, (*lows, *lows) + (zero,) * (nf * many))
        for f in range(nf):
            for i, (h, t) in enumerate(spots):
                back[f, h, pl.ds(g0 + t, 8, stride=span), :] = res[many * (f + 1) + i]
    for f in range(nf):
        for h in range(2):
            out[f, 0, :, h * BLOCK : (h + 1) * BLOCK] = back[f, h]


def edges_kernel(thick, e_ref, lo_ref, n_ref, col):
    quarter = thick.shape[3]
    levels = 4 * quarter
    row = lax.broadcasted_iota(jnp.int32, (levels, levels), 0)
    level = (row & 7) * (levels // 8) + lax.shift_right_logical(row, 3)
    j = lax.broadcasted_iota(jnp.int32, (levels, levels), 1)
    lower = (level >= j).astype(F32)
    at_level = level[:, :BLOCK].astype(F32) + 1.0
    low = jnp.zeros((1, 1), F32)
    high = jnp.zeros((1, 1), F32)
    for h in range(2):
        for s in range(4):
            col[h, s * quarter : (s + 1) * quarter, :] = thick[s, 0, h]
        upper = jnp.dot(lower, col[h], precision=HIGH, preferred_element_type=F32)
        e = upper * (levels / upper[levels - 1 :, :])
        e_ref[0, h] = e
        shift = e - at_level
        low = jnp.minimum(low, jnp.min(jnp.min(shift, axis=0, keepdims=True), axis=1, keepdims=True))
        high = jnp.maximum(high, jnp.max(jnp.max(shift, axis=0, keepdims=True), axis=1, keepdims=True))
    lo = jnp.maximum(-jnp.ceil(high), 1.0 - PAD).astype(jnp.int32)
    hi = jnp.minimum(-jnp.floor(low), PAD - 2.0 * RUN).astype(jnp.int32)
    n = lax.shift_right_logical(hi - lo + RUN, RUN.bit_length() - 1)
    lo_ref[0] = jnp.broadcast_to(lo, (1, BLOCK))
    n_ref[0] = jnp.broadcast_to(n, (1, BLOCK))


def edges(thick):
    _, rows, _, quarter, _ = thick.shape
    levels = 4 * quarter
    bound = jax.ShapeDtypeStruct((rows, 1, BLOCK), jnp.int32)
    bspec = pl.BlockSpec((1, 1, BLOCK), lambda r: (r, 0, 0))
    return pl.pallas_call(
        edges_kernel,
        grid=(rows,),
        in_specs=[pl.BlockSpec((4, 1, 2, quarter, BLOCK), lambda r: (0, r, 0, 0, 0))],
        out_specs=[pl.BlockSpec((1, 2, levels, BLOCK), lambda r: (r, 0, 0, 0)), bspec, bspec],
        out_shape=[jax.ShapeDtypeStruct((rows, 2, levels, BLOCK), F32), bound, bound],
        scratch_shapes=[pltpu.VMEM((2, levels, BLOCK), F32)],
        compiler_params=params(12),
        cost_estimate=COST,
        name="edges",
    )(thick)


def halves(x):
    top = x.astype(jnp.bfloat16)
    return top, (x - top.astype(F32)).astype(jnp.bfloat16)


def heat_kernel(row_of, skip, lo_ref, n_ref, own_ref, day_ref, e_ref, exch, solar, so_far, *rest):
    *pieces, out, heating, shares, edge, cols, back, mats = rest
    pieces = pieces[skip:]
    step = pl.program_id(0)
    r = row_of(step)

    @pl.when(step == 0)
    def _():
        shares[...] = so_far[...]
        both = jnp.concatenate([exch[0], exch[1]], axis=1)
        mats[0], mats[1] = halves(both)

    remap_row(lo_ref[r, 0, 0], n_ref[r, 0, 0], e_ref, pieces, edge, cols, back, out)
    temp = out[0, 0]
    hum = out[1, 0]
    levels, width = temp.shape
    square = hum * hum
    clear = 1.0 / (1.0 + square)
    absorb = square * clear
    top, rest_of = halves(jnp.concatenate([absorb * temp, clear * temp], axis=0))
    heat = jnp.dot(mats[0], rest_of, preferred_element_type=F32) + jnp.dot(mats[1], top, preferred_element_type=F32)
    heat = heat + jnp.dot(mats[0], top, preferred_element_type=F32)
    lane = lax.broadcasted_iota(jnp.int32, (1, width), 1)
    d0 = jnp.full((1, width), day_ref[2 * r], jnp.int32)
    d1 = jnp.full((1, width), day_ref[2 * r + 1], jnp.int32)
    day = jnp.where(lane < BLOCK, d0, d1).astype(F32)
    heat = heat + (day * solar[...]) * clear
    heating[0] = heat
    total = jnp.sum(heat, axis=0, keepdims=True)
    line = lax.broadcasted_iota(jnp.int32, (1, BLOCK), 1)
    acc = shares[...]
    for b in range(2):
        mean = jnp.sum(total[:, b * BLOCK : (b + 1) * BLOCK], axis=1, keepdims=True) * (1.0 / (levels * BLOCK))
        acc = acc + jnp.where(line == own_ref[2 * r + b], mean, 0.0)
    shares[...] = acc


def piece_spec(pieces):
    many, _, _, quarter, _ = pieces[0].shape[-5:]
    shape = (many, 1, 2, quarter, BLOCK)
    if len(pieces) == 1:
        return [pl.BlockSpec((4, *shape), lambda r: (0, 0, r, 0, 0, 0))]
    return [pl.BlockSpec(shape, lambda r: (0, r, 0, 0, 0))] * 4


def row_scratch(levels, half):
    tall = levels + 2 * PAD * 8
    return [
        pltpu.VMEM((2, tall, BLOCK), F32),
        pltpu.VMEM((half, 2, tall, BLOCK), F32),
        pltpu.VMEM((half, 2, levels, BLOCK), F32),
    ]


def heat(pieces, bounds, e, rows, row_of, owners, day, exchange, solar, shares, made=()):
    half, count, _, quarter, _ = pieces[0].shape[-5:]
    levels = 4 * quarter
    width = 2 * BLOCK
    whole = pl.BlockSpec((1, BLOCK), lambda r: (0, 0))
    return pl.pallas_call(
        functools.partial(heat_kernel, row_of, len(made)),
        grid=(count,),
        in_specs=[
            SMEM,
            SMEM,
            SMEM,
            SMEM,
            pl.BlockSpec((1, 2, levels, BLOCK), lambda r: (row_of(r), 0, 0, 0)),
            pl.BlockSpec((2, levels, levels), lambda r: (0, 0, 0)),
            pl.BlockSpec((levels, 1), lambda r: (0, 0)),
            whole,
        ]
        + [ANY] * len(made)
        + piece_spec(pieces),
        out_specs=[
            pl.BlockSpec((half, 1, levels, width), lambda r: (0, row_of(r), 0, 0)),
            pl.BlockSpec((1, levels, width), lambda r: (row_of(r), 0, 0)),
            whole,
        ],
        out_shape=[
            jax.ShapeDtypeStruct((2 * half, rows, levels, width), F32),
            jax.ShapeDtypeStruct((rows, levels, width), F32),
            jax.ShapeDtypeStruct((1, BLOCK), F32),
        ],
        input_output_aliases={8: 0, 9: 1} if made else {},
        scratch_shapes=row_scratch(levels, half) + [pltpu.VMEM((2, levels, 2 * levels), jnp.bfloat16)],
        compiler_params=params(12),
        cost_estimate=COST,
        name="heat",
    )(*bounds, owners, day, e, exchange, solar, shares, *made, *pieces)


def remap_kernel(lo_ref, n_ref, e_ref, base, *rest):
    *pieces, out, edge, cols, back = rest
    r = pl.program_id(0)
    remap_row(lo_ref[r, 0, 0], n_ref[r, 0, 0], e_ref, pieces, edge, cols, back, out)


def remap(pieces, bounds, e, base):
    half, rows, _, quarter, _ = pieces[0].shape[-5:]
    levels = 4 * quarter
    width = 2 * BLOCK
    return pl.pallas_call(
        remap_kernel,
        grid=(rows,),
        in_specs=[SMEM] * 2 + [pl.BlockSpec((1, 2, levels, BLOCK), lambda r: (r, 0, 0, 0)), ANY] + piece_spec(pieces),
        out_specs=pl.BlockSpec((half, 1, levels, width), lambda r: (1, r, 0, 0)),
        out_shape=jax.ShapeDtypeStruct((2 * half, rows, levels, width), F32),
        input_output_aliases={3: 0},
        scratch_shapes=row_scratch(levels, half),
        compiler_params=params(12),
        cost_estimate=COST,
        name="remap",
    )(*bounds, e, base, *pieces)


def per_device(fields, thickness, courant_lon, courant_lat, exchange, solar_profile, owners, daylight):
    count = lax.axis_size("lat")
    rows = fields.shape[1]
    ends = count - 1
    hbm = lambda xs: [pltpu.with_memory_space_constraint(x, pltpu.HBM) for x in xs]
    turn = lambda s: [(i, (i + s) % 4) for i in range(4)]
    around = lambda ps: hbm(ps[:1]) + [lax.ppermute(p, "lev", turn(s + 1)) for s, p in enumerate(ps[1:])]
    regroup = lambda x: lax.all_to_all(x, "lev", split_axis=0, concat_axis=0, tiled=True)

    fields, thickness, courant_lon, courant_lat = hbm([fields, thickness, courant_lon, courant_lat])
    thick = spread(thickness)
    head, tail, *inside = inner(fields, courant_lon, courant_lat, *hbm([thick]))
    e, *bounds = edges(regroup(thick))
    prev = lax.ppermute(tail, "lat", [(i, i + 1) for i in range(ends)])
    nxt = lax.ppermute(head, "lat", [(i + 1, i) for i in range(ends)])
    inside = around(inside)
    head, tail = hbm([head, tail])
    outside = [regroup(outer(head, tail, fields, courant_lon, courant_lat, prev, nxt, bounds[0]))]
    second = around(advect(1, fields, courant_lon, courant_lat, prev, nxt))

    other = (owners[:, 0], daylight, exchange, solar_profile[:, None])
    shares = jnp.zeros((1, BLOCK), F32)
    remapped, heating, shares = heat(inside, bounds, e, rows, lambda r: r + 1, *other, shares)
    made = (remapped, heating)
    remapped, heating, shares = heat(outside, bounds, e, rows, lambda r: r * (rows - 1), *other, shares, made)
    remapped = remap(second, bounds, e, remapped)
    shares = shares[0, :count].reshape(count, 1, 1)
    owner_heat = jnp.sum(lax.all_to_all(shares, "lat", split_axis=0, concat_axis=0, tiled=True)).reshape(1, 1)
    return (remapped, heating, owner_heat)


def solution(mesh):
    placed = (
        P(None, "lat", "lev", None),
        P("lat", "lev", None),
        P("lat", "lev", None),
        P("lat", "lev", None),
        P(),
        P(),
        P(("lat", "lev"), None),
        P(("lat", "lev")),
    )
    return jax.shard_map(
        per_device,
        mesh=mesh,
        in_specs=placed,
        out_specs=(P(None, "lat", None, "lev"), P("lat", None, "lev"), P("lat", "lev")),
        check_vma=False,
    )
```

time: 86.7 us -> 80.4 us (0.927)
  the two profiles are of different devices: /device:TPU:2 before, /device:TPU:1 now
where the time goes in v4:
time: 80.4 us; the launch traced here: 78.8 us
  Pallas kernels  41.2 us (51%)
  starting transfers between devices  34.8 us (43%)
  local copies, waits for them, and re-layouts  0.82 us (1%)
    pallas_call x2, Pallas kernels, heat(): pl.pallas_call(functools.partial(heat_kernel, row_of, len(made)), grid=(c...  13.7 us
    ppermute x6, starting transfers between devices, per_device(): lax.ppermute(p, 'lev', turn(s + 1))  10.5 us
    pallas_call x1, Pallas kernels, remap(): pl.pallas_call(remap_kernel, grid=(rows,), in_specs=[SMEM] * 2 + [pl.Bloc...  9.79 us
    all_to_all x2, starting transfers between devices, per_device(): lax.all_to_all(x, 'lev', split_axis=0, concat_axis=0, tiled=True)  9.69 us
    all_to_all x1, starting transfers between devices, per_device(): lax.all_to_all(shares, 'lat', split_axis=0, concat_axis=0, tiled=True)  8.28 us
    pallas_call x1, Pallas kernels, inner(): pl.pallas_call(inner_kernel, in_specs=[ANY] * 4, out_specs=[ANY] * 6, out...  4.45 us
    ppermute x1, starting transfers between devices, per_device(): prev = lax.ppermute(tail, 'lat', [(i, i + 1) for i in range(ends)])  4.39 us
    pallas_call x1, Pallas kernels, advect(): pl.pallas_call(functools.partial(advect_kernel, group), in_specs=[ANY] *...  4.26 us
  transfers between devices with their start and end apart: 11, of which 1 were waited for; matrix products, arithmetic and copies ran while one was open for 1% of the time, Pallas kernels for 50%

profile of v4, /device:TPU:1, one launch (start us, length us, event | category | flops | bytes accessed | tf_op | source)
XLA Modules:
  0.0 78.8 jit_solution(1067221871620826111)
XLA Ops:
  0.6 2.2 %spread.1.after = f32[4,8,2,32,128]{4,3,2,1,0:T(8,128)} custom-call(f32[8,32,1024]{2,1,0:T(8,128)} %thick.1), custom_call_target="tpu_custom_call" | custom-call | flops 1 | bytes 1 | tf_op jit(solution)/shard_map/spread/pallas_call | solution.py:93
  2.8 5.0 %all-to-all-start = ((f32[4,8,2,32,128]{4,3,2,1,0:T(8,128)}), f32[4,8,2,32,128]{4,3,2,1,0:T(8,128)S(1)}, u32[]{:S(2)}, u32[]{:S(2)}) async-start(f32[4,8,2,32,128]{4,3,2,1,0:T(8,128)} %spread.1.after), calls=%async_computation | async-start | bytes 2097152 | tf_op jit(solution)/shard_map/all_to_all | solution.py:532
  7.9 4.5 %inner.1 = (f32[4,32,1024]{2,1,0:T(8,128)}, f32[4,32,1024]{2,1,0:T(8,128)}, f32[2,6,2,32,128]{4,3,2,1,0:T(8,128)}, f32[2,6,2,32,128]{4,3,2,1,0:T(8,128)}, f32[2,...) custom-call(f32[4,8,32,1024]{3,2,1,0:T(8,128)} %fields.3, f32[8,32,1024]{2,1,0:T(8,128)} %c_lon.3, ...), custom_call_target="tpu_custom_call" | custom-call | flops 1 | bytes 1 | tf_op jit(solution)/shard_map/inner/pallas_call | solution.py:152
  12.3 4.4 %collective-permute-start.3 = (f32[4,32,1024]{2,1,0:T(8,128)}, f32[4,32,1024]{2,1,0:T(8,128)S(1)}, u32[]{:S(2)}, u32[]{:S(2)}) collective-permute-start(f32[4,32,1024]{2,1,0:T(8,128)} %get-tuple-element.33.tail), channel_id=1, source_target_pairs={{0,4},{4,8},{8,12},{12,16},{16,20},{20,24},{24,28},{28,32},{32,36}... | collective-permute-start | bytes 1572872 | tf_op jit(solution)/shard_map/ppermute | solution.py:538
  16.7 1.9 %collective-permute-start.4 = (f32[4,32,1024]{2,1,0:T(8,128)}, f32[4,32,1024]{2,1,0:T(8,128)S(1)}, u32[]{:S(2)}, u32[]{:S(2)}) collective-permute-start(f32[4,32,1024]{2,1,0:T(8,128)} %get-tuple-element.32.head), channel_id=1, source_target_pairs={{4,0},{8,4},{12,8},{16,12},{20,16},{24,20},{28,24},{32,28},{36,32}... | collective-permute-start | bytes 1572872 | tf_op jit(solution)/shard_map/ppermute | solution.py:539
  18.7 1.8 %collective-permute-start = (f32[2,6,2,32,128]{4,3,2,1,0:T(8,128)}, f32[2,6,2,32,128]{4,3,2,1,0:T(8,128)}, u32[]{:S(2)}, u32[]{:S(2)}) collective-permute-start(f32[2,6,2,32,128]{4,3,2,1,0:T(8,128)} %get-tuple-element.26), channel_id=1, source_target_pairs={{0,1},{1,2},{2,3},{3,0},{4,5},{5,6},{6,7},{7,4},{8,9},{9,10},{10,1... | collective-permute-start | bytes 1179656 | tf_op jit(solution)/shard_map/ppermute | solution.py:531
  20.5 2.4 %collective-permute-start.1 = (f32[2,6,2,32,128]{4,3,2,1,0:T(8,128)}, f32[2,6,2,32,128]{4,3,2,1,0:T(8,128)}, u32[]{:S(2)}, u32[]{:S(2)}) collective-permute-start(f32[2,6,2,32,128]{4,3,2,1,0:T(8,128)} %get-tuple-element.27), channel_id=1, source_target_pairs={{0,2},{1,3},{2,0},{3,1},{4,6},{5,7},{6,4},{7,5},{8,10},{9,11},{10,... | collective-permute-start | bytes 1179656 | tf_op jit(solution)/shard_map/ppermute | solution.py:531
  22.9 1.2 %collective-permute-start.2 = (f32[2,6,2,32,128]{4,3,2,1,0:T(8,128)}, f32[2,6,2,32,128]{4,3,2,1,0:T(8,128)}, u32[]{:S(2)}, u32[]{:S(2)}) collective-permute-start(f32[2,6,2,32,128]{4,3,2,1,0:T(8,128)} %get-tuple-element.28), channel_id=1, source_target_pairs={{0,3},{1,0},{2,1},{3,2},{4,7},{5,4},{6,5},{7,6},{8,11},{9,8},{10,9... | collective-permute-start | bytes 1179656 | tf_op jit(solution)/shard_map/ppermute | solution.py:531
  24.0 0.0 all-to-all-done.thick
  24.0 3.2 %edges.1 = (f32[8,2,128,128]{3,2,1,0:T(8,128)S(1)}, s32[8,1,128]{2,1,0:T(1,128)S(1)}, s32[8,1,128]{2,1,0:T(1,128)S(1)}) custom-call(f32[4,8,2,32,128]{4,3,2,1,0:T(8,128)S(1)} %all-to-all-done.thick), custom_call_target="tpu_custom_call" | custom-call | flops 1 | bytes 1 | tf_op jit(solution)/shard_map/edges/pallas_call | solution.py:391
  27.3 0.0 collective-permute-done.3.prev
  27.3 0.6 collective-permute-done.4.nxt
  27.8 3.6 %outer.1 = f32[4,2,2,2,32,128]{5,4,3,2,1,0:T(8,128)} custom-call(f32[4,32,1024]{2,1,0:T(8,128)} %get-tuple-element.32.head, f32[4,32,1024]{2,1,0:T(8,128)} %get-tuple-element.33.tail, f32[4,8,32,1024]{3,2,1,0:T(8,128)} %fields.3, f32[4,8,32,1024]{3,2,1,0:T(8,128)} %fields.3, f32[8,32,1024]{2,1,0:T(8,128)} %c_lon.3, f32[8,32,1024]{2,1,0:T(8,128)} %c_lon.3, ...), custom_call_target="tpu_custom_call" | custom-call | flops 1 | bytes 1 | tf_op jit(solution)/shard_map/outer/pallas_call | solution.py:194
  31.4 0.0 copy-start.3
  31.4 0.0 copy-start
  31.4 0.0 copy-start.1
  31.4 0.0 copy-start.2
  31.4 4.7 %all-to-all-start.1 = ((f32[4,2,2,2,32,128]{5,4,3,2,1,0:T(8,128)}), f32[4,2,2,2,32,128]{5,4,3,2,1,0:T(8,128)S(1)}, u32[]{:S(2)}, u32[]{:S(2)}) async-start(f32[4,2,2,2,32,128]{5,4,3,2,1,0:T(8,128)} %outer.1), calls=%async_computation.1 | async-start | bytes 1048576 | tf_op jit(solution)/shard_map/all_to_all | solution.py:532
  36.1 4.3 %advect.1 = (f32[2,8,2,32,128]{4,3,2,1,0:T(8,128)}, f32[2,8,2,32,128]{4,3,2,1,0:T(8,128)}, f32[2,8,2,32,128]{4,3,2,1,0:T(8,128)}, f32[2,8,2,32,128]{4,3,2,1,0:T(8,128)}) custom-call(f32[4,8,32,1024]{3,2,1,0:T(8,128)} %fields.3, f32[8,32,1024]{2,1,0:T(8,128)} %c_lon.3, f32[8,32,1024]{2,1,0:T(8,128)} %c_lat.3, f32[4,32,1024]{2,1,0:T(8,128)S(1)} %collective-permute-done.3.prev, ...), custom_call_target="tpu_custom_call" | custom-call | flops 1 | bytes 1 | tf_op jit(solution)/shard_map/advect/pallas_call | solution.py:258
  40.4 1.5 %collective-permute-start.5 = (f32[2,8,2,32,128]{4,3,2,1,0:T(8,128)}, f32[2,8,2,32,128]{4,3,2,1,0:T(8,128)S(1)}, u32[]{:S(2)}, u32[]{:S(2)}) collective-permute-start(f32[2,8,2,32,128]{4,3,2,1,0:T(8,128)} %get-tuple-element.36), channel_id=1, source_target_pairs={{0,1},{1,2},{2,3},{3,0},{4,5},{5,6},{6,7},{7,4},{8,9},{9,10},{10,1... | collective-permute-start | bytes 1572872 | tf_op jit(solution)/shard_map/ppermute | solution.py:531
  41.9 2.4 %collective-permute-start.6 = (f32[2,8,2,32,128]{4,3,2,1,0:T(8,128)}, f32[2,8,2,32,128]{4,3,2,1,0:T(8,128)S(1)}, u32[]{:S(2)}, u32[]{:S(2)}) collective-permute-start(f32[2,8,2,32,128]{4,3,2,1,0:T(8,128)} %get-tuple-element.37), channel_id=1, source_target_pairs={{0,2},{1,3},{2,0},{3,1},{4,6},{5,7},{6,4},{7,5},{8,10},{9,11},{10,... | collective-permute-start | bytes 1572872 | tf_op jit(solution)/shard_map/ppermute | solution.py:531
  44.3 0.0 collective-permute-done.rest_1_
  44.3 1.2 %collective-permute-start.7 = (f32[2,8,2,32,128]{4,3,2,1,0:T(8,128)}, f32[2,8,2,32,128]{4,3,2,1,0:T(8,128)S(1)}, u32[]{:S(2)}, u32[]{:S(2)}) collective-permute-start(f32[2,8,2,32,128]{4,3,2,1,0:T(8,128)} %get-tuple-element.38), channel_id=1, source_target_pairs={{0,3},{1,0},{2,1},{3,2},{4,7},{5,4},{6,5},{7,6},{8,11},{9,8},{10,9... | collective-permute-start | bytes 1572872 | tf_op jit(solution)/shard_map/ppermute | solution.py:531
  45.5 0.0 copy-done.3
  45.5 0.1 copy.17.solar
  45.6 0.0 collective-permute-done.1.rest_2_
  45.6 0.0 collective-permute-done.2.rest_3_
  45.6 0.0 copy-done
  45.6 0.0 copy-done.1
  45.6 0.0 copy-done.2
  45.6 9.7 %heat.2 = (f32[4,8,128,256]{3,2,1,0:T(8,128)}, f32[8,128,256]{2,1,0:T(8,128)}, f32[1,128]{1,0:T(1,128)S(1)}) custom-call(s32[8,1,128]{2,1,0:T(1,128)S(1)} %get-tuple-element.22.lo_ref.after, s32[8,1,128]{2,1,0:T(1,128)S(1)} %get-tuple-element.23.n_ref, s32[16]{0:T(128)S(1)} %bitcast.5, s32[16]{0:T(128)S(1)} %copy-done.2, ...), custom_call_target="tpu_custom_call" | custom-call | flops 1 | bytes 1 | tf_op jit(solution)/shard_map/heat/pallas_call | solution.py:468
  55.3 0.0 all-to-all-done.1.rest_2_
  55.4 4.0 %heat.3 = (f32[4,8,128,256]{3,2,1,0:T(8,128)}, f32[8,128,256]{2,1,0:T(8,128)}, f32[1,128]{1,0:T(1,128)S(1)}) custom-call(s32[8,1,128]{2,1,0:T(1,128)S(1)} %get-tuple-element.22.lo_ref.after, s32[8,1,128]{2,1,0:T(1,128)S(1)} %get-tuple-element.23.n_ref, s32[16]{0:T(128)S(1)} %bitcast.6, ...), custom_call_target="tpu_custom_call", output_to_operand_aliasing={{0}: (8, {}), {1}: (9, {})} | custom-call | flops 1 | bytes 1 | tf_op jit(solution)/shard_map/heat/pallas_call | solution.py:468
  59.4 0.7 copy.18
  60.1 8.3 %all-to-all-start.2 = ((f32[32,1,1]{2,1,0:T(1,128)}), f32[32,1,1]{2,1,0:T(1,128)S(1)}, u32[]{:S(2)}, u32[]{:S(2)}) async-start(f32[32,1,1]{2,1,0:T(1,128)} %copy.18), calls=%async_computation.2 | async-start | bytes 32768 | tf_op jit(solution)/shard_map/all_to_all | solution.py:552
  68.4 0.0 collective-permute-done.5.rest_1_
  68.4 0.0 collective-permute-done.6.rest_2_
  68.4 0.0 collective-permute-done.7.rest_3_
  68.4 9.8 %remap.1 = f32[4,8,128,256]{3,2,1,0:T(8,128)} custom-call(s32[8,1,128]{2,1,0:T(1,128)S(1)} %get-tuple-element.22.lo_ref.after, s32[8,1,128]{2,1,0:T(1,128)S(1)} %get-tuple-element.23.n_ref, f32[8,2,128,128]{3,2,1,0:T(8,128)S(1)} %get-tuple-element.24.e_ref, f32[4,8,128,256]{3,2,1,0:T(8,128)} %get-tuple-element.34.base, ...), custom_call_target="tpu_custom_call", output_to_operand_aliasing={{}: (3, {})} | custom-call | flops 1 | bytes 1 | tf_op jit(solution)/shard_map/remap/pallas_call | solution.py:511
  78.2 0.0 all-to-all-done.2
  78.2 0.6 reduce_sum.9
  (2 shorter events, 0.0 us)
Async XLA Ops:
  2.8 21.2 %all-to-all-start = ((f32[4,8,2,32,128]{4,3,2,1,0:T(8,128)}), f32[4,8,2,32,128]{4,3,2,1,0:T(8,128)S(1)}, u32[]{:S(2)}, u32[]{:S(2)}) async-start(f32[4,8,2,32,128]{4,3,2,1,0:T(8,128)} %spread.1.after), calls=%async_computation | async-start | bytes 2097152 | tf_op jit(solution)/shard_map/all_to_all | solution.py:532
  12.3 14.9 %collective-permute-start.3 = (f32[4,32,1024]{2,1,0:T(8,128)}, f32[4,32,1024]{2,1,0:T(8,128)S(1)}, u32[]{:S(2)}, u32[]{:S(2)}) collective-permute-start(f32[4,32,1024]{2,1,0:T(8,128)} %get-tuple-element.33.tail), channel_id=1, source_target_pairs={{0,4},{4,8},{8,12},{12,16},{16,20},{20,24},{24,28},{28,32},{32,36}... | collective-permute-start | bytes 1572872 | tf_op jit(solution)/shard_map/ppermute | solution.py:538
  16.7 11.1 %collective-permute-start.4 = (f32[4,32,1024]{2,1,0:T(8,128)}, f32[4,32,1024]{2,1,0:T(8,128)S(1)}, u32[]{:S(2)}, u32[]{:S(2)}) collective-permute-start(f32[4,32,1024]{2,1,0:T(8,128)} %get-tuple-element.32.head), channel_id=1, source_target_pairs={{4,0},{8,4},{12,8},{16,12},{20,16},{24,20},{28,24},{32,28},{36,32}... | collective-permute-start | bytes 1572872 | tf_op jit(solution)/shard_map/ppermute | solution.py:539
  18.7 25.6 %collective-permute-start = (f32[2,6,2,32,128]{4,3,2,1,0:T(8,128)}, f32[2,6,2,32,128]{4,3,2,1,0:T(8,128)}, u32[]{:S(2)}, u32[]{:S(2)}) collective-permute-start(f32[2,6,2,32,128]{4,3,2,1,0:T(8,128)} %get-tuple-element.26), channel_id=1, source_target_pairs={{0,1},{1,2},{2,3},{3,0},{4,5},{5,6},{6,7},{7,4},{8,9},{9,10},{10,1... | collective-permute-start | bytes 1179656 | tf_op jit(solution)/shard_map/ppermute | solution.py:531
  20.5 25.1 %collective-permute-start.1 = (f32[2,6,2,32,128]{4,3,2,1,0:T(8,128)}, f32[2,6,2,32,128]{4,3,2,1,0:T(8,128)}, u32[]{:S(2)}, u32[]{:S(2)}) collective-permute-start(f32[2,6,2,32,128]{4,3,2,1,0:T(8,128)} %get-tuple-element.27), channel_id=1, source_target_pairs={{0,2},{1,3},{2,0},{3,1},{4,6},{5,7},{6,4},{7,5},{8,10},{9,11},{10,... | collective-permute-start | bytes 1179656 | tf_op jit(solution)/shard_map/ppermute | solution.py:531
  22.9 22.7 %collective-permute-start.2 = (f32[2,6,2,32,128]{4,3,2,1,0:T(8,128)}, f32[2,6,2,32,128]{4,3,2,1,0:T(8,128)}, u32[]{:S(2)}, u32[]{:S(2)}) collective-permute-start(f32[2,6,2,32,128]{4,3,2,1,0:T(8,128)} %get-tuple-element.28), channel_id=1, source_target_pairs={{0,3},{1,0},{2,1},{3,2},{4,7},{5,4},{6,5},{7,6},{8,11},{9,8},{10,9... | collective-permute-start | bytes 1179656 | tf_op jit(solution)/shard_map/ppermute | solution.py:531
  31.4 14.1 %copy-start.3 = (f32[128]{0:T(128)S(1)}, f32[128]{0:T(128)}, u32[]{:S(2)}) copy-start(f32[128]{0:T(128)} %param.13) | copy-start | bytes 1540
  31.4 14.2 %copy-start = (f32[2,128,128]{2,1,0:T(8,128)S(1)}, f32[2,128,128]{2,1,0:T(8,128)}, u32[]{:S(2)}) copy-start(f32[2,128,128]{2,1,0:T(8,128)} %exch.3) | copy-start | bytes 393220
  31.4 14.2 %copy-start.1 = (s32[16,1]{0,1:T(1,128)S(1)}, s32[16,1]{0,1:T(1,128)}, u32[]{:S(2)}) copy-start(s32[16,1]{0,1:T(1,128)} %param.14) | copy-start | bytes 196
  31.4 14.2 %copy-start.2 = (s32[16]{0:T(128)S(1)}, s32[16]{0:T(128)}, u32[]{:S(2)}) copy-start(s32[16]{0:T(128)} %day_ref.3) | copy-start | bytes 196
  31.4 23.9 %all-to-all-start.1 = ((f32[4,2,2,2,32,128]{5,4,3,2,1,0:T(8,128)}), f32[4,2,2,2,32,128]{5,4,3,2,1,0:T(8,128)S(1)}, u32[]{:S(2)}, u32[]{:S(2)}) async-start(f32[4,2,2,2,32,128]{5,4,3,2,1,0:T(8,128)} %outer.1), calls=%async_computation.1 | async-start | bytes 1048576 | tf_op jit(solution)/shard_map/all_to_all | solution.py:532
  40.4 28.0 %collective-permute-start.5 = (f32[2,8,2,32,128]{4,3,2,1,0:T(8,128)}, f32[2,8,2,32,128]{4,3,2,1,0:T(8,128)S(1)}, u32[]{:S(2)}, u32[]{:S(2)}) collective-permute-start(f32[2,8,2,32,128]{4,3,2,1,0:T(8,128)} %get-tuple-element.36), channel_id=1, source_target_pairs={{0,1},{1,2},{2,3},{3,0},{4,5},{5,6},{6,7},{7,4},{8,9},{9,10},{10,1... | collective-permute-start | bytes 1572872 | tf_op jit(solution)/shard_map/ppermute | solution.py:531
  41.9 26.5 %collective-permute-start.6 = (f32[2,8,2,32,128]{4,3,2,1,0:T(8,128)}, f32[2,8,2,32,128]{4,3,2,1,0:T(8,128)S(1)}, u32[]{:S(2)}, u32[]{:S(2)}) collective-permute-start(f32[2,8,2,32,128]{4,3,2,1,0:T(8,128)} %get-tuple-element.37), channel_id=1, source_target_pairs={{0,2},{1,3},{2,0},{3,1},{4,6},{5,7},{6,4},{7,5},{8,10},{9,11},{10,... | collective-permute-start | bytes 1572872 | tf_op jit(solution)/shard_map/ppermute | solution.py:531
  44.3 24.1 %collective-permute-start.7 = (f32[2,8,2,32,128]{4,3,2,1,0:T(8,128)}, f32[2,8,2,32,128]{4,3,2,1,0:T(8,128)S(1)}, u32[]{:S(2)}, u32[]{:S(2)}) collective-permute-start(f32[2,8,2,32,128]{4,3,2,1,0:T(8,128)} %get-tuple-element.38), channel_id=1, source_target_pairs={{0,3},{1,0},{2,1},{3,2},{4,7},{5,4},{6,5},{7,6},{8,11},{9,8},{10,9... | collective-permute-start | bytes 1572872 | tf_op jit(solution)/shard_map/ppermute | solution.py:531
  60.1 18.1 %all-to-all-start.2 = ((f32[32,1,1]{2,1,0:T(1,128)}), f32[32,1,1]{2,1,0:T(1,128)S(1)}, u32[]{:S(2)}, u32[]{:S(2)}) async-start(f32[32,1,1]{2,1,0:T(1,128)} %copy.18), calls=%async_computation.2 | async-start | bytes 32768 | tf_op jit(solution)/shard_map/all_to_all | solution.py:552

commit v5 on v4

--- a/solution.py
+++ b/solution.py
@@ -12,9 +12,10 @@
 ANY = pl.BlockSpec(memory_space=pl.ANY)
 SMEM = pl.BlockSpec(memory_space=pltpu.SMEM)
 BLOCK = 128
-PAD = 48
-RUN = 4
-BUNCH = 4
+PAD = 56
+RUN = 8
+BUNCH = 2
+EARLY = 0
 MIB = 1024 * 1024
 
 
@@ -35,13 +36,6 @@
     n = x.shape[-1]
     mid, up, down = w
     return mid * x + up * pltpu.roll(x, n - 1, 1) + down * pltpu.roll(x, 1, 1)
-
-
-def put(sent, k, r, value):
-    for d in range(4):
-        for h in range(2):
-            at = (2 * d + h) * BLOCK
-            sent[d, k, r, h] = value[:, at : at + BLOCK]
 
 
 def staged(ins, outs, sems, body):
@@ -71,18 +65,19 @@
     return pl.ds(pl.multiple_of(k * 8, 8), 8)
 
 
+def fanned(sent, part, sems, k):
+    out = []
+    for d in range(4):
+        for h in range(2):
+            at = (2 * d + h) * BLOCK
+            dst = sent.at[(d,) + (slice(None),) * (len(sent.shape) - 4) + (h, levs_of(k), slice(None))]
+            out.append(pltpu.make_async_copy(part(pl.ds(at, BLOCK)), dst, sems.at[k, d, h]))
+    return out
+
+
 def spread_kernel(thick, sent, buf, in_sems, sems):
     def outs(k):
-        out = []
-        for d in range(4):
-            for h in range(2):
-                at = (2 * d + h) * BLOCK
-                out.append(
-                    pltpu.make_async_copy(
-                        buf.at[k, :, :, pl.ds(at, BLOCK)], sent.at[d, :, h, levs_of(k), :], sems.at[k, d, h]
-                    )
-                )
-        return out
+        return fanned(sent, lambda cols: buf.at[k, :, :, cols], sems, k)
 
     staged([(lambda k: thick.at[:, levs_of(k), :], buf)], outs, in_sems, lambda k, bufs: None)
 
@@ -107,12 +102,13 @@
 
 
 def inner_kernel(fields, c_lon, c_lat, after, head, tail, *rest):
-    *sent, q_b, h_b, t_b, lon_b, lat_b, keep, ends, in_sems, sems, end_sems = rest
+    *sent, q_b, p_b, t_b, lon_b, lat_b, keep, ends, in_sems, sems, end_sems = rest
     nf, rows = q_b.shape[1], q_b.shape[2]
+    more = p_b.shape[2]
     ins = [
         (lambda k: fields.at[:nf, :, levs_of(k), :], q_b),
         (lambda k: c_lon.at[:, levs_of(k), :], lon_b),
-        (lambda k: fields.at[nf:, 0, levs_of(k), :], h_b),
+        (lambda k: fields.at[nf:, :more, levs_of(k), :], p_b),
         (lambda k: fields.at[nf:, rows - 1, levs_of(k), :], t_b),
         (lambda k: c_lat.at[:, levs_of(k), :], lat_b),
     ]
@@ -123,85 +119,102 @@
             out.append(pltpu.make_async_copy(ends.at[k, e], dst.at[:, levs_of(k), :], end_sems.at[k, e]))
         return out
 
-    def body(k, bufs):
-        q, lon, head_in, tail_in, lat = bufs
+    def body(k, got):
+        q, lon, p, tail_in, lat = got
         before = here = None
         for r in range(rows):
             w = coefs(lon[r])
             ahead = [lon_step(q[f, r], w) for f in range(nf)]
-            if r in (0, rows - 1):
-                e, src = (0, head_in) if r == 0 else (1, tail_in)
+            ahead += [lon_step(p[f, r], w) for f in range(nf if r < more else 0)]
+            if r == 0:
+                for f in range(2 * nf):
+                    ends[k, 0, f] = ahead[f]
+            if r == rows - 1:
                 for f in range(nf):
-                    ends[k, e, f] = ahead[f]
-                    ends[k, e, nf + f] = lon_step(src[f], w)
+                    ends[k, 1, f] = ahead[f]
+                    ends[k, 1, nf + f] = lon_step(tail_in[f], w)
             if r > 1:
                 mid, up, down = coefs(lat[r - 1])
-                for f in range(nf):
-                    keep[k, f, r - 2] = mid * here[f] + up * ahead[f] + down * before[f]
+                for f in range(len(ahead)):
+                    slot = r - 2 if f < nf else rows - 4 + r
+                    keep[k, f % nf, slot] = mid * here[f] + up * ahead[f] + down * before[f]
             before, here = here, ahead
 
     staged(ins, outs, in_sems, body)
 
 
-def inner(fields, c_lon, c_lat, after):
+def inner(fields, c_lon, c_lat, after, early):
     nf, rows, levs, lon = fields.shape
     half = nf // 2
     steps = levs // 8
+    count = rows - 2 + early
     side = pltpu.HBM((nf, levs, lon), F32)
     sem = pltpu.SemaphoreType.DMA
+    shapes = [(half, rows), (half, early + 2), (half,), (rows,), (rows,), (half, count), (2, nf)]
     return pl.pallas_call(
         inner_kernel,
         in_specs=[ANY] * 4,
         out_specs=[ANY] * 6,
-        out_shape=[side, side] + [pltpu.HBM((half, rows - 2, 2, levs, BLOCK), F32)] * 4,
-        scratch_shapes=[
-            pltpu.VMEM((steps, half, rows, 8, lon), F32),
-            pltpu.VMEM((steps, half, 8, lon), F32),
-            pltpu.VMEM((steps, half, 8, lon), F32),
-            pltpu.VMEM((steps, rows, 8, lon), F32),
-            pltpu.VMEM((steps, rows, 8, lon), F32),
-            pltpu.VMEM((steps, half, rows - 2, 8, lon), F32),
-            pltpu.VMEM((steps, 2, nf, 8, lon), F32),
-            sem((steps, 5)),
-            sem((steps, 4, 2)),
-            sem((steps, 2)),
-        ],
+        out_shape=[side, side] + [pltpu.HBM((half, count, 2, levs, BLOCK), F32)] * 4,
+        scratch_shapes=[pltpu.VMEM((steps, *x, 8, lon), F32) for x in shapes]
+        + [sem((steps, 5)), sem((steps, 4, 2)), sem((steps, 2))],
         compiler_params=params(20),
         cost_estimate=COST,
         name="inner",
     )(fields, c_lon, c_lat, after)
 
 
-def outer_kernel(head, tail, q1, q2, c1, c2, l1, l2, prev, nxt, after, sent):
-    nf = head.shape[0]
-    for e, (here, q, c, lat) in enumerate(((head, q1, c1, l1), (tail, q2, c2, l2))):
-        w = coefs(c[0])
-        mid, up, down = coefs(lat[0])
+def outer_kernel(fields, c_lon, c_lat, head, tail, prev, nxt, after, sent, *rest):
+    *bufs, keep, in_sems, sems = rest
+    nf = keep.shape[1]
+    rows = c_lon.shape[0]
+    reads = (
+        lambda k: head.at[:nf, levs_of(k), :],
+        lambda k: tail.at[:nf, levs_of(k), :],
+        lambda k: prev.at[:nf, levs_of(k), :],
+        lambda k: nxt.at[:nf, levs_of(k), :],
+        lambda k: fields.at[:nf, 1, levs_of(k), :],
+        lambda k: fields.at[:nf, rows - 2, levs_of(k), :],
+        lambda k: c_lon.at[1, levs_of(k), :],
+        lambda k: c_lon.at[rows - 2, levs_of(k), :],
+        lambda k: c_lat.at[0, levs_of(k), :],
+        lambda k: c_lat.at[rows - 1, levs_of(k), :],
+    )
+
+    def outs(k):
+        return fanned(sent, lambda cols: keep.at[k, :, :, :, cols], sems, k)
+
+    def body(k, got):
+        top, end, north, south, q_top, q_end, lon, lon_end, lat, lat_end = got
+        w = coefs(lon[...])
+        mid, up, down = coefs(lat[...])
         for f in range(nf):
-            beside = lon_step(q[f, 0], w)
-            before, ahead = (prev[f], beside) if e == 0 else (beside, nxt[f])
-            put(sent, f, e, mid * here[f] + up * ahead + down * before)
-
-
-def outer(head, tail, fields, c_lon, c_lat, prev, nxt, after):
+            keep[k, f, 0] = mid * top[f] + up * lon_step(q_top[f], w) + down * north[f]
+        w = coefs(lon_end[...])
+        mid, up, down = coefs(lat_end[...])
+        for f in range(nf):
+            keep[k, f, 1] = mid * end[f] + up * south[f] + down * lon_step(q_end[f], w)
+
+    staged(list(zip(reads, bufs)), outs, in_sems, body)
+
+
+def outer(fields, c_lon, c_lat, head, tail, prev, nxt, after):
     nf, rows, levs, lon = fields.shape
     half = nf // 2
     steps = levs // 8
-    sspec = pl.BlockSpec((half, 8, lon), lambda i: (0, i, 0))
-    qrow = lambda r: pl.BlockSpec((half, 1, 8, lon), lambda i: (0, r, i, 0))
-    crow = lambda r: pl.BlockSpec((1, 8, lon), lambda i: (r, i, 0))
-    end = rows - 1
+    sem = pltpu.SemaphoreType.DMA
+    shapes = [(half,)] * 6 + [()] * 4
     return pl.pallas_call(
         outer_kernel,
-        grid=(steps,),
-        in_specs=[sspec, sspec, qrow(1), qrow(end - 1), crow(1), crow(end - 1)]
-        + [crow(0), crow(end), sspec, sspec, ANY],
-        out_specs=pl.BlockSpec((4, half, 2, 2, 8, BLOCK), lambda i: (0, 0, 0, 0, i, 0)),
+        in_specs=[ANY] * 8,
+        out_specs=ANY,
         out_shape=pltpu.HBM((4, half, 2, 2, levs, BLOCK), F32),
-        compiler_params=params(12),
+        scratch_shapes=[pltpu.VMEM((steps, *x, 8, lon), F32) for x in shapes]
+        + [pltpu.VMEM((steps, half, 2, 8, lon), F32), sem((steps, len(shapes))), sem((steps, 4, 2))],
+        compiler_params=params(20),
         cost_estimate=COST,
         name="outer",
-    )(head, tail, fields, fields, c_lon, c_lon, c_lat, c_lat, prev, nxt, after)
+    )(fields, c_lon, c_lat, head, tail, prev, nxt, after)
 
 
 def turned(sent, part, sems, k):
@@ -216,60 +229,57 @@
     return out
 
 
-def advect_kernel(group, fields, c_lon, c_lat, prev, nxt, *rest):
+def advect_kernel(fields, c_lon, c_lat, prev, nxt, *rest):
     *sent, q_b, lon_b, lat_b, prev_b, nxt_b, keep, in_sems, sems = rest
-    nf, rows = q_b.shape[1], q_b.shape[2]
-    which = slice(group * nf, (group + 1) * nf)
+    nf, count = keep.shape[1], keep.shape[2]
+    rows = c_lon.shape[0]
+    early = rows - count
     ins = [
-        (lambda k: fields.at[which, :, levs_of(k), :], q_b),
+        (lambda k: fields.at[nf:, :, levs_of(k), :], q_b),
         (lambda k: c_lon.at[:, levs_of(k), :], lon_b),
         (lambda k: c_lat.at[:, levs_of(k), :], lat_b),
-        (lambda k: prev.at[which, levs_of(k), :], prev_b),
-        (lambda k: nxt.at[which, levs_of(k), :], nxt_b),
+        (lambda k: prev.at[nf:, levs_of(k), :], prev_b),
+        (lambda k: nxt.at[nf:, levs_of(k), :], nxt_b),
     ]
 
     def outs(k):
         return turned(sent, lambda cols: keep.at[k, :, :, :, cols], sems, k)
 
-    def body(k, bufs):
-        q, lon, lat, prev_in, nxt_in = bufs
-        before = [prev_in[f] for f in range(nf)]
-        w = coefs(lon[0])
-        here = [lon_step(q[f, 0], w) for f in range(nf)]
-        for r in range(rows):
-            if r + 1 < rows:
-                w = coefs(lon[r + 1])
-                ahead = [lon_step(q[f, r + 1], w) for f in range(nf)]
-            else:
-                ahead = [nxt_in[f] for f in range(nf)]
+    def body(k, got):
+        q, lon, lat, north, south = got
+
+        def stepped(r):
+            w = coefs(lon[r])
+            return [lon_step(q[f, r], w) for f in range(nf)]
+
+        def finish(slot, r, before, here, ahead):
             mid, up, down = coefs(lat[r])
             for f in range(nf):
-                keep[k, f, r] = mid * here[f] + up * ahead[f] + down * before[f]
+                keep[k, f, slot] = mid * here[f] + up * ahead[f] + down * before[f]
+
+        here, ahead = stepped(0), stepped(1)
+        finish(0, 0, [north[f] for f in range(nf)], here, ahead)
+        before, here = (stepped(early), stepped(early + 1)) if early else (here, ahead)
+        for r in range(early + 1, rows):
+            ahead = stepped(r + 1) if r + 1 < rows else [south[f] for f in range(nf)]
+            finish(r - early, r, before, here, ahead)
             before, here = here, ahead
 
     staged(ins, outs, in_sems, body)
 
 
-def advect(group, fields, c_lon, c_lat, prev, nxt):
+def advect(fields, c_lon, c_lat, prev, nxt, early):
     nf, rows, levs, lon = fields.shape
-    half = nf // 2
+    half, count = nf // 2, rows - early
     steps = levs // 8
     sem = pltpu.SemaphoreType.DMA
-    return pl.pallas_call(
-        functools.partial(advect_kernel, group),
+    shapes = [(half, rows), (rows,), (rows,), (half,), (half,), (half, count)]
+    return pl.pallas_call(
+        advect_kernel,
         in_specs=[ANY] * 5,
         out_specs=[ANY] * 4,
-        out_shape=[pltpu.HBM((half, rows, 2, levs, BLOCK), F32)] * 4,
-        scratch_shapes=[
-            pltpu.VMEM((steps, half, rows, 8, lon), F32),
-            pltpu.VMEM((steps, rows, 8, lon), F32),
-            pltpu.VMEM((steps, rows, 8, lon), F32),
-            pltpu.VMEM((steps, half, 8, lon), F32),
-            pltpu.VMEM((steps, half, 8, lon), F32),
-            pltpu.VMEM((steps, half, rows, 8, lon), F32),
-            sem((steps, 5)),
-            sem((steps, 4, 2)),
-        ],
+        out_shape=[pltpu.HBM((half, count, 2, levs, BLOCK), F32)] * 4,
+        scratch_shapes=[pltpu.VMEM((steps, *x, 8, lon), F32) for x in shapes] + [sem((steps, 5)), sem((steps, 4, 2))],
         compiler_params=params(20),
         cost_estimate=COST,
         name="advect",
@@ -363,19 +373,22 @@
     row = lax.broadcasted_iota(jnp.int32, (levels, levels), 0)
     level = (row & 7) * (levels // 8) + lax.shift_right_logical(row, 3)
     j = lax.broadcasted_iota(jnp.int32, (levels, levels), 1)
-    lower = (level >= j).astype(F32)
-    at_level = level[:, :BLOCK].astype(F32) + 1.0
-    low = jnp.zeros((1, 1), F32)
-    high = jnp.zeros((1, 1), F32)
+    lower = (level >= j).astype(jnp.bfloat16)
+    at_level = (level[:, :1] + 1).astype(F32)
     for h in range(2):
         for s in range(4):
-            col[h, s * quarter : (s + 1) * quarter, :] = thick[s, 0, h]
-        upper = jnp.dot(lower, col[h], precision=HIGH, preferred_element_type=F32)
-        e = upper * (levels / upper[levels - 1 :, :])
-        e_ref[0, h] = e
-        shift = e - at_level
-        low = jnp.minimum(low, jnp.min(jnp.min(shift, axis=0, keepdims=True), axis=1, keepdims=True))
-        high = jnp.maximum(high, jnp.max(jnp.max(shift, axis=0, keepdims=True), axis=1, keepdims=True))
+            col[s * quarter : (s + 1) * quarter, h * BLOCK : (h + 1) * BLOCK] = thick[s, 0, h]
+    top, low = halves(col[...])
+    least = col[...] - top.astype(F32) - low.astype(F32)
+    upper = jnp.dot(lower, least.astype(jnp.bfloat16), preferred_element_type=F32)
+    upper = upper + jnp.dot(lower, low, preferred_element_type=F32)
+    upper = upper + jnp.dot(lower, top, preferred_element_type=F32)
+    e = upper * (levels / upper[levels - 1 :, :])
+    for h in range(2):
+        e_ref[0, h] = e[:, h * BLOCK : (h + 1) * BLOCK]
+    shift = e - at_level
+    low = jnp.minimum(jnp.min(jnp.min(shift, axis=0, keepdims=True), axis=1, keepdims=True), 0.0)
+    high = jnp.maximum(jnp.max(jnp.max(shift, axis=0, keepdims=True), axis=1, keepdims=True), 0.0)
     lo = jnp.maximum(-jnp.ceil(high), 1.0 - PAD).astype(jnp.int32)
     hi = jnp.minimum(-jnp.floor(low), PAD - 2.0 * RUN).astype(jnp.int32)
     n = lax.shift_right_logical(hi - lo + RUN, RUN.bit_length() - 1)
@@ -394,7 +407,7 @@
         in_specs=[pl.BlockSpec((4, 1, 2, quarter, BLOCK), lambda r: (0, r, 0, 0, 0))],
         out_specs=[pl.BlockSpec((1, 2, levels, BLOCK), lambda r: (r, 0, 0, 0)), bspec, bspec],
         out_shape=[jax.ShapeDtypeStruct((rows, 2, levels, BLOCK), F32), bound, bound],
-        scratch_shapes=[pltpu.VMEM((2, levels, BLOCK), F32)],
+        scratch_shapes=[pltpu.VMEM((levels, 2 * BLOCK), F32)],
         compiler_params=params(12),
         cost_estimate=COST,
         name="edges",
@@ -443,12 +456,12 @@
     shares[...] = acc
 
 
-def piece_spec(pieces):
+def piece_spec(pieces, skip=0):
     many, _, _, quarter, _ = pieces[0].shape[-5:]
     shape = (many, 1, 2, quarter, BLOCK)
     if len(pieces) == 1:
-        return [pl.BlockSpec((4, *shape), lambda r: (0, 0, r, 0, 0, 0))]
-    return [pl.BlockSpec(shape, lambda r: (0, r, 0, 0, 0))] * 4
+        return [pl.BlockSpec((4, *shape), lambda r: (0, 0, skip + r, 0, 0, 0))]
+    return [pl.BlockSpec(shape, lambda r: (0, skip + r, 0, 0, 0))] * 4
 
 
 def row_scratch(levels, half):
@@ -460,8 +473,8 @@
     ]
 
 
-def heat(pieces, bounds, e, rows, row_of, owners, day, exchange, solar, shares, made=()):
-    half, count, _, quarter, _ = pieces[0].shape[-5:]
+def heat(pieces, count, bounds, e, rows, row_of, owners, day, exchange, solar, shares, made=()):
+    half, _, _, quarter, _ = pieces[0].shape[-5:]
     levels = 4 * quarter
     width = 2 * BLOCK
     whole = pl.BlockSpec((1, BLOCK), lambda r: (0, 0))
@@ -498,22 +511,24 @@
     )(*bounds, owners, day, e, exchange, solar, shares, *made, *pieces)
 
 
-def remap_kernel(lo_ref, n_ref, e_ref, base, *rest):
+def remap_kernel(row_of, lo_ref, n_ref, e_ref, base, *rest):
     *pieces, out, edge, cols, back = rest
-    r = pl.program_id(0)
+    r = row_of(pl.program_id(0))
     remap_row(lo_ref[r, 0, 0], n_ref[r, 0, 0], e_ref, pieces, edge, cols, back, out)
 
 
-def remap(pieces, bounds, e, base):
-    half, rows, _, quarter, _ = pieces[0].shape[-5:]
+def remap(pieces, skip, count, row_of, bounds, e, base):
+    half, _, _, quarter, _ = pieces[0].shape[-5:]
     levels = 4 * quarter
     width = 2 * BLOCK
     return pl.pallas_call(
-        remap_kernel,
-        grid=(rows,),
-        in_specs=[SMEM] * 2 + [pl.BlockSpec((1, 2, levels, BLOCK), lambda r: (r, 0, 0, 0)), ANY] + piece_spec(pieces),
-        out_specs=pl.BlockSpec((half, 1, levels, width), lambda r: (1, r, 0, 0)),
-        out_shape=jax.ShapeDtypeStruct((2 * half, rows, levels, width), F32),
+        functools.partial(remap_kernel, row_of),
+        grid=(count,),
+        in_specs=[SMEM] * 2
+        + [pl.BlockSpec((1, 2, levels, BLOCK), lambda r: (row_of(r), 0, 0, 0)), ANY]
+        + piece_spec(pieces, skip),
+        out_specs=pl.BlockSpec((half, 1, levels, width), lambda r: (1, row_of(r), 0, 0)),
+        out_shape=jax.ShapeDtypeStruct(base.shape, F32),
         input_output_aliases={3: 0},
         scratch_shapes=row_scratch(levels, half),
         compiler_params=params(12),
@@ -533,21 +548,22 @@
 
     fields, thickness, courant_lon, courant_lat = hbm([fields, thickness, courant_lon, courant_lat])
     thick = spread(thickness)
-    head, tail, *inside = inner(fields, courant_lon, courant_lat, *hbm([thick]))
+    head, tail, *inside = inner(fields, courant_lon, courant_lat, *hbm([thick]), EARLY)
     e, *bounds = edges(regroup(thick))
     prev = lax.ppermute(tail, "lat", [(i, i + 1) for i in range(ends)])
     nxt = lax.ppermute(head, "lat", [(i + 1, i) for i in range(ends)])
     inside = around(inside)
     head, tail = hbm([head, tail])
-    outside = [regroup(outer(head, tail, fields, courant_lon, courant_lat, prev, nxt, bounds[0]))]
-    second = around(advect(1, fields, courant_lon, courant_lat, prev, nxt))
+    outside = [regroup(outer(fields, courant_lon, courant_lat, head, tail, prev, nxt, bounds[0]))]
+    second = around(advect(fields, courant_lon, courant_lat, prev, nxt, EARLY))
 
     other = (owners[:, 0], daylight, exchange, solar_profile[:, None])
     shares = jnp.zeros((1, BLOCK), F32)
-    remapped, heating, shares = heat(inside, bounds, e, rows, lambda r: r + 1, *other, shares)
+    remapped, heating, shares = heat(inside, rows - 2, bounds, e, rows, lambda r: r + 1, *other, shares)
     made = (remapped, heating)
-    remapped, heating, shares = heat(outside, bounds, e, rows, lambda r: r * (rows - 1), *other, shares, made)
-    remapped = remap(second, bounds, e, remapped)
+    remapped, heating, shares = heat(outside, 2, bounds, e, rows, lambda r: r * (rows - 1), *other, shares, made)
+    later = lambda r: r + EARLY * jnp.minimum(r, 1)
+    remapped = remap(second, 0, rows - EARLY, later, bounds, e, remapped)
     shares = shares[0, :count].reshape(count, 1, 1)
     owner_heat = jnp.sum(lax.all_to_all(shares, "lat", split_axis=0, concat_axis=0, tiled=True)).reshape(1, 1)
     return (remapped, heating, owner_heat)

time: 80.4 us -> 80.5 us (level)
  the two profiles are of different devices: /device:TPU:1 before, /device:TPU:45 now
where the time goes in v5:
time: 80.5 us; the launch traced here: 79.7 us
  Pallas kernels  41.4 us (51%)
  starting transfers between devices  31.6 us (39%)
  waiting for transfers between devices  4.42 us (5%)
  local copies, waits for them, and re-layouts  0.83 us (1%)
    pallas_call x2, Pallas kernels, heat(): pl.pallas_call(functools.partial(heat_kernel, row_of, len(made)), grid=(c...  14.4 us
    pallas_call x1, Pallas kernels, remap(): pl.pallas_call(functools.partial(remap_kernel, row_of), grid=(count,), in...  10.4 us
    all_to_all x2, starting transfers between devices, per_device(): lax.all_to_all(x, 'lev', split_axis=0, concat_axis=0, tiled=True)  8.73 us
    all_to_all x1, starting transfers between devices, per_device(): lax.all_to_all(shares, 'lat', split_axis=0, concat_axis=0, tiled=True)  8.4 us
    ppermute x6, starting transfers between devices, per_device(): lax.ppermute(p, 'lev', turn(s + 1))  7.86 us
    ppermute x1, starting transfers between devices, per_device(): prev = lax.ppermute(tail, 'lat', [(i, i + 1) for i in range(ends)])  4.67 us
    pallas_call x1, Pallas kernels, inner(): pl.pallas_call(inner_kernel, in_specs=[ANY] * 4, out_specs=[ANY] * 6, out...  4.48 us
    pallas_call x1, Pallas kernels, advect(): pl.pallas_call(advect_kernel, in_specs=[ANY] * 5, out_specs=[ANY] * 4, ou...  4.25 us
  transfers between devices with their start and end apart: 11, of which 2 were waited for; matrix products, arithmetic and copies ran while one was open for 1% of the time, Pallas kernels for 49%

profile of v5, /device:TPU:45, one launch (start us, length us, event | category | flops | bytes accessed | tf_op | source)
XLA Modules:
  0.0 79.7 jit_solution(2696188570775863726)
XLA Ops:
  0.6 2.2 %spread.1.after = f32[4,8,2,32,128]{4,3,2,1,0:T(8,128)} custom-call(f32[8,32,1024]{2,1,0:T(8,128)} %thick.1), custom_call_target="tpu_custom_call" | custom-call | flops 1 | bytes 1 | tf_op jit(solution)/shard_map/spread/pallas_call | solution.py:88
  2.8 4.4 %all-to-all-start = ((f32[4,8,2,32,128]{4,3,2,1,0:T(8,128)}), f32[4,8,2,32,128]{4,3,2,1,0:T(8,128)S(1)}, u32[]{:S(2)}, u32[]{:S(2)}) async-start(f32[4,8,2,32,128]{4,3,2,1,0:T(8,128)} %spread.1.after), calls=%async_computation | async-start | bytes 2097152 | tf_op jit(solution)/shard_map/all_to_all | solution.py:547
  7.2 4.5 %inner.1 = (f32[4,32,1024]{2,1,0:T(8,128)}, f32[4,32,1024]{2,1,0:T(8,128)}, f32[2,6,2,32,128]{4,3,2,1,0:T(8,128)}, f32[2,6,2,32,128]{4,3,2,1,0:T(8,128)}, f32[2,...) custom-call(f32[4,8,32,1024]{3,2,1,0:T(8,128)} %fields.5, f32[8,32,1024]{2,1,0:T(8,128)} %c_lon.5, ...), custom_call_target="tpu_custom_call" | custom-call | flops 1 | bytes 1 | tf_op jit(solution)/shard_map/inner/pallas_call | solution.py:154
  11.7 4.7 %collective-permute-start.3 = (f32[4,32,1024]{2,1,0:T(8,128)}, f32[4,32,1024]{2,1,0:T(8,128)S(1)}, u32[]{:S(2)}, u32[]{:S(2)}) collective-permute-start(f32[4,32,1024]{2,1,0:T(8,128)} %get-tuple-element.33.tail), channel_id=1, source_target_pairs={{0,4},{4,8},{8,12},{12,16},{16,20},{20,24},{24,28},{28,32},{32,36}... | collective-permute-start | bytes 1572872 | tf_op jit(solution)/shard_map/ppermute | solution.py:553
  16.4 1.9 %collective-permute-start.4 = (f32[4,32,1024]{2,1,0:T(8,128)}, f32[4,32,1024]{2,1,0:T(8,128)S(1)}, u32[]{:S(2)}, u32[]{:S(2)}) collective-permute-start(f32[4,32,1024]{2,1,0:T(8,128)} %get-tuple-element.32.head), channel_id=1, source_target_pairs={{4,0},{8,4},{12,8},{16,12},{20,16},{24,20},{28,24},{32,28},{36,32}... | collective-permute-start | bytes 1572872 | tf_op jit(solution)/shard_map/ppermute | solution.py:554
  18.3 1.2 %collective-permute-start = (f32[2,6,2,32,128]{4,3,2,1,0:T(8,128)}, f32[2,6,2,32,128]{4,3,2,1,0:T(8,128)}, u32[]{:S(2)}, u32[]{:S(2)}) collective-permute-start(f32[2,6,2,32,128]{4,3,2,1,0:T(8,128)} %get-tuple-element.26), channel_id=1, source_target_pairs={{0,1},{1,2},{2,3},{3,0},{4,5},{5,6},{6,7},{7,4},{8,9},{9,10},{10,1... | collective-permute-start | bytes 1179656 | tf_op jit(solution)/shard_map/ppermute | solution.py:546
  19.5 0.7 collective-permute-start.1
  20.3 2.0 %collective-permute-start.2 = (f32[2,6,2,32,128]{4,3,2,1,0:T(8,128)}, f32[2,6,2,32,128]{4,3,2,1,0:T(8,128)}, u32[]{:S(2)}, u32[]{:S(2)}) collective-permute-start(f32[2,6,2,32,128]{4,3,2,1,0:T(8,128)} %get-tuple-element.28), channel_id=1, source_target_pairs={{0,3},{1,0},{2,1},{3,2},{4,7},{5,4},{6,5},{7,6},{8,11},{9,8},{10,9... | collective-permute-start | bytes 1179656 | tf_op jit(solution)/shard_map/ppermute | solution.py:546
  22.2 0.0 all-to-all-done.thick
  22.2 2.7 %edges.1 = (f32[8,2,128,128]{3,2,1,0:T(8,128)S(1)}, s32[8,1,128]{2,1,0:T(1,128)S(1)}, s32[8,1,128]{2,1,0:T(1,128)S(1)}) custom-call(f32[4,8,2,32,128]{4,3,2,1,0:T(8,128)S(1)} %all-to-all-done.thick), custom_call_target="tpu_custom_call" | custom-call | flops 1 | bytes 1 | tf_op jit(solution)/shard_map/edges/pallas_call | solution.py:404
  25.0 0.0 collective-permute-done.3.prev
  25.0 2.5 %collective-permute-done.4.nxt = f32[4,32,1024]{2,1,0:T(8,128)S(1)} collective-permute-done((f32[4,32,1024]{2,1,0:T(8,128)}, f32[4,32,1024]{2,1,0:T(8,128)S(1)}, u32[]{:S(2)}, u32[]{:S(2)}) %collective-permute-start.4) | collective-permute-done | bytes 524320 | tf_op jit(solution)/shard_map/ppermute | solution.py:554
  27.5 2.9 %outer.1 = f32[4,2,2,2,32,128]{5,4,3,2,1,0:T(8,128)} custom-call(f32[4,8,32,1024]{3,2,1,0:T(8,128)} %fields.5, f32[8,32,1024]{2,1,0:T(8,128)} %c_lon.5, f32[8,32,1024]{2,1,0:T(8,128)} %c_lat.5, f32[4,32,1024]{2,1,0:T(8,128)} %get-tuple-element.32.head, f32[4,32,1024]{2,1,0:T(8,128)} %get-tuple-element.33.tail, ...), custom_call_target="tpu_custom_call" | custom-call | flops 1 | bytes 1 | tf_op jit(solution)/shard_map/outer/pallas_call | solution.py:207
  30.4 0.0 copy-start.3
  30.4 0.0 copy-start
  30.5 0.0 copy-start.1
  30.5 0.0 copy-start.2
  30.5 4.4 %all-to-all-start.1 = ((f32[4,2,2,2,32,128]{5,4,3,2,1,0:T(8,128)}), f32[4,2,2,2,32,128]{5,4,3,2,1,0:T(8,128)S(1)}, u32[]{:S(2)}, u32[]{:S(2)}) async-start(f32[4,2,2,2,32,128]{5,4,3,2,1,0:T(8,128)} %outer.1), calls=%async_computation.1 | async-start | bytes 1048576 | tf_op jit(solution)/shard_map/all_to_all | solution.py:547
  34.9 4.3 %advect.1 = (f32[2,8,2,32,128]{4,3,2,1,0:T(8,128)}, f32[2,8,2,32,128]{4,3,2,1,0:T(8,128)}, f32[2,8,2,32,128]{4,3,2,1,0:T(8,128)}, f32[2,8,2,32,128]{4,3,2,1,0:T(8,128)}) custom-call(f32[4,8,32,1024]{3,2,1,0:T(8,128)} %fields.5, f32[8,32,1024]{2,1,0:T(8,128)} %c_lon.5, f32[8,32,1024]{2,1,0:T(8,128)} %c_lat.5, f32[4,32,1024]{2,1,0:T(8,128)S(1)} %collective-permute-done.3.prev, ...), custom_call_target="tpu_custom_call" | custom-call | flops 1 | bytes 1 | tf_op jit(solution)/shard_map/advect/pallas_call | solution.py:277
  39.1 1.2 %collective-permute-start.5 = (f32[2,8,2,32,128]{4,3,2,1,0:T(8,128)}, f32[2,8,2,32,128]{4,3,2,1,0:T(8,128)S(1)}, u32[]{:S(2)}, u32[]{:S(2)}) collective-permute-start(f32[2,8,2,32,128]{4,3,2,1,0:T(8,128)} %get-tuple-element.36), channel_id=1, source_target_pairs={{0,1},{1,2},{2,3},{3,0},{4,5},{5,6},{6,7},{7,4},{8,9},{9,10},{10,1... | collective-permute-start | bytes 1572872 | tf_op jit(solution)/shard_map/ppermute | solution.py:546
  40.4 0.7 collective-permute-start.6
  41.1 0.0 collective-permute-done.rest_1_
  41.1 2.0 %collective-permute-start.7 = (f32[2,8,2,32,128]{4,3,2,1,0:T(8,128)}, f32[2,8,2,32,128]{4,3,2,1,0:T(8,128)S(1)}, u32[]{:S(2)}, u32[]{:S(2)}) collective-permute-start(f32[2,8,2,32,128]{4,3,2,1,0:T(8,128)} %get-tuple-element.38), channel_id=1, source_target_pairs={{0,3},{1,0},{2,1},{3,2},{4,7},{5,4},{6,5},{7,6},{8,11},{9,8},{10,9... | collective-permute-start | bytes 1572872 | tf_op jit(solution)/shard_map/ppermute | solution.py:546
  43.0 0.0 copy-done.3
  43.0 0.1 copy.17.solar
  43.2 0.0 collective-permute-done.1.rest_2_
  43.2 0.0 collective-permute-done.2.rest_3_
  43.2 0.0 copy-done
  43.2 0.0 copy-done.1
  43.2 0.0 copy-done.2
  43.2 9.7 %heat.2 = (f32[4,8,128,256]{3,2,1,0:T(8,128)}, f32[8,128,256]{2,1,0:T(8,128)}, f32[1,128]{1,0:T(1,128)S(1)}) custom-call(s32[8,1,128]{2,1,0:T(1,128)S(1)} %get-tuple-element.22.lo_ref.after, s32[8,1,128]{2,1,0:T(1,128)S(1)} %get-tuple-element.23.n_ref, s32[16]{0:T(128)S(1)} %bitcast.5, s32[16]{0:T(128)S(1)} %copy-done.2, ...), custom_call_target="tpu_custom_call" | custom-call | flops 1 | bytes 1 | tf_op jit(solution)/shard_map/heat/pallas_call | solution.py:481
  53.0 0.0 all-to-all-done.1.rest_2_
  53.0 4.6 %heat.3 = (f32[4,8,128,256]{3,2,1,0:T(8,128)}, f32[8,128,256]{2,1,0:T(8,128)}, f32[1,128]{1,0:T(1,128)S(1)}) custom-call(s32[8,1,128]{2,1,0:T(1,128)S(1)} %get-tuple-element.22.lo_ref.after, s32[8,1,128]{2,1,0:T(1,128)S(1)} %get-tuple-element.23.n_ref, s32[16]{0:T(128)S(1)} %bitcast.6, ...), custom_call_target="tpu_custom_call", output_to_operand_aliasing={{0}: (8, {}), {1}: (9, {})} | custom-call | flops 1 | bytes 1 | tf_op jit(solution)/shard_map/heat/pallas_call | solution.py:481
  57.6 0.7 copy.18
  58.3 8.4 %all-to-all-start.2 = ((f32[32,1,1]{2,1,0:T(1,128)}), f32[32,1,1]{2,1,0:T(1,128)S(1)}, u32[]{:S(2)}, u32[]{:S(2)}) async-start(f32[32,1,1]{2,1,0:T(1,128)} %copy.18), calls=%async_computation.2 | async-start | bytes 32768 | tf_op jit(solution)/shard_map/all_to_all | solution.py:568
  66.7 0.0 collective-permute-done.5.rest_1_
  66.7 0.0 collective-permute-done.6.rest_2_
  66.7 1.9 %collective-permute-done.7.rest_3_ = f32[2,8,2,32,128]{4,3,2,1,0:T(8,128)S(1)} collective-permute-done((f32[2,8,2,32,128]{4,3,2,1,0:T(8,128)}, f32[2,8,2,32,128]{4,3,2,1,0:T(8,128)S(1)}, u32[]{:S(2)}, u32[]{:S(2)}) %collective-permute-start.7) | collective-permute-done | bytes 524320 | tf_op jit(solution)/shard_map/ppermute | solution.py:546
  68.6 10.4 %remap.1 = f32[4,8,128,256]{3,2,1,0:T(8,128)} custom-call(s32[8,1,128]{2,1,0:T(1,128)S(1)} %get-tuple-element.22.lo_ref.after, s32[8,1,128]{2,1,0:T(1,128)S(1)} %get-tuple-element.23.n_ref, f32[8,2,128,128]{3,2,1,0:T(8,128)S(1)} %get-tuple-element.24.e_ref, f32[4,8,128,256]{3,2,1,0:T(8,128)} %get-tuple-element.34.base, ...), custom_call_target="tpu_custom_call", output_to_operand_aliasing={{}: (3, {})} | custom-call | flops 1 | bytes 1 | tf_op jit(solution)/shard_map/remap/pallas_call | solution.py:524
  79.0 0.0 all-to-all-done.2
  79.0 0.6 reduce_sum.9
  (2 shorter events, 0.0 us)
Async XLA Ops:
  2.8 19.4 %all-to-all-start = ((f32[4,8,2,32,128]{4,3,2,1,0:T(8,128)}), f32[4,8,2,32,128]{4,3,2,1,0:T(8,128)S(1)}, u32[]{:S(2)}, u32[]{:S(2)}) async-start(f32[4,8,2,32,128]{4,3,2,1,0:T(8,128)} %spread.1.after), calls=%async_computation | async-start | bytes 2097152 | tf_op jit(solution)/shard_map/all_to_all | solution.py:547
  11.7 13.3 %collective-permute-start.3 = (f32[4,32,1024]{2,1,0:T(8,128)}, f32[4,32,1024]{2,1,0:T(8,128)S(1)}, u32[]{:S(2)}, u32[]{:S(2)}) collective-permute-start(f32[4,32,1024]{2,1,0:T(8,128)} %get-tuple-element.33.tail), channel_id=1, source_target_pairs={{0,4},{4,8},{8,12},{12,16},{16,20},{20,24},{24,28},{28,32},{32,36}... | collective-permute-start | bytes 1572872 | tf_op jit(solution)/shard_map/ppermute | solution.py:553
  16.4 11.1 %collective-permute-start.4 = (f32[4,32,1024]{2,1,0:T(8,128)}, f32[4,32,1024]{2,1,0:T(8,128)S(1)}, u32[]{:S(2)}, u32[]{:S(2)}) collective-permute-start(f32[4,32,1024]{2,1,0:T(8,128)} %get-tuple-element.32.head), channel_id=1, source_target_pairs={{4,0},{8,4},{12,8},{16,12},{20,16},{24,20},{28,24},{32,28},{36,32}... | collective-permute-start | bytes 1572872 | tf_op jit(solution)/shard_map/ppermute | solution.py:554
  18.3 22.8 %collective-permute-start = (f32[2,6,2,32,128]{4,3,2,1,0:T(8,128)}, f32[2,6,2,32,128]{4,3,2,1,0:T(8,128)}, u32[]{:S(2)}, u32[]{:S(2)}) collective-permute-start(f32[2,6,2,32,128]{4,3,2,1,0:T(8,128)} %get-tuple-element.26), channel_id=1, source_target_pairs={{0,1},{1,2},{2,3},{3,0},{4,5},{5,6},{6,7},{7,4},{8,9},{9,10},{10,1... | collective-permute-start | bytes 1179656 | tf_op jit(solution)/shard_map/ppermute | solution.py:546
  19.5 23.6 %collective-permute-start.1 = (f32[2,6,2,32,128]{4,3,2,1,0:T(8,128)}, f32[2,6,2,32,128]{4,3,2,1,0:T(8,128)}, u32[]{:S(2)}, u32[]{:S(2)}) collective-permute-start(f32[2,6,2,32,128]{4,3,2,1,0:T(8,128)} %get-tuple-element.27), channel_id=1, source_target_pairs={{0,2},{1,3},{2,0},{3,1},{4,6},{5,7},{6,4},{7,5},{8,10},{9,11},{10,... | collective-permute-start | bytes 1179656 | tf_op jit(solution)/shard_map/ppermute | solution.py:546
  20.3 22.9 %collective-permute-start.2 = (f32[2,6,2,32,128]{4,3,2,1,0:T(8,128)}, f32[2,6,2,32,128]{4,3,2,1,0:T(8,128)}, u32[]{:S(2)}, u32[]{:S(2)}) collective-permute-start(f32[2,6,2,32,128]{4,3,2,1,0:T(8,128)} %get-tuple-element.28), channel_id=1, source_target_pairs={{0,3},{1,0},{2,1},{3,2},{4,7},{5,4},{6,5},{7,6},{8,11},{9,8},{10,9... | collective-permute-start | bytes 1179656 | tf_op jit(solution)/shard_map/ppermute | solution.py:546
  30.4 12.6 %copy-start.3 = (f32[128]{0:T(128)S(1)}, f32[128]{0:T(128)}, u32[]{:S(2)}) copy-start(f32[128]{0:T(128)} %param.13) | copy-start | bytes 1540
  30.4 12.7 %copy-start = (f32[2,128,128]{2,1,0:T(8,128)S(1)}, f32[2,128,128]{2,1,0:T(8,128)}, u32[]{:S(2)}) copy-start(f32[2,128,128]{2,1,0:T(8,128)} %exch.3) | copy-start | bytes 393220
  30.5 12.7 %copy-start.1 = (s32[16,1]{0,1:T(1,128)S(1)}, s32[16,1]{0,1:T(1,128)}, u32[]{:S(2)}) copy-start(s32[16,1]{0,1:T(1,128)} %param.14) | copy-start | bytes 196
  30.5 12.7 %copy-start.2 = (s32[16]{0:T(128)S(1)}, s32[16]{0:T(128)}, u32[]{:S(2)}) copy-start(s32[16]{0:T(128)} %day_ref.3) | copy-start | bytes 196
  30.5 22.5 %all-to-all-start.1 = ((f32[4,2,2,2,32,128]{5,4,3,2,1,0:T(8,128)}), f32[4,2,2,2,32,128]{5,4,3,2,1,0:T(8,128)S(1)}, u32[]{:S(2)}, u32[]{:S(2)}) async-start(f32[4,2,2,2,32,128]{5,4,3,2,1,0:T(8,128)} %outer.1), calls=%async_computation.1 | async-start | bytes 1048576 | tf_op jit(solution)/shard_map/all_to_all | solution.py:547
  39.1 27.6 %collective-permute-start.5 = (f32[2,8,2,32,128]{4,3,2,1,0:T(8,128)}, f32[2,8,2,32,128]{4,3,2,1,0:T(8,128)S(1)}, u32[]{:S(2)}, u32[]{:S(2)}) collective-permute-start(f32[2,8,2,32,128]{4,3,2,1,0:T(8,128)} %get-tuple-element.36), channel_id=1, source_target_pairs={{0,1},{1,2},{2,3},{3,0},{4,5},{5,6},{6,7},{7,4},{8,9},{9,10},{10,1... | collective-permute-start | bytes 1572872 | tf_op jit(solution)/shard_map/ppermute | solution.py:546
  40.4 26.4 %collective-permute-start.6 = (f32[2,8,2,32,128]{4,3,2,1,0:T(8,128)}, f32[2,8,2,32,128]{4,3,2,1,0:T(8,128)S(1)}, u32[]{:S(2)}, u32[]{:S(2)}) collective-permute-start(f32[2,8,2,32,128]{4,3,2,1,0:T(8,128)} %get-tuple-element.37), channel_id=1, source_target_pairs={{0,2},{1,3},{2,0},{3,1},{4,6},{5,7},{6,4},{7,5},{8,10},{9,11},{10,... | collective-permute-start | bytes 1572872 | tf_op jit(solution)/shard_map/ppermute | solution.py:546
  41.1 27.6 %collective-permute-start.7 = (f32[2,8,2,32,128]{4,3,2,1,0:T(8,128)}, f32[2,8,2,32,128]{4,3,2,1,0:T(8,128)S(1)}, u32[]{:S(2)}, u32[]{:S(2)}) collective-permute-start(f32[2,8,2,32,128]{4,3,2,1,0:T(8,128)} %get-tuple-element.38), channel_id=1, source_target_pairs={{0,3},{1,0},{2,1},{3,2},{4,7},{5,4},{6,5},{7,6},{8,11},{9,8},{10,9... | collective-permute-start | bytes 1572872 | tf_op jit(solution)/shard_map/ppermute | solution.py:546
  58.3 20.7 %all-to-all-start.2 = ((f32[32,1,1]{2,1,0:T(1,128)}), f32[32,1,1]{2,1,0:T(1,128)S(1)}, u32[]{:S(2)}, u32[]{:S(2)}) async-start(f32[32,1,1]{2,1,0:T(1,128)} %copy.18), calls=%async_computation.2 | async-start | bytes 32768 | tf_op jit(solution)/shard_map/all_to_all | solution.py:568

commit v6 on v5

--- a/solution.py
+++ b/solution.py
@@ -448,12 +448,9 @@
     heat = heat + (day * solar[...]) * clear
     heating[0] = heat
     total = jnp.sum(heat, axis=0, keepdims=True)
-    line = lax.broadcasted_iota(jnp.int32, (1, BLOCK), 1)
-    acc = shares[...]
     for b in range(2):
-        mean = jnp.sum(total[:, b * BLOCK : (b + 1) * BLOCK], axis=1, keepdims=True) * (1.0 / (levels * BLOCK))
-        acc = acc + jnp.where(line == own_ref[2 * r + b], mean, 0.0)
-    shares[...] = acc
+        own = own_ref[2 * r + b]
+        shares[own] = shares[own] + total[:, b * BLOCK : (b + 1) * BLOCK] * (1.0 / (levels * BLOCK))
 
 
 def piece_spec(pieces, skip=0):
@@ -477,7 +474,7 @@
     half, _, _, quarter, _ = pieces[0].shape[-5:]
     levels = 4 * quarter
     width = 2 * BLOCK
-    whole = pl.BlockSpec((1, BLOCK), lambda r: (0, 0))
+    whole = pl.BlockSpec(shares.shape, lambda r: (0, 0, 0))
     return pl.pallas_call(
         functools.partial(heat_kernel, row_of, len(made)),
         grid=(count,),
@@ -501,7 +498,7 @@
         out_shape=[
             jax.ShapeDtypeStruct((2 * half, rows, levels, width), F32),
             jax.ShapeDtypeStruct((rows, levels, width), F32),
-            jax.ShapeDtypeStruct((1, BLOCK), F32),
+            jax.ShapeDtypeStruct(shares.shape, F32),
         ],
         input_output_aliases={8: 0, 9: 1} if made else {},
         scratch_shapes=row_scratch(levels, half) + [pltpu.VMEM((2, levels, 2 * levels), jnp.bfloat16)],
@@ -558,13 +555,12 @@
     second = around(advect(fields, courant_lon, courant_lat, prev, nxt, EARLY))
 
     other = (owners[:, 0], daylight, exchange, solar_profile[:, None])
-    shares = jnp.zeros((1, BLOCK), F32)
+    shares = jnp.zeros((count, 1, BLOCK), F32)
     remapped, heating, shares = heat(inside, rows - 2, bounds, e, rows, lambda r: r + 1, *other, shares)
     made = (remapped, heating)
     remapped, heating, shares = heat(outside, 2, bounds, e, rows, lambda r: r * (rows - 1), *other, shares, made)
     later = lambda r: r + EARLY * jnp.minimum(r, 1)
     remapped = remap(second, 0, rows - EARLY, later, bounds, e, remapped)
-    shares = shares[0, :count].reshape(count, 1, 1)
     owner_heat = jnp.sum(lax.all_to_all(shares, "lat", split_axis=0, concat_axis=0, tiled=True)).reshape(1, 1)
     return (remapped, heating, owner_heat)
 

time: 80.5 us -> 109 us (1.35)
  the two profiles are of different devices: /device:TPU:45 before, /device:TPU:1 now
where the time goes in v6:
time: 109 us; the launch traced here: 108 us
  Pallas kernels  38.6 us (35%)
  starting transfers between devices  37 us (34%)
  waiting for transfers between devices  30.4 us (28%)
    ppermute x6, waiting for transfers between devices, per_device(): lax.ppermute(p, 'lev', turn(s + 1))  23.1 us
    pallas_call x2, Pallas kernels, heat(): pl.pallas_call(functools.partial(heat_kernel, row_of, len(made)), grid=(c...  12.6 us
    all_to_all x1, starting transfers between devices, per_device(): lax.all_to_all(shares, 'lat', split_axis=0, concat_axis=0, tiled=True)  12.3 us
    ppermute x6, starting transfers between devices, per_device(): lax.ppermute(p, 'lev', turn(s + 1))  9.89 us
    pallas_call x1, Pallas kernels, remap(): pl.pallas_call(functools.partial(remap_kernel, row_of), grid=(count,), in...  9.29 us
    all_to_all x2, starting transfers between devices, per_device(): lax.all_to_all(x, 'lev', split_axis=0, concat_axis=0, tiled=True)  8.51 us
    ppermute x1, waiting for transfers between devices, per_device(): nxt = lax.ppermute(head, 'lat', [(i + 1, i) for i in range(ends)])  4.58 us
    pallas_call x1, Pallas kernels, inner(): pl.pallas_call(inner_kernel, in_specs=[ANY] * 4, out_specs=[ANY] * 6, out...  4.45 us
  transfers between devices with their start and end apart: 11, of which 4 were waited for; matrix products, arithmetic and copies ran while one was open for 0% of the time, Pallas kernels for 34%

profile of v6, /device:TPU:1, one launch (start us, length us, event | category | flops | bytes accessed | tf_op | source)
XLA Modules:
  0.0 107.6 jit_solution(2968018801596812313)
XLA Ops:
  0.6 2.2 %spread.1.after = f32[4,8,2,32,128]{4,3,2,1,0:T(8,128)} custom-call(f32[8,32,1024]{2,1,0:T(8,128)} %thick.1), custom_call_target="tpu_custom_call" | custom-call | flops 1 | bytes 1 | tf_op jit(solution)/shard_map/spread/pallas_call | solution.py:88
  2.8 5.0 %all-to-all-start = ((f32[4,8,2,32,128]{4,3,2,1,0:T(8,128)}), f32[4,8,2,32,128]{4,3,2,1,0:T(8,128)S(1)}, u32[]{:S(2)}, u32[]{:S(2)}) async-start(f32[4,8,2,32,128]{4,3,2,1,0:T(8,128)} %spread.1.after), calls=%async_computation | async-start | bytes 2097152 | tf_op jit(solution)/shard_map/all_to_all | solution.py:544
  7.9 4.5 %inner.1 = (f32[4,32,1024]{2,1,0:T(8,128)}, f32[4,32,1024]{2,1,0:T(8,128)}, f32[2,6,2,32,128]{4,3,2,1,0:T(8,128)}, f32[2,6,2,32,128]{4,3,2,1,0:T(8,128)}, f32[2,...) custom-call(f32[4,8,32,1024]{3,2,1,0:T(8,128)} %fields.5, f32[8,32,1024]{2,1,0:T(8,128)} %c_lon.5, ...), custom_call_target="tpu_custom_call" | custom-call | flops 1 | bytes 1 | tf_op jit(solution)/shard_map/inner/pallas_call | solution.py:154
  12.3 4.4 %collective-permute-start.3 = (f32[4,32,1024]{2,1,0:T(8,128)}, f32[4,32,1024]{2,1,0:T(8,128)S(1)}, u32[]{:S(2)}, u32[]{:S(2)}) collective-permute-start(f32[4,32,1024]{2,1,0:T(8,128)} %get-tuple-element.33.tail), channel_id=1, source_target_pairs={{0,4},{4,8},{8,12},{12,16},{16,20},{20,24},{24,28},{28,32},{32,36}... | collective-permute-start | bytes 1572872 | tf_op jit(solution)/shard_map/ppermute | solution.py:550
  16.7 1.9 %collective-permute-start.4 = (f32[4,32,1024]{2,1,0:T(8,128)}, f32[4,32,1024]{2,1,0:T(8,128)S(1)}, u32[]{:S(2)}, u32[]{:S(2)}) collective-permute-start(f32[4,32,1024]{2,1,0:T(8,128)} %get-tuple-element.32.head), channel_id=1, source_target_pairs={{4,0},{8,4},{12,8},{16,12},{20,16},{24,20},{28,24},{32,28},{36,32}... | collective-permute-start | bytes 1572872 | tf_op jit(solution)/shard_map/ppermute | solution.py:551
  18.7 1.8 %collective-permute-start = (f32[2,6,2,32,128]{4,3,2,1,0:T(8,128)}, f32[2,6,2,32,128]{4,3,2,1,0:T(8,128)S(1)}, u32[]{:S(2)}, u32[]{:S(2)}) collective-permute-start(f32[2,6,2,32,128]{4,3,2,1,0:T(8,128)} %get-tuple-element.26), channel_id=1, source_target_pairs={{0,1},{1,2},{2,3},{3,0},{4,5},{5,6},{6,7},{7,4},{8,9},{9,10},{10,1... | collective-permute-start | bytes 1179656 | tf_op jit(solution)/shard_map/ppermute | solution.py:543
  20.5 2.7 %collective-permute-done.3.prev = f32[4,32,1024]{2,1,0:T(8,128)S(1)} collective-permute-done((f32[4,32,1024]{2,1,0:T(8,128)}, f32[4,32,1024]{2,1,0:T(8,128)S(1)}, u32[]{:S(2)}, u32[]{:S(2)}) %collective-permute-start.3) | collective-permute-done | bytes 524320 | tf_op jit(solution)/shard_map/ppermute | solution.py:550
  23.1 4.6 %collective-permute-done.4.nxt = f32[4,32,1024]{2,1,0:T(8,128)S(1)} collective-permute-done((f32[4,32,1024]{2,1,0:T(8,128)}, f32[4,32,1024]{2,1,0:T(8,128)S(1)}, u32[]{:S(2)}, u32[]{:S(2)}) %collective-permute-start.4) | collective-permute-done | bytes 524320 | tf_op jit(solution)/shard_map/ppermute | solution.py:551
  27.7 4.3 %advect.1 = (f32[2,8,2,32,128]{4,3,2,1,0:T(8,128)}, f32[2,8,2,32,128]{4,3,2,1,0:T(8,128)}, f32[2,8,2,32,128]{4,3,2,1,0:T(8,128)}, f32[2,8,2,32,128]{4,3,2,1,0:T(8,128)}) custom-call(f32[4,8,32,1024]{3,2,1,0:T(8,128)} %fields.5, f32[8,32,1024]{2,1,0:T(8,128)} %c_lon.5, f32[8,32,1024]{2,1,0:T(8,128)} %c_lat.5, f32[4,32,1024]{2,1,0:T(8,128)S(1)} %collective-permute-done.3.prev, ...), custom_call_target="tpu_custom_call" | custom-call | flops 1 | bytes 1 | tf_op jit(solution)/shard_map/advect/pallas_call | solution.py:277
  32.0 1.5 %collective-permute-start.5 = (f32[2,8,2,32,128]{4,3,2,1,0:T(8,128)}, f32[2,8,2,32,128]{4,3,2,1,0:T(8,128)}, u32[]{:S(2)}, u32[]{:S(2)}) collective-permute-start(f32[2,8,2,32,128]{4,3,2,1,0:T(8,128)} %get-tuple-element.36), channel_id=1, source_target_pairs={{0,1},{1,2},{2,3},{3,0},{4,5},{5,6},{6,7},{7,4},{8,9},{9,10},{10,1... | collective-permute-start | bytes 1572872 | tf_op jit(solution)/shard_map/ppermute | solution.py:543
  33.5 2.7 %collective-permute-start.6 = (f32[2,8,2,32,128]{4,3,2,1,0:T(8,128)}, f32[2,8,2,32,128]{4,3,2,1,0:T(8,128)}, u32[]{:S(2)}, u32[]{:S(2)}) collective-permute-start(f32[2,8,2,32,128]{4,3,2,1,0:T(8,128)} %get-tuple-element.37), channel_id=1, source_target_pairs={{0,2},{1,3},{2,0},{3,1},{4,6},{5,7},{6,4},{7,5},{8,10},{9,11},{10,... | collective-permute-start | bytes 1572872 | tf_op jit(solution)/shard_map/ppermute | solution.py:543
  36.2 1.2 %collective-permute-start.7 = (f32[2,8,2,32,128]{4,3,2,1,0:T(8,128)}, f32[2,8,2,32,128]{4,3,2,1,0:T(8,128)}, u32[]{:S(2)}, u32[]{:S(2)}) collective-permute-start(f32[2,8,2,32,128]{4,3,2,1,0:T(8,128)} %get-tuple-element.38), channel_id=1, source_target_pairs={{0,3},{1,0},{2,1},{3,2},{4,7},{5,4},{6,5},{7,6},{8,11},{9,8},{10,9... | collective-permute-start | bytes 1572872 | tf_op jit(solution)/shard_map/ppermute | solution.py:543
  37.4 0.1 collective-permute-start.1
  37.5 0.0 collective-permute-done.rest_1_
  37.5 2.6 %collective-permute-start.2 = (f32[2,6,2,32,128]{4,3,2,1,0:T(8,128)}, f32[2,6,2,32,128]{4,3,2,1,0:T(8,128)}, u32[]{:S(2)}, u32[]{:S(2)}) collective-permute-start(f32[2,6,2,32,128]{4,3,2,1,0:T(8,128)} %get-tuple-element.28), channel_id=1, source_target_pairs={{0,3},{1,0},{2,1},{3,2},{4,7},{5,4},{6,5},{7,6},{8,11},{9,8},{10,9... | collective-permute-start | bytes 1179656 | tf_op jit(solution)/shard_map/ppermute | solution.py:543
  40.1 0.0 all-to-all-done.thick
  40.1 2.7 %edges.1 = (f32[8,2,128,128]{3,2,1,0:T(8,128)S(1)}, s32[8,1,128]{2,1,0:T(1,128)S(1)}, s32[8,1,128]{2,1,0:T(1,128)S(1)}) custom-call(f32[4,8,2,32,128]{4,3,2,1,0:T(8,128)S(1)} %all-to-all-done.thick), custom_call_target="tpu_custom_call" | custom-call | flops 1 | bytes 1 | tf_op jit(solution)/shard_map/edges/pallas_call | solution.py:404
  42.8 0.0 copy-start.3
  42.8 0.0 copy-start
  42.9 0.0 copy-start.1
  42.9 0.0 copy-start.2
  42.9 3.1 %outer.1 = f32[4,2,2,2,32,128]{5,4,3,2,1,0:T(8,128)} custom-call(f32[4,8,32,1024]{3,2,1,0:T(8,128)} %fields.5, f32[8,32,1024]{2,1,0:T(8,128)} %c_lon.5, f32[8,32,1024]{2,1,0:T(8,128)} %c_lat.5, f32[4,32,1024]{2,1,0:T(8,128)} %get-tuple-element.32.head, f32[4,32,1024]{2,1,0:T(8,128)} %get-tuple-element.33.tail, ...), custom_call_target="tpu_custom_call" | custom-call | flops 1 | bytes 1 | tf_op jit(solution)/shard_map/outer/pallas_call | solution.py:207
  45.9 3.5 %all-to-all-start.1 = ((f32[4,2,2,2,32,128]{5,4,3,2,1,0:T(8,128)}), f32[4,2,2,2,32,128]{5,4,3,2,1,0:T(8,128)S(1)}, u32[]{:S(2)}, u32[]{:S(2)}) async-start(f32[4,2,2,2,32,128]{5,4,3,2,1,0:T(8,128)} %outer.1), calls=%async_computation.1 | async-start | bytes 1048576 | tf_op jit(solution)/shard_map/all_to_all | solution.py:544
  49.4 0.0 copy-done.3
  49.4 0.1 copy.15.solar
  49.5 16.0 %collective-permute-done.1.rest_2_ = f32[2,6,2,32,128]{4,3,2,1,0:T(8,128)} collective-permute-done((f32[2,6,2,32,128]{4,3,2,1,0:T(8,128)}, f32[2,6,2,32,128]{4,3,2,1,0:T(8,128)}, u32[]{:S(2)}, u32[]{:S(2)}) %collective-permute-start.1) | collective-permute-done | bytes 393248 | tf_op jit(solution)/shard_map/ppermute | solution.py:543
  65.6 7.1 %collective-permute-done.2.rest_3_ = f32[2,6,2,32,128]{4,3,2,1,0:T(8,128)} collective-permute-done((f32[2,6,2,32,128]{4,3,2,1,0:T(8,128)}, f32[2,6,2,32,128]{4,3,2,1,0:T(8,128)}, u32[]{:S(2)}, u32[]{:S(2)}) %collective-permute-start.2) | collective-permute-done | bytes 393248 | tf_op jit(solution)/shard_map/ppermute | solution.py:543
  72.7 0.0 copy-done
  72.7 0.0 copy-done.1
  72.7 0.0 copy-done.2
  72.7 8.8 %heat.2 = (f32[4,8,128,256]{3,2,1,0:T(8,128)}, f32[8,128,256]{2,1,0:T(8,128)}, f32[32,1,128]{2,1,0:T(1,128)S(1)}) custom-call(s32[8,1,128]{2,1,0:T(1,128)S(1)} %get-tuple-element.22.lo_ref.after, s32[8,1,128]{2,1,0:T(1,128)S(1)} %get-tuple-element.23.n_ref, s32[16]{0:T(128)S(1)} %bitcast.3, s32[16]{0:T(128)S(1)} %copy-done.2, ...), custom_call_target="tpu_custom_call" | custom-call | flops 1 | bytes 1 | tf_op jit(solution)/shard_map/heat/pallas_call | solution.py:478
  81.5 0.0 all-to-all-done.1.rest_2_
  81.5 3.8 %heat.3 = (f32[4,8,128,256]{3,2,1,0:T(8,128)}, f32[8,128,256]{2,1,0:T(8,128)}, f32[32,1,128]{2,1,0:T(1,128)}) custom-call(s32[8,1,128]{2,1,0:T(1,128)S(1)} %get-tuple-element.22.lo_ref.after, s32[8,1,128]{2,1,0:T(1,128)S(1)} %get-tuple-element.23.n_ref, s32[16]{0:T(128)S(1)} %bitcast.4, ...), custom_call_target="tpu_custom_call", output_to_operand_aliasing={{0}: (8, {}), {1}: (9, {})} | custom-call | flops 1 | bytes 1 | tf_op jit(solution)/shard_map/heat/pallas_call | solution.py:478
  85.3 12.3 %all-to-all-start.2 = ((f32[32,1,128]{2,1,0:T(1,128)}), f32[32,1,128]{2,1,0:T(1,128)S(1)}, u32[]{:S(2)}, u32[]{:S(2)}) async-start(f32[32,1,128]{2,1,0:T(1,128)} %get-tuple-element.40), calls=%async_computation.2 | async-start | bytes 32768 | tf_op jit(solution)/shard_map/all_to_all | solution.py:564
  97.6 0.0 collective-permute-done.5.rest_1_
  97.6 0.0 collective-permute-done.6.rest_2_
  97.7 0.0 collective-permute-done.7.rest_3_
  97.7 9.3 %remap.1 = f32[4,8,128,256]{3,2,1,0:T(8,128)} custom-call(s32[8,1,128]{2,1,0:T(1,128)S(1)} %get-tuple-element.22.lo_ref.after, s32[8,1,128]{2,1,0:T(1,128)S(1)} %get-tuple-element.23.n_ref, f32[8,2,128,128]{3,2,1,0:T(8,128)S(1)} %get-tuple-element.24.e_ref, f32[4,8,128,256]{3,2,1,0:T(8,128)} %get-tuple-element.34.base, ...), custom_call_target="tpu_custom_call", output_to_operand_aliasing={{}: (3, {})} | custom-call | flops 1 | bytes 1 | tf_op jit(solution)/shard_map/remap/pallas_call | solution.py:521
  107.0 0.0 all-to-all-done.2
  107.0 0.6 reduce_sum.9
  (1 shorter events, 0.0 us)
Async XLA Ops:
  2.8 37.2 %all-to-all-start = ((f32[4,8,2,32,128]{4,3,2,1,0:T(8,128)}), f32[4,8,2,32,128]{4,3,2,1,0:T(8,128)S(1)}, u32[]{:S(2)}, u32[]{:S(2)}) async-start(f32[4,8,2,32,128]{4,3,2,1,0:T(8,128)} %spread.1.after), calls=%async_computation | async-start | bytes 2097152 | tf_op jit(solution)/shard_map/all_to_all | solution.py:544
  12.3 10.8 %collective-permute-start.3 = (f32[4,32,1024]{2,1,0:T(8,128)}, f32[4,32,1024]{2,1,0:T(8,128)S(1)}, u32[]{:S(2)}, u32[]{:S(2)}) collective-permute-start(f32[4,32,1024]{2,1,0:T(8,128)} %get-tuple-element.33.tail), channel_id=1, source_target_pairs={{0,4},{4,8},{8,12},{12,16},{16,20},{20,24},{24,28},{28,32},{32,36}... | collective-permute-start | bytes 1572872 | tf_op jit(solution)/shard_map/ppermute | solution.py:550
  16.7 11.0 %collective-permute-start.4 = (f32[4,32,1024]{2,1,0:T(8,128)}, f32[4,32,1024]{2,1,0:T(8,128)S(1)}, u32[]{:S(2)}, u32[]{:S(2)}) collective-permute-start(f32[4,32,1024]{2,1,0:T(8,128)} %get-tuple-element.32.head), channel_id=1, source_target_pairs={{4,0},{8,4},{12,8},{16,12},{20,16},{24,20},{28,24},{32,28},{36,32}... | collective-permute-start | bytes 1572872 | tf_op jit(solution)/shard_map/ppermute | solution.py:551
  18.7 18.9 %collective-permute-start = (f32[2,6,2,32,128]{4,3,2,1,0:T(8,128)}, f32[2,6,2,32,128]{4,3,2,1,0:T(8,128)S(1)}, u32[]{:S(2)}, u32[]{:S(2)}) collective-permute-start(f32[2,6,2,32,128]{4,3,2,1,0:T(8,128)} %get-tuple-element.26), channel_id=1, source_target_pairs={{0,1},{1,2},{2,3},{3,0},{4,5},{5,6},{6,7},{7,4},{8,9},{9,10},{10,1... | collective-permute-start | bytes 1179656 | tf_op jit(solution)/shard_map/ppermute | solution.py:543
  32.0 65.6 %collective-permute-start.5 = (f32[2,8,2,32,128]{4,3,2,1,0:T(8,128)}, f32[2,8,2,32,128]{4,3,2,1,0:T(8,128)}, u32[]{:S(2)}, u32[]{:S(2)}) collective-permute-start(f32[2,8,2,32,128]{4,3,2,1,0:T(8,128)} %get-tuple-element.36), channel_id=1, source_target_pairs={{0,1},{1,2},{2,3},{3,0},{4,5},{5,6},{6,7},{7,4},{8,9},{9,10},{10,1... | collective-permute-start | bytes 1572872 | tf_op jit(solution)/shard_map/ppermute | solution.py:543
  33.5 64.1 %collective-permute-start.6 = (f32[2,8,2,32,128]{4,3,2,1,0:T(8,128)}, f32[2,8,2,32,128]{4,3,2,1,0:T(8,128)}, u32[]{:S(2)}, u32[]{:S(2)}) collective-permute-start(f32[2,8,2,32,128]{4,3,2,1,0:T(8,128)} %get-tuple-element.37), channel_id=1, source_target_pairs={{0,2},{1,3},{2,0},{3,1},{4,6},{5,7},{6,4},{7,5},{8,10},{9,11},{10,... | collective-permute-start | bytes 1572872 | tf_op jit(solution)/shard_map/ppermute | solution.py:543
  36.2 61.4 %collective-permute-start.7 = (f32[2,8,2,32,128]{4,3,2,1,0:T(8,128)}, f32[2,8,2,32,128]{4,3,2,1,0:T(8,128)}, u32[]{:S(2)}, u32[]{:S(2)}) collective-permute-start(f32[2,8,2,32,128]{4,3,2,1,0:T(8,128)} %get-tuple-element.38), channel_id=1, source_target_pairs={{0,3},{1,0},{2,1},{3,2},{4,7},{5,4},{6,5},{7,6},{8,11},{9,8},{10,9... | collective-permute-start | bytes 1572872 | tf_op jit(solution)/shard_map/ppermute | solution.py:543
  37.4 28.2 %collective-permute-start.1 = (f32[2,6,2,32,128]{4,3,2,1,0:T(8,128)}, f32[2,6,2,32,128]{4,3,2,1,0:T(8,128)}, u32[]{:S(2)}, u32[]{:S(2)}) collective-permute-start(f32[2,6,2,32,128]{4,3,2,1,0:T(8,128)} %get-tuple-element.27), channel_id=1, source_target_pairs={{0,2},{1,3},{2,0},{3,1},{4,6},{5,7},{6,4},{7,5},{8,10},{9,11},{10,... | collective-permute-start | bytes 1179656 | tf_op jit(solution)/shard_map/ppermute | solution.py:543
  37.5 35.2 %collective-permute-start.2 = (f32[2,6,2,32,128]{4,3,2,1,0:T(8,128)}, f32[2,6,2,32,128]{4,3,2,1,0:T(8,128)}, u32[]{:S(2)}, u32[]{:S(2)}) collective-permute-start(f32[2,6,2,32,128]{4,3,2,1,0:T(8,128)} %get-tuple-element.28), channel_id=1, source_target_pairs={{0,3},{1,0},{2,1},{3,2},{4,7},{5,4},{6,5},{7,6},{8,11},{9,8},{10,9... | collective-permute-start | bytes 1179656 | tf_op jit(solution)/shard_map/ppermute | solution.py:543
  42.8 6.6 %copy-start.3 = (f32[128]{0:T(128)S(1)}, f32[128]{0:T(128)}, u32[]{:S(2)}) copy-start(f32[128]{0:T(128)} %param.13) | copy-start | bytes 1540
  42.8 29.9 %copy-start = (f32[2,128,128]{2,1,0:T(8,128)S(1)}, f32[2,128,128]{2,1,0:T(8,128)}, u32[]{:S(2)}) copy-start(f32[2,128,128]{2,1,0:T(8,128)} %exch.3) | copy-start | bytes 393220
  42.9 29.9 %copy-start.1 = (s32[16,1]{0,1:T(1,128)S(1)}, s32[16,1]{0,1:T(1,128)}, u32[]{:S(2)}) copy-start(s32[16,1]{0,1:T(1,128)} %param.14) | copy-start | bytes 196
  42.9 29.9 %copy-start.2 = (s32[16]{0:T(128)S(1)}, s32[16]{0:T(128)}, u32[]{:S(2)}) copy-start(s32[16]{0:T(128)} %day_ref.3) | copy-start | bytes 196
  45.9 35.6 %all-to-all-start.1 = ((f32[4,2,2,2,32,128]{5,4,3,2,1,0:T(8,128)}), f32[4,2,2,2,32,128]{5,4,3,2,1,0:T(8,128)S(1)}, u32[]{:S(2)}, u32[]{:S(2)}) async-start(f32[4,2,2,2,32,128]{5,4,3,2,1,0:T(8,128)} %outer.1), calls=%async_computation.1 | async-start | bytes 1048576 | tf_op jit(solution)/shard_map/all_to_all | solution.py:544
  85.3 21.6 %all-to-all-start.2 = ((f32[32,1,128]{2,1,0:T(1,128)}), f32[32,1,128]{2,1,0:T(1,128)S(1)}, u32[]{:S(2)}, u32[]{:S(2)}) async-start(f32[32,1,128]{2,1,0:T(1,128)} %get-tuple-element.40), calls=%async_computation.2 | async-start | bytes 32768 | tf_op jit(solution)/shard_map/all_to_all | solution.py:564
